TPU v7x, 32 devices: a whole 2x2x4 slice. The times are simulated.
32 devices in a mesh: section: 2 (over y), dp: 4 (over z), tensor: 4 (over x, core).
Axes of the slice: x: 2, y: 2, z: 4, core: 2. Of those that a mesh axis runs over, the one named last changes fastest.
Arguments:
- ends_in: bfloat16 [2, 3, 16, 128, 768], P('section', None, 'dp'), may hold values from -6 to 6
- segment_ids: int32 [3, 16, 128], P(None, 'dp'), may hold values from 0 to 3, never falling along the last dimension, each value on 1 to 64 neighbouring positions
- w_qkv: bfloat16 [2, 768, 3, 768], P('section', None, None, 'tensor'), may hold values from -0.21875 to 0.21875
- bias_qv: bfloat16 [2, 2, 768], P('section', None, 'tensor'), may hold values from -0.59765625 to 0.59765625
- w_out: bfloat16 [2, 768, 768], P('section', 'tensor'), may hold values from -0.75 to 0.75
- bias_out: bfloat16 [2, 768], P('section'), may hold values from -0.59765625 to 0.59765625
- gain_one: bfloat16 [2, 768], P('section'), may hold values from 0.5 to 1.5
- shift_one: bfloat16 [2, 768], P('section'), may hold values from -0.59765625 to 0.59765625
- w_up: bfloat16 [2, 768, 3072], P('section', None, 'tensor'), may hold values from -0.21875 to 0.21875
- bias_up: bfloat16 [2, 3072], P('section', 'tensor'), may hold values from -0.59765625 to 0.59765625
- w_down: bfloat16 [2, 3072, 768], P('section', 'tensor'), may hold values from -0.109375 to 0.109375
- bias_down: bfloat16 [2, 768], P('section'), may hold values from -0.59765625 to 0.59765625
- gain_two: bfloat16 [2, 768], P('section'), may hold values from 0.5 to 1.5
- shift_two: bfloat16 [2, 768], P('section'), may hold values from -0.59765625 to 0.59765625
Outputs:
- ends_out: float32 [2, 3, 16, 128, 768], P('section', None, 'dp')
- grad_qkv: float32 [2, 768, 3, 768], P('section', None, None, 'tensor')
- grad_bias_qv: float32 [2, 2, 768], P('section', None, 'tensor')
- grad_out: float32 [2, 768, 768], P('section', 'tensor')
- grad_bias_out: float32 [2, 768], P('section')
- grad_gain_one: float32 [2, 768], P('section')
- grad_shift_one: float32 [2, 768], P('section')
- grad_up: float32 [2, 768, 3072], P('section', None, 'tensor')
- grad_bias_up: float32 [2, 3072], P('section', 'tensor')
- grad_down: float32 [2, 3072, 768], P('section', 'tensor')
- grad_bias_down: float32 [2, 768], P('section')
- grad_gain_two: float32 [2, 768], P('section')
- grad_shift_two: float32 [2, 768], P('section')
Inputs may be any that keep to these rules, and one draw needn't show every extreme that they name: `segment_ids`: within each sequence the numbers never fall; each of 0 to 3 holds 1 to 64 rows, and one holds exactly 64.
All inputs are finite; a program needn't handle non-finite values.
Results may differ from a plain program's by a relative error of at most 0.025.
Values may be sent and summed in bfloat16 or wider, within the bound.
No kernel may reach another device: no remote copies, remote signals or barrier semaphores. Data moves between devices by JAX's collectives and lax.ppermute only.
A program may use at most 192 MiB of HBM per device.

v0:
```python
import jax
import jax.numpy as jnp
from jax import lax
from jax.sharding import PartitionSpec as P

HEAD = 64


epsilon = 1e-05


def from_behind(x, axis, by):
    size = lax.axis_size(axis)
    pairs = [(i, i + by) for i in range(size) if 0 <= i + by < size]
    return lax.ppermute(x, axis, pairs)


def combine_forward(partial_value):
    return lax.psum(partial_value.astype(jnp.bfloat16), "tensor").astype(jnp.float32)


def combine_backward(partial_value):
    return lax.psum(partial_value.astype(jnp.bfloat16), "tensor").astype(jnp.float32)


def contract_rows(left, right):
    return lax.dot_general(
        left, right, (((0,), (0,)), ((), ())), preferred_element_type=jnp.float32
    )


def contract_cols(left, right):
    return lax.dot_general(
        left, right, (((1,), (1,)), ((), ())), preferred_element_type=jnp.float32
    )


def standardize(summed):
    center = summed - jnp.mean(summed, -1, keepdims=True)
    inverse = lax.rsqrt(jnp.mean(center * center, -1, keepdims=True) + epsilon)
    return (center * inverse, inverse)


def layer_norm(summed, gain, shift):
    normed, inverse = standardize(summed)
    return normed * gain.astype(jnp.float32) + shift.astype(jnp.float32)


def norm_back(summed, gain, grad_output):
    normed, inverse = standardize(summed)
    grad_gain = jnp.sum(grad_output * normed, 0)
    grad_shift = jnp.sum(grad_output, 0)
    scaled = grad_output * gain.astype(jnp.float32)
    grad_summed = inverse * (
        scaled
        - jnp.mean(scaled, -1, keepdims=True)
        - normed * jnp.mean(scaled * normed, -1, keepdims=True)
    )
    return (grad_gain, grad_shift, grad_summed)


def gelu_value(value):
    return jax.nn.gelu(value, approximate=False)


def gelu_slope(value):
    normal_cdf = 0.5 * (1.0 + lax.erf(value * 0.7071067811865476))
    density = jnp.exp(-0.5 * value * value) * 0.3989422804014327
    return normal_cdf + value * density


def split_heads(mixed, segments):
    count, length = segments.shape
    width = mixed.shape[1] // 3
    parts = mixed.reshape(count, length, 3, width // HEAD, HEAD)
    return (parts[:, :, 0], parts[:, :, 1], parts[:, :, 2])


def masked_scores(query, keys, segments):
    raw = jnp.einsum("sqhd,skhd->shqk", query, keys, preferred_element_type=jnp.float32) * HEAD ** (
        -0.5
    )
    same = segments[:, None, :, None] == segments[:, None, None, :]
    return jnp.where(same, raw, -1000000000.0)


def attend(mixed, segments):
    query, keys, value = split_heads(mixed, segments)
    scores = masked_scores(query, keys, segments)
    top = jnp.max(scores, -1, keepdims=True)
    logsum = top + jnp.log(jnp.sum(jnp.exp(scores - top), -1, keepdims=True))
    probs = jnp.exp(scores - logsum).astype(jnp.bfloat16)
    result = jnp.einsum("shqk,skhd->sqhd", probs, value, preferred_element_type=jnp.float32)
    return (result.astype(jnp.bfloat16).reshape(mixed.shape[0], -1), logsum)


def attend_back(mixed, segments, logsum, grad_result):
    query, keys, value = split_heads(mixed, segments)
    probs = jnp.exp(masked_scores(query, keys, segments) - logsum)
    grad_heads = grad_result.reshape(query.shape)
    grad_probs = jnp.einsum(
        "sqhd,skhd->shqk", grad_heads, value, preferred_element_type=jnp.float32
    )
    grad_value = jnp.einsum(
        "shqk,sqhd->skhd",
        probs.astype(jnp.bfloat16),
        grad_heads,
        preferred_element_type=jnp.float32,
    )
    inner = jnp.sum(probs * grad_probs, -1, keepdims=True)
    grad_scores = (probs * (grad_probs - inner)).astype(jnp.bfloat16)
    grad_query = jnp.einsum(
        "shqk,skhd->sqhd", grad_scores, keys, preferred_element_type=jnp.float32
    ) * HEAD ** (-0.5)
    grad_keys = jnp.einsum(
        "shqk,sqhd->skhd", grad_scores, query, preferred_element_type=jnp.float32
    ) * HEAD ** (-0.5)
    stacked = jnp.stack([grad_query, grad_keys, grad_value], 2)
    return stacked.reshape(mixed.shape).astype(jnp.bfloat16)


def layer_forward(rows_in, segments, weights):
    (
        w_qkv,
        bias_qv,
        w_out,
        bias_out,
        gain_one,
        shift_one,
        w_up,
        bias_up,
        w_down,
        bias_down,
        gain_two,
        shift_two,
    ) = weights
    whole_in = rows_in.astype(jnp.bfloat16)
    width = w_qkv.shape[2]
    joined = jnp.concatenate([bias_qv[0], jnp.zeros_like(bias_qv[0]), bias_qv[1]]).astype(
        jnp.float32
    )
    flat_qkv = w_qkv.reshape(w_qkv.shape[0], 3 * width)
    mixed = (jnp.dot(whole_in, flat_qkv, preferred_element_type=jnp.float32) + joined).astype(
        jnp.bfloat16
    )
    attended, logsum = attend(mixed, segments)
    first = (
        combine_forward(jnp.dot(attended, w_out, preferred_element_type=jnp.float32))
        + bias_out.astype(jnp.float32)
        + rows_in
    )
    hidden = layer_norm(first, gain_one, shift_one)
    hidden_in = hidden.astype(jnp.bfloat16)
    upward = jnp.dot(hidden_in, w_up, preferred_element_type=jnp.float32) + bias_up.astype(
        jnp.float32
    )
    active = gelu_value(upward).astype(jnp.bfloat16)
    second = (
        combine_forward(jnp.dot(active, w_down, preferred_element_type=jnp.float32))
        + bias_down.astype(jnp.float32)
        + hidden
    )
    output = layer_norm(second, gain_two, shift_two)
    return (output, (whole_in, mixed, logsum, attended, first, hidden_in, upward, second))


def layer_backward(grad_output, segments, kept, weights):
    (
        w_qkv,
        bias_qv,
        w_out,
        bias_out,
        gain_one,
        shift_one,
        w_up,
        bias_up,
        w_down,
        bias_down,
        gain_two,
        shift_two,
    ) = weights
    whole_in, mixed, logsum, attended, first, hidden_in, upward, second = kept
    grad_gain_two, grad_shift_two, grad_second = norm_back(second, gain_two, grad_output)
    grad_bias_down = jnp.sum(grad_second, 0)
    branch_two = grad_second.astype(jnp.bfloat16)
    grad_down = contract_rows(gelu_value(upward).astype(jnp.bfloat16), branch_two)
    grad_upward = (contract_cols(branch_two, w_down) * gelu_slope(upward)).astype(jnp.bfloat16)
    grad_bias_up = jnp.sum(grad_upward, 0, dtype=jnp.float32)
    grad_up = contract_rows(hidden_in, grad_upward)
    grad_hidden = combine_backward(contract_cols(grad_upward, w_up)) + grad_second
    grad_gain_one, grad_shift_one, grad_first = norm_back(first, gain_one, grad_hidden)
    grad_bias_out = jnp.sum(grad_first, 0)
    branch_one = grad_first.astype(jnp.bfloat16)
    grad_out = contract_rows(attended, branch_one)
    grad_attended = contract_cols(branch_one, w_out).astype(jnp.bfloat16)
    grad_mixed = attend_back(mixed, segments, logsum, grad_attended)
    width = w_qkv.shape[2]
    grad_bias_qv = jnp.stack(
        [
            jnp.sum(grad_mixed[:, :width], 0, dtype=jnp.float32),
            jnp.sum(grad_mixed[:, 2 * width :], 0, dtype=jnp.float32),
        ]
    )
    flat_qkv = w_qkv.reshape(w_qkv.shape[0], 3 * width)
    grad_qkv = contract_rows(whole_in, grad_mixed).reshape(w_qkv.shape)
    grad_in = combine_backward(contract_cols(grad_mixed, flat_qkv)) + grad_first
    grads = (
        grad_qkv,
        grad_bias_qv,
        grad_out,
        grad_bias_out,
        grad_gain_one,
        grad_shift_one,
        grad_up,
        grad_bias_up,
        grad_down,
        grad_bias_down,
        grad_gain_two,
        grad_shift_two,
    )
    return (grad_in, grads)


def body(
    ends_in,
    segment_ids,
    w_qkv,
    bias_qv,
    w_out,
    bias_out,
    gain_one,
    shift_one,
    w_up,
    bias_up,
    w_down,
    bias_down,
    gain_two,
    shift_two,
):
    weights = tuple(
        (
            item[0]
            for item in (
                w_qkv,
                bias_qv,
                w_out,
                bias_out,
                gain_one,
                shift_one,
                w_up,
                bias_up,
                w_down,
                bias_down,
                gain_two,
                shift_two,
            )
        )
    )
    section = lax.axis_index("section")
    micro = ends_in.shape[1]
    width = ends_in.shape[-1]
    own = ends_in[0].reshape(micro, -1, width)
    steps = micro + 1
    received = jnp.zeros(own[0].shape, jnp.float32)
    outputs = []
    stash = []
    for step in range(steps):
        fresh = own[min(step, micro - 1)].astype(jnp.float32)
        rows_in = jnp.where(section == 0, fresh, received)
        segments = lax.dynamic_index_in_dim(
            segment_ids, jnp.clip(step - section, 0, micro - 1), 0, keepdims=False
        )
        output, kept = layer_forward(rows_in, segments, weights)
        outputs.append(output)
        stash.append(kept)
        if step + 1 < steps:
            received = from_behind(output.astype(jnp.bfloat16), "section", 1).astype(jnp.float32)
    kept_all = jax.tree.map(lambda *items: jnp.stack(items), *stash)
    returned = jnp.zeros_like(received)
    totals = None
    grads_in = []
    for step in range(steps):
        fresh = own[min(step, micro - 1)].astype(jnp.float32)
        grad_here = jnp.where(section == 1, fresh, returned)
        batch = step - 1 + section
        valid = (batch >= 0) & (batch < micro)
        segments = lax.dynamic_index_in_dim(
            segment_ids, jnp.clip(batch, 0, micro - 1), 0, keepdims=False
        )
        slot = jnp.clip(batch + section, 0, steps - 1)
        kept = jax.tree.map(
            lambda item: lax.dynamic_index_in_dim(item, slot, 0, keepdims=False), kept_all
        )
        grad_in, grads = layer_backward(grad_here, segments, kept, weights)
        grads = jax.tree.map(lambda item: jnp.where(valid, item, 0.0), grads)
        totals = grads if totals is None else jax.tree.map(jnp.add, totals, grads)
        grads_in.append(grad_in)
        if step + 1 < steps:
            returned = from_behind(grad_in.astype(jnp.bfloat16), "section", -1).astype(jnp.float32)
    edges = jnp.stack(
        [jnp.where(section == 1, outputs[batch + 1], grads_in[batch + 1]) for batch in range(micro)]
    )
    edges = edges.reshape(ends_in.shape)
    (
        grad_qkv,
        grad_bias_qv,
        grad_out,
        grad_bias_out,
        grad_gain_one,
        grad_shift_one,
        grad_up,
        grad_bias_up,
        grad_down,
        grad_bias_down,
        grad_gain_two,
        grad_shift_two,
    ) = totals
    summed = (
        lax.psum(grad_qkv.astype(jnp.bfloat16), "dp").astype(jnp.float32),
        lax.psum(grad_bias_qv.astype(jnp.bfloat16), "dp").astype(jnp.float32),
        lax.psum(grad_out.astype(jnp.bfloat16), "dp").astype(jnp.float32),
        lax.psum(grad_bias_out.astype(jnp.bfloat16), "dp").astype(jnp.float32),
        lax.psum(grad_gain_one.astype(jnp.bfloat16), "dp").astype(jnp.float32),
        lax.psum(grad_shift_one.astype(jnp.bfloat16), "dp").astype(jnp.float32),
        lax.psum(grad_up.astype(jnp.bfloat16), "dp").astype(jnp.float32),
        lax.psum(grad_bias_up.astype(jnp.bfloat16), "dp").astype(jnp.float32),
        lax.psum(grad_down.astype(jnp.bfloat16), "dp").astype(jnp.float32),
        lax.psum(grad_bias_down.astype(jnp.bfloat16), "dp").astype(jnp.float32),
        lax.psum(grad_gain_two.astype(jnp.bfloat16), "dp").astype(jnp.float32),
        lax.psum(grad_shift_two.astype(jnp.bfloat16), "dp").astype(jnp.float32),
    )
    return (edges,) + tuple((item[None] for item in summed))


def solution(mesh):
    return jax.shard_map(
        body,
        mesh=mesh,
        in_specs=(
            P("section", None, "dp", None, None),
            P(None, "dp", None),
            P("section", None, None, "tensor"),
            P("section", None, "tensor"),
            P("section", "tensor", None),
            P("section", None),
            P("section", None),
            P("section", None),
            P("section", None, "tensor"),
            P("section", "tensor"),
            P("section", "tensor", None),
            P("section", None),
            P("section", None),
            P("section", None),
        ),
        out_specs=(
            P("section", None, "dp", None, None),
            P("section", None, None, "tensor"),
            P("section", None, "tensor"),
            P("section", "tensor", None),
            P("section", None),
            P("section", None),
            P("section", None),
            P("section", None, "tensor"),
            P("section", "tensor"),
            P("section", "tensor", None),
            P("section", None),
            P("section", None),
            P("section", None),
        ),
        check_vma=False,
    )
```

profile of v0, /device:TPU:0, one launch (start us, length us, event | category | flops | bytes accessed | tf_op | source)
XLA Modules:
  0.0 1064.9 jit_solution(12446722414149293318)
XLA Ops:
  16.7 37.3 %all-reduce.20.cloned.1.call-done = bf16[512,768]{1,0:T(8,128)(2,1)} async-done(((bf16[512,768]{1,0:T(8,128)(2,1)}), bf16[512,768]{1,0:T(8,128)(2,1)}) %all-reduce.20.cloned.1.call-update) | async-done | bytes 786448 | tf_op jit(solution)/shard_map/psum | solution.py:19
  59.8 4.9 convolution_convert_fusion.7
  64.9 34.7 %all-reduce.22.cloned.1.call-done = bf16[512,768]{1,0:T(8,128)(2,1)} async-done(((bf16[512,768]{1,0:T(8,128)(2,1)}), bf16[512,768]{1,0:T(8,128)(2,1)}) %all-reduce.22.cloned.1.call-update) | async-done | bytes 786448 | tf_op jit(solution)/shard_map/psum | solution.py:19
  103.3 3.5 collective-permute-start
  107.0 15.7 %collective-permute-done = bf16[512,768]{1,0:T(8,128)(2,1)S(1)} collective-permute-done((bf16[512,768]{1,0:T(8,128)(2,1)S(1)}, bf16[512,768]{1,0:T(8,128)(2,1)S(1)}, u32[]{:S(2)}, u32[]{:S(2)}) %collective-permute-start) | collective-permute-done | bytes 786464 | tf_op jit(solution)/shard_map/ppermute | solution.py:15
  133.2 36.0 %all-reduce.24.cloned.1.call-done = bf16[512,768]{1,0:T(8,128)(2,1)} async-done(((bf16[512,768]{1,0:T(8,128)(2,1)}), bf16[512,768]{1,0:T(8,128)(2,1)}) %all-reduce.24.cloned.1.call-update) | async-done | bytes 786448 | tf_op jit(solution)/shard_map/psum | solution.py:19
  174.8 4.9 convolution_convert_fusion.6
  179.8 34.8 %all-reduce.26.cloned.1.call-done = bf16[512,768]{1,0:T(8,128)(2,1)} async-done(((bf16[512,768]{1,0:T(8,128)(2,1)}), bf16[512,768]{1,0:T(8,128)(2,1)}) %all-reduce.26.cloned.1.call-update) | async-done | bytes 786448 | tf_op jit(solution)/shard_map/psum | solution.py:19
  218.6 3.5 collective-permute-start.1
  223.1 15.0 %collective-permute-done.1 = bf16[512,768]{1,0:T(8,128)(2,1)S(1)} collective-permute-done((bf16[512,768]{1,0:T(8,128)(2,1)S(1)}, bf16[512,768]{1,0:T(8,128)(2,1)S(1)}, u32[]{:S(2)}, u32[]{:S(2)}) %collective-permute-start.1) | collective-permute-done | bytes 786464 | tf_op jit(solution)/shard_map/ppermute | solution.py:15
  249.2 36.2 %all-reduce.28.cloned.1.call-done = bf16[512,768]{1,0:T(8,128)(2,1)} async-done(((bf16[512,768]{1,0:T(8,128)(2,1)}), bf16[512,768]{1,0:T(8,128)(2,1)}) %all-reduce.28.cloned.1.call-update) | async-done | bytes 786448 | tf_op jit(solution)/shard_map/psum | solution.py:19
  291.2 4.9 convolution_convert_fusion.5
  298.4 32.6 %all-reduce.30.cloned.1.call-done = bf16[512,768]{1,0:T(8,128)(2,1)} async-done(((bf16[512,768]{1,0:T(8,128)(2,1)}), bf16[512,768]{1,0:T(8,128)(2,1)}) %all-reduce.30.cloned.1.call-update) | async-done | bytes 786448 | tf_op jit(solution)/shard_map/psum | solution.py:19
  335.7 4.3 collective-permute-start.2
  349.1 6.2 collective-permute-done.2
  396.5 9.3 all-reduce.32.cloned.1.call-done
  417.1 4.9 convolution_convert_fusion.4
  423.6 4.8 pad_maximum_fusion.2
  428.4 28.5 %all-reduce.34.cloned.1.call-done = bf16[512,768]{1,0:T(8,128)(2,1)} async-done(((bf16[512,768]{1,0:T(8,128)(2,1)}), bf16[512,768]{1,0:T(8,128)(2,1)}) %all-reduce.34.cloned.1.call-update) | async-done | bytes 786448 | tf_op jit(solution)/shard_map/psum | solution.py:19
  456.9 3.8 fusion.840
  473.2 5.1 fusion.223
  486.2 28.6 %all-reduce.36.cloned.1.call-done = bf16[512,768]{1,0:T(8,128)(2,1)} async-done(((bf16[512,768]{1,0:T(8,128)(2,1)}), bf16[512,768]{1,0:T(8,128)(2,1)}) %all-reduce.36.cloned.1.call-update) | async-done | bytes 786448 | tf_op jit(solution)/shard_map/psum | solution.py:23
  514.8 5.4 multiply_reduce_fusion.7
  534.7 3.6 fusion.230
  538.3 29.7 %all-reduce.38.cloned.1.call-done = bf16[512,768]{1,0:T(8,128)(2,1)} async-done(((bf16[512,768]{1,0:T(8,128)(2,1)}), bf16[512,768]{1,0:T(8,128)(2,1)}) %all-reduce.38.cloned.1.call-update) | async-done | bytes 786448 | tf_op jit(solution)/shard_map/psum | solution.py:23
  575.1 14.2 %collective-permute-done.3 = bf16[512,768]{1,0:T(8,128)(2,1)S(1)} collective-permute-done((bf16[512,768]{1,0:T(8,128)(2,1)S(1)}, bf16[512,768]{1,0:T(8,128)(2,1)S(1)}, u32[]{:S(2)}, u32[]{:S(2)}) %collective-permute-start.3) | collective-permute-done | bytes 786464 | tf_op jit(solution)/shard_map/ppermute | solution.py:15
  589.3 3.6 multiply_reduce_fusion.2
  595.0 3.7 convert_reduce_fusion.2
  603.9 32.1 %all-reduce.40.cloned.1.call-done = bf16[512,768]{1,0:T(8,128)(2,1)} async-done(((bf16[512,768]{1,0:T(8,128)(2,1)}), bf16[512,768]{1,0:T(8,128)(2,1)}) %all-reduce.40.cloned.1.call-update) | async-done | bytes 786448 | tf_op jit(solution)/shard_map/psum | solution.py:23
  649.3 3.7 fusion.228
  653.0 30.5 %all-reduce.42.cloned.1.call-done = bf16[512,768]{1,0:T(8,128)(2,1)} async-done(((bf16[512,768]{1,0:T(8,128)(2,1)}), bf16[512,768]{1,0:T(8,128)(2,1)}) %all-reduce.42.cloned.1.call-update) | async-done | bytes 786448 | tf_op jit(solution)/shard_map/psum | solution.py:23
  683.5 3.4 fusion.189
  688.8 6.8 fusion.221
  695.6 11.6 %collective-permute-done.4 = bf16[512,768]{1,0:T(8,128)(2,1)S(1)} collective-permute-done((bf16[512,768]{1,0:T(8,128)(2,1)S(1)}, bf16[512,768]{1,0:T(8,128)(2,1)S(1)}, u32[]{:S(2)}, u32[]{:S(2)}) %collective-permute-start.4) | collective-permute-done | bytes 786464 | tf_op jit(solution)/shard_map/ppermute | solution.py:15
  709.3 3.7 convert_reduce_fusion.1
  722.1 28.3 %all-reduce.44.cloned.1.call-done = bf16[512,768]{1,0:T(8,128)(2,1)} async-done(((bf16[512,768]{1,0:T(8,128)(2,1)}), bf16[512,768]{1,0:T(8,128)(2,1)}) %all-reduce.44.cloned.1.call-update) | async-done | bytes 786448 | tf_op jit(solution)/shard_map/psum | solution.py:23
  763.2 7.4 fusion.219
  770.6 27.4 %all-reduce.46.cloned.1.call-done = bf16[512,768]{1,0:T(8,128)(2,1)} async-done(((bf16[512,768]{1,0:T(8,128)(2,1)}), bf16[512,768]{1,0:T(8,128)(2,1)}) %all-reduce.46.cloned.1.call-update) | async-done | bytes 786448 | tf_op jit(solution)/shard_map/psum | solution.py:23
  798.0 3.4 fusion.192
  803.1 3.4 fusion.226
  811.9 9.8 collective-permute-done.5
  823.8 3.2 convert_reduce_fusion
  828.8 8.3 fusion.143
  837.2 3.3 fusion.142
  840.4 22.9 %all-reduce.48.cloned.1.call-done = bf16[512,768]{1,0:T(8,128)(2,1)} async-done(((bf16[512,768]{1,0:T(8,128)(2,1)}), bf16[512,768]{1,0:T(8,128)(2,1)}) %all-reduce.48.cloned.1.call-update) | async-done | bytes 786448 | tf_op jit(solution)/shard_map/psum | solution.py:23
  881.4 3.5 fusion.155
  887.9 18.9 %all-reduce = (bf16[1,2,192]{2,1,0:T(2,128)(2,1)S(1)}, bf16[1,768]{1,0:T(2,128)(2,1)S(1)}, bf16[1,768]{1,0:T(2,128)(2,1)S(1)}, bf16[1,768]{1,0:T(2,128)(2,1)S(1)...) all-reduce(bf16[1,2,192]{2,1,0:T(2,128)(2,1)S(1)} %fusion.580, ...), channel_id=1, replica_groups=mesh['section'=2,'dp'=4,'tensor'=4] {'dp'}, use_global_device_ids=true, to_apply=%region_85.86 | all-reduce | flops 5760 | bytes 23040 | tf_op jit(solution)/shard_map/psum | solution.py:320
  918.3 132.9 %all-reduce.52.cloned.1.call-done = (bf16[1,768,3,192]{1,3,2,0:T(8,128)(2,1)}, bf16[1,192,768]{2,1,0:T(8,128)(2,1)}, bf16[1,768,768]{2,1,0:T(8,128)(2,1)}, bf16[1,768,768]{2,1,0:T(8,128)(2,1)}) async-done(((bf16[1,768,3,192]{1,3,2,0:T(8,128)(2,1)}, bf16[1,192,768]{2,1,0:T(8,128)(2,1)}, bf16[1,768,768]{2,1,0:T(8,128)(2,1)}, bf16[1,768,768]{2,1,0:T(8,128)(2,1)}), (bf16[1,768,3,192]{1,3,2,0:T(8,128)(2,1)}, ...) | async-done | bytes 3538960 | tf_op jit(solution)/shard_map/psum | solution.py:319
  (742 shorter events, 263.6 us)
Async XLA Ops:
  7.2 52.6 %copy-start = (bf16[1,768,768]{2,1,0:T(8,128)(2,1)S(1)}, bf16[1,768,768]{2,1,0:T(8,128)(2,1)}, u32[]{:S(2)}) copy-start(bf16[1,768,768]{2,1,0:T(8,128)(2,1)} %param.24) | copy-start | bytes 3538948
  7.2 46.8 %all-reduce.20.cloned.1.call-start = ((), (), s32[]{:S(2)}) async-start(), calls=%async_computation | async-start | bytes 1572864 | tf_op jit(solution)/shard_map/psum | solution.py:19
  15.2 40.7 %copy-start.73 = (bf16[4,128,3,64]{1,0,3,2:T(4,128)(2,1)}, bf16[4,128,3,64]{1,0,3,2:T(4,128)(2,1)S(1)}, u32[]{:S(2)}) copy-start(bf16[4,128,3,64]{1,0,3,2:T(4,128)(2,1)S(1)} %copy.67) | copy-start | bytes 589828
  16.5 83.0 %all-reduce.22.cloned.1.call-start = ((), (), s32[]{:S(2)}) async-start(), calls=%async_computation.1 | async-start | bytes 1572864 | tf_op jit(solution)/shard_map/psum | solution.py:19
  16.7 39.5 %copy-start.180 = (f32[768]{0:T(1024)}, f32[768]{0:T(1024)S(1)}, u32[]{:S(2)}) copy-start(f32[768]{0:T(1024)S(1)} %get-tuple-element.206) | copy-start | bytes 9220
  16.7 82.9 %copy-start.102 = (f32[768]{0:T(1024)}, f32[768]{0:T(1024)S(1)}, u32[]{:S(2)}) copy-start(f32[768]{0:T(1024)S(1)} %get-tuple-element.207) | copy-start | bytes 9220
  55.9 43.7 %copy-start.14 = (f32[512,768]{1,0:T(8,128)}, f32[512,768]{1,0:T(8,128)S(1)}, u32[]{:S(2)}) copy-start(f32[512,768]{1,0:T(8,128)S(1)} %get-tuple-element.109) | copy-start | bytes 4718596
  64.7 104.5 %all-reduce.24.cloned.1.call-start = ((), (), s32[]{:S(2)}) async-start(), calls=%async_computation.2 | async-start | bytes 1572864 | tf_op jit(solution)/shard_map/psum | solution.py:19
  64.8 37.3 %copy-start.106 = (f32[768]{0:T(1024)}, f32[768]{0:T(1024)S(1)}, u32[]{:S(2)}) copy-start(f32[768]{0:T(1024)S(1)} %convert_reduce_fusion.14) | copy-start | bytes 9220
  103.3 19.4 %collective-permute-start = (bf16[512,768]{1,0:T(8,128)(2,1)S(1)}, bf16[512,768]{1,0:T(8,128)(2,1)S(1)}, u32[]{:S(2)}, u32[]{:S(2)}) collective-permute-start(bf16[512,768]{1,0:T(8,128)(2,1)S(1)} %add_convert_fusion.4), channel_id=1, source_target_pairs={{0,16},{1,17},{2,18},{3,19},{4,20},{5,21},{6,22},{7,23},{8,24},{9,... | collective-permute-start | bytes 2359304 | tf_op jit(solution)/shard_map/ppermute | solution.py:15
  107.0 62.2 %copy-start.25 = (bf16[1,1,4,128,768]{4,3,2,1,0:T(8,128)(2,1)}, bf16[1,1,4,128,768]{4,3,2,1,0:T(8,128)(2,1)S(1)}, u32[]{:S(2)}) copy-start(bf16[1,1,4,128,768]{4,3,2,1,0:T(8,128)(2,1)S(1)} %get-tuple-element.123) | copy-start | bytes 2359300
  133.0 81.6 %all-reduce.26.cloned.1.call-start = ((), (), s32[]{:S(2)}) async-start(), calls=%async_computation.3 | async-start | bytes 1572864 | tf_op jit(solution)/shard_map/psum | solution.py:19
  179.8 105.6 %all-reduce.28.cloned.1.call-start = ((), (), s32[]{:S(2)}) async-start(), calls=%async_computation.4 | async-start | bytes 1572864 | tf_op jit(solution)/shard_map/psum | solution.py:19
  217.7 243.0 %copy-start.3 = (f32[512,768]{1,0:T(8,128)}, f32[512,768]{1,0:T(8,128)S(1)}, u32[]{:S(2)}) copy-start(f32[512,768]{1,0:T(8,128)S(1)} %get-tuple-element.103) | copy-start | bytes 4718596
  218.0 21.2 %copy-start.129 = (f32[512]{0:T(512)}, f32[512]{0:T(512)S(1)}, u32[]{:S(2)}) copy-start(f32[512]{0:T(512)S(1)} %add_rsqrt_fusion.12) | copy-start | bytes 6148
  218.6 21.4 %copy-start.189 = (f32[576]{0:T(1024)S(1)}, f32[576]{0:T(1024)}, u32[]{:S(2)}) copy-start(f32[576]{0:T(1024)} %copy-done.187) | copy-start | bytes 6916
  218.6 21.4 %copy-start.208 = (bf16[1,768,3,192]{1,3,2,0:T(8,128)(2,1)S(1)}, bf16[1,768,3,192]{1,3,2,0:T(8,128)(2,1)}, u32[]{:S(2)}) copy-start(bf16[1,768,3,192]{1,3,2,0:T(8,128)(2,1)} %param.16) | copy-start | bytes 2654212
  218.6 19.4 %collective-permute-start.1 = (bf16[512,768]{1,0:T(8,128)(2,1)S(1)}, bf16[512,768]{1,0:T(8,128)(2,1)S(1)}, u32[]{:S(2)}, u32[]{:S(2)}) collective-permute-start(bf16[512,768]{1,0:T(8,128)(2,1)S(1)} %fusion.190), channel_id=1, source_target_pairs={{0,16},{1,17},{2,18},{3,19},{4,20},{5,21},{6,22},{7,23},{8,24},{9,... | collective-permute-start | bytes 2359304 | tf_op jit(solution)/shard_map/ppermute | solution.py:15
  249.2 81.8 %all-reduce.30.cloned.1.call-start = ((), (), s32[]{:S(2)}) async-start(), calls=%async_computation.5 | async-start | bytes 1572864 | tf_op jit(solution)/shard_map/psum | solution.py:19
  296.2 109.6 %all-reduce.32.cloned.1.call-start = ((), (), s32[]{:S(2)}) async-start(), calls=%async_computation.6 | async-start | bytes 1572864 | tf_op jit(solution)/shard_map/psum | solution.py:19
  335.7 19.6 %collective-permute-start.2 = (bf16[512,768]{1,0:T(8,128)(2,1)}, bf16[512,768]{1,0:T(8,128)(2,1)}, u32[]{:S(2)}, u32[]{:S(2)}) collective-permute-start(bf16[512,768]{1,0:T(8,128)(2,1)} %fusion.193), channel_id=1, source_target_pairs={{0,16},{1,17},{2,18},{3,19},{4,20},{5,21},{6,22},{7,23},{8,24},{9,... | collective-permute-start | bytes 2359304 | tf_op jit(solution)/shard_map/ppermute | solution.py:15
  369.5 87.4 %all-reduce.34.cloned.1.call-start = ((), (), s32[]{:S(2)}) async-start(), calls=%async_computation.7 | async-start | bytes 1572864 | tf_op jit(solution)/shard_map/psum | solution.py:19
  422.1 92.8 %all-reduce.36.cloned.1.call-start = ((), (), s32[]{:S(2)}) async-start(), calls=%async_computation.8 | async-start | bytes 1572864 | tf_op jit(solution)/shard_map/psum | solution.py:23
  480.0 88.0 %all-reduce.38.cloned.1.call-start = ((), (), s32[]{:S(2)}) async-start(), calls=%async_computation.9 | async-start | bytes 1572864 | tf_op jit(solution)/shard_map/psum | solution.py:23
  522.8 45.2 %copy-start.12 = (f32[512,768]{1,0:T(8,128)}, f32[512,768]{1,0:T(8,128)S(1)}, u32[]{:S(2)}) copy-start(f32[512,768]{1,0:T(8,128)S(1)} %get-tuple-element.84) | copy-start | bytes 4718596
  533.2 102.9 %all-reduce.40.cloned.1.call-start = ((), (), s32[]{:S(2)}) async-start(), calls=%async_computation.10 | async-start | bytes 1572864 | tf_op jit(solution)/shard_map/psum | solution.py:23
  569.4 19.9 %collective-permute-start.3 = (bf16[512,768]{1,0:T(8,128)(2,1)S(1)}, bf16[512,768]{1,0:T(8,128)(2,1)S(1)}, u32[]{:S(2)}, u32[]{:S(2)}) collective-permute-start(bf16[512,768]{1,0:T(8,128)(2,1)S(1)} %add_convert_fusion.3), channel_id=1, source_target_pairs={{16,0},{17,1},{18,2},{19,3},{20,4},{21,5},{22,6},{23,7},{24,8},{25... | collective-permute-start | bytes 2359304 | tf_op jit(solution)/shard_map/ppermute | solution.py:15
  594.9 44.2 %copy-start.34 = (f32[512,768]{1,0:T(8,128)}, f32[512,768]{1,0:T(8,128)S(1)}, u32[]{:S(2)}) copy-start(f32[512,768]{1,0:T(8,128)S(1)} %subtract_multiply_fusion.5) | copy-start | bytes 4718596
  599.6 36.5 %copy-start.127 = (f32[512]{0:T(512)S(1)}, f32[512]{0:T(512)}, u32[]{:S(2)}) copy-start(f32[512]{0:T(512)} %broadcast_multiply_fusion.25) | copy-start | bytes 6148
  601.3 82.2 %all-reduce.42.cloned.1.call-start = ((), (), s32[]{:S(2)}) async-start(), calls=%async_computation.11 | async-start | bytes 1572864 | tf_op jit(solution)/shard_map/psum | solution.py:23
  648.6 101.8 %all-reduce.44.cloned.1.call-start = ((), (), s32[]{:S(2)}) async-start(), calls=%async_computation.12 | async-start | bytes 1572864 | tf_op jit(solution)/shard_map/psum | solution.py:23
  649.3 34.2 %copy-start.4 = (f32[512,768]{1,0:T(8,128)S(1)}, f32[512,768]{1,0:T(8,128)}, u32[]{:S(2)}) copy-start(f32[512,768]{1,0:T(8,128)} %copy-done.3) | copy-start | bytes 4718596
  649.3 34.2 %copy-start.117 = (f32[512]{0:T(512)S(1)}, f32[512]{0:T(512)}, u32[]{:S(2)}) copy-start(f32[512]{0:T(512)} %copy-done.116) | copy-start | bytes 6148
  686.8 20.4 %copy-start.115 = (f32[512]{0:T(512)S(1)}, f32[512]{0:T(512)}, u32[]{:S(2)}) copy-start(f32[512]{0:T(512)} %copy-done.114) | copy-start | bytes 6148
  686.8 20.4 %copy-start.144 = (f32[512]{0:T(512)S(1)}, f32[512]{0:T(512)}, u32[]{:S(2)}) copy-start(f32[512]{0:T(512)} %add_rsqrt_fusion.3) | copy-start | bytes 6148
  686.8 20.3 %collective-permute-start.4 = (bf16[512,768]{1,0:T(8,128)(2,1)S(1)}, bf16[512,768]{1,0:T(8,128)(2,1)S(1)}, u32[]{:S(2)}, u32[]{:S(2)}) collective-permute-start(bf16[512,768]{1,0:T(8,128)(2,1)S(1)} %get-tuple-element.115), channel_id=1, source_target_pairs={{16,0},{17,1},{18,2},{19,3},{20,4},{21,5},{22,6},{23,7},{24,8},{25... | collective-permute-start | bytes 2359304 | tf_op jit(solution)/shard_map/ppermute | solution.py:15
  715.7 82.2 %all-reduce.46.cloned.1.call-start = ((), (), s32[]{:S(2)}) async-start(), calls=%async_computation.13 | async-start | bytes 1572864 | tf_op jit(solution)/shard_map/psum | solution.py:23
  719.0 31.4 %copy-start.37 = (f32[512,768]{1,0:T(8,128)S(1)}, f32[512,768]{1,0:T(8,128)}, u32[]{:S(2)}) copy-start(f32[512,768]{1,0:T(8,128)} %copy-done.36) | copy-start | bytes 4718596
  719.0 31.4 %copy-start.126 = (f32[512]{0:T(512)S(1)}, f32[512]{0:T(512)}, u32[]{:S(2)}) copy-start(f32[512]{0:T(512)} %broadcast_multiply_fusion.14) | copy-start | bytes 6148
  763.1 34.8 %copy-start.7 = (f32[512,768]{1,0:T(8,128)S(1)}, f32[512,768]{1,0:T(8,128)}, u32[]{:S(2)}) copy-start(f32[512,768]{1,0:T(8,128)} %copy-done.5) | copy-start | bytes 4718596
  763.1 34.8 %copy-start.119 = (f32[512]{0:T(512)S(1)}, f32[512]{0:T(512)}, u32[]{:S(2)}) copy-start(f32[512]{0:T(512)} %copy-done.118) | copy-start | bytes 6148
  763.1 100.2 %all-reduce.48.cloned.1.call-start = ((), (), s32[]{:S(2)}) async-start(), calls=%async_computation.14 | async-start | bytes 1572864 | tf_op jit(solution)/shard_map/psum | solution.py:23
  798.0 23.7 %slice-start.2 = ((s8[6291456]{0:T(1024)(128)(4,1)}), s8[2097152]{0:T(1024)(128)(4,1)S(1)}, s32[]{:S(2)}) async-start(s8[6291456]{0:T(1024)(128)(4,1)} %bitcast.792), calls=%async_computation.19 | async-start | bytes 4194304
  801.4 20.3 %collective-permute-start.5 = (bf16[512,768]{1,0:T(8,128)(2,1)S(1)}, bf16[512,768]{1,0:T(8,128)(2,1)S(1)}, u32[]{:S(2)}, u32[]{:S(2)}) collective-permute-start(bf16[512,768]{1,0:T(8,128)(2,1)S(1)} %get-tuple-element.117), channel_id=1, source_target_pairs={{16,0},{17,1},{18,2},{19,3},{20,4},{21,5},{22,6},{23,7},{24,8},{25... | collective-permute-start | bytes 2359304 | tf_op jit(solution)/shard_map/ppermute | solution.py:15
  828.7 84.5 %all-reduce.50.cloned.1.call-start = ((), (), s32[]{:S(2)}) async-start(), calls=%async_computation.15 | async-start | bytes 1572864 | tf_op jit(solution)/shard_map/psum | solution.py:23
  837.1 26.2 %copy-start.125 = (f32[512]{0:T(512)S(1)}, f32[512]{0:T(512)}, u32[]{:S(2)}) copy-start(f32[512]{0:T(512)} %broadcast_multiply_fusion.7) | copy-start | bytes 6148
  840.4 26.1 %copy-start.131 = (f32[512]{0:T(512)S(1)}, f32[512]{0:T(512)}, u32[]{:S(2)}) copy-start(f32[512]{0:T(512)} %add_rsqrt_fusion.1) | copy-start | bytes 6148
  878.4 172.8 %all-reduce.52.cloned.1.call-start = ((), (), s32[]{:S(2)}) async-start(), calls=%async_computation.16 | async-start | bytes 7077888 | tf_op jit(solution)/shard_map/psum | solution.py:319
  (195 other events, 688.0 us)
Sparse Core Ops, SparseCore 0:
  16.6 37.2 all-reduce.19
  64.9 34.6 all-reduce.21
  133.1 36.0 all-reduce.23
  179.9 34.6 all-reduce.25
  249.3 36.0 all-reduce.27
  296.3 34.6 all-reduce.29
  369.6 36.0 all-reduce.31
  422.2 34.6 all-reduce.33
  480.1 34.6 all-reduce.35
  533.3 34.6 all-reduce.37
  601.4 34.5 all-reduce.39
  648.8 34.6 all-reduce.41
  715.9 34.5 all-reduce.43
  763.2 34.6 all-reduce.45
  828.9 34.4 all-reduce.47
  878.5 34.6 all-reduce.49
  916.3 134.8 all-reduce.51
where the time goes:
time: 1070 us; the launch traced here: 1060 us
  waiting for transfers between devices  656 us (61%)
  matrix products  141 us (13%)
  other arithmetic  128 us (12%)
  local copies, waits for them, and re-layouts  84.8 us (8%)
  blocking collectives  18.9 us (2%)
  starting transfers between devices  18.6 us (2%)
  between operations  17.1 us (2%)
    psum x8, waiting for transfers between devices, combine_forward(): lax.psum(partial_value.astype(jnp.bfloat16), 'tensor').astype(jnp.float32)  249 us
    psum x8, waiting for transfers between devices, combine_backward(): lax.psum(partial_value.astype(jnp.bfloat16), 'tensor').astype(jnp.float32)  201 us
    psum x1, waiting for transfers between devices, body(): lax.psum(grad_qkv.astype(jnp.bfloat16), 'dp').astype(jnp.float32)  133 us
    ppermute x6, waiting for transfers between devices, from_behind(): return lax.ppermute(x, axis, pairs)  72.5 us
    dot_general x16, matrix products, contract_rows(): lax.dot_general(left, right, (((0,), (0,)), ((), ())), preferred_element_...  64.2 us
    unnamed x447, local copies, waits for them, and re-layouts  39 us
    dot_general x16, matrix products, contract_cols(): lax.dot_general(left, right, (((1,), (1,)), ((), ())), preferred_element_...  28.4 us
    reduce_sum x8, other arithmetic, norm_back(): grad_gain = jnp.sum(grad_output * normed, 0)  24 us
  transfers between devices with their start and end apart: 23, of which 23 were waited for; matrix products, arithmetic and copies ran while one was open for 12% of the time, Pallas kernels for 0%

commit v1 on v0

v1 whole, which is shorter than its diff:
```python
import jax
import jax.numpy as jnp
from jax import lax
from jax.sharding import PartitionSpec as P

HEAD = 64
epsilon = 1e-05
bf16 = jnp.bfloat16
f32 = jnp.float32


def to_partner(x, bits):
    size = lax.axis_size("tensor")
    return lax.ppermute(x, "tensor", [(i, i ^ bits) for i in range(size)])


def gather(x):
    near = to_partner(x, 1)
    far = to_partner(x, 2)
    return [x, near, far, to_partner(far, 1)]


def dot(left, right):
    return jnp.dot(left, right, preferred_element_type=f32)


def contract_rows(left, right):
    return lax.dot_general(left, right, (((0,), (0,)), ((), ())), preferred_element_type=f32)


def contract_cols(left, right):
    return lax.dot_general(left, right, (((1,), (1,)), ((), ())), preferred_element_type=f32)


def standardize(summed):
    center = summed - jnp.mean(summed, -1, keepdims=True)
    inverse = lax.rsqrt(jnp.mean(center * center, -1, keepdims=True) + epsilon)
    return (center * inverse, inverse)


def layer_norm(summed, gain, shift):
    normed, inverse = standardize(summed)
    return normed * gain + shift


def norm_back(summed, gain, grad_output):
    normed, inverse = standardize(summed)
    scaled = grad_output * gain
    grad_summed = inverse * (
        scaled
        - jnp.mean(scaled, -1, keepdims=True)
        - normed * jnp.mean(scaled * normed, -1, keepdims=True)
    )
    return normed, grad_summed


def gelu_value(value):
    return jax.nn.gelu(value, approximate=False)


def gelu_slope(value):
    normal_cdf = 0.5 * (1.0 + lax.erf(value * 0.7071067811865476))
    density = jnp.exp(-0.5 * value * value) * 0.3989422804014327
    return normal_cdf + value * density


def split_heads(mixed, segments):
    count, length = segments.shape
    width = mixed.shape[1] // 3
    parts = mixed.reshape(count, length, 3, width // HEAD, HEAD)
    return (parts[:, :, 0], parts[:, :, 1], parts[:, :, 2])


def probabilities(query, keys, segments):
    raw = jnp.einsum("sqhd,skhd->shqk", query, keys, preferred_element_type=f32) * HEAD**-0.5
    same = segments[:, None, :, None] == segments[:, None, None, :]
    return jax.nn.softmax(jnp.where(same, raw, -1000000000.0), axis=-1)


def attend(mixed, segments):
    query, keys, value = split_heads(mixed, segments)
    probs = probabilities(query, keys, segments).astype(bf16)
    result = jnp.einsum("shqk,skhd->sqhd", probs, value, preferred_element_type=f32)
    return result.astype(bf16).reshape(mixed.shape[0], -1)


def attend_back(mixed, segments, grad_result):
    query, keys, value = split_heads(mixed, segments)
    probs = probabilities(query, keys, segments)
    grad_heads = grad_result.reshape(query.shape)
    grad_probs = jnp.einsum("sqhd,skhd->shqk", grad_heads, value, preferred_element_type=f32)
    grad_value = jnp.einsum(
        "shqk,sqhd->skhd", probs.astype(bf16), grad_heads, preferred_element_type=f32
    )
    inner = jnp.sum(probs * grad_probs, -1, keepdims=True)
    grad_scores = (probs * (grad_probs - inner)).astype(bf16)
    scale = HEAD**-0.5
    grad_query = jnp.einsum("shqk,skhd->sqhd", grad_scores, keys, preferred_element_type=f32) * scale
    grad_keys = jnp.einsum("shqk,sqhd->skhd", grad_scores, query, preferred_element_type=f32) * scale
    stacked = jnp.stack([grad_query, grad_keys, grad_value], 2)
    return stacked.reshape(mixed.shape).astype(bf16)


def forward(rows, segments, w):
    mixed = [
        (dot(rows, w["qkv"][s]) + w["bias_mixed"][s]).astype(bf16) for s in range(4)
    ]
    attended = [attend(m, segments) for m in mixed]
    first = sum(dot(attended[s], w["out"][s]) for s in range(4)) + w["bias_out"] + rows.astype(f32)
    hidden = layer_norm(first, w["gain_one"], w["shift_one"])
    hidden_low = hidden.astype(bf16)
    upward = [dot(hidden_low, w["up"][s]) + w["bias_up"][s] for s in range(4)]
    second = sum(dot(gelu_value(upward[s]).astype(bf16), w["down"][s]) for s in range(4))
    second = second + w["bias_down"] + hidden
    out = layer_norm(second, w["gain_two"], w["shift_two"])
    return out, (rows, mixed, attended, first, hidden_low, upward, second)


def backward(grad_output, segments, kept, w, weights_too):
    rows, mixed, attended, first, hidden_low, upward, second = kept
    normed, grad_second = norm_back(second, w["gain_two"], grad_output)
    branch_two = grad_second.astype(bf16)
    grad_upward = [
        (contract_cols(branch_two, w["down"][s]) * gelu_slope(upward[s])).astype(bf16)
        for s in range(4)
    ]
    grad_hidden = sum(contract_cols(grad_upward[s], w["up"][s]) for s in range(4)) + grad_second
    normed_one, grad_first = norm_back(first, w["gain_one"], grad_hidden)
    branch_one = grad_first.astype(bf16)
    grad_mixed = [
        attend_back(mixed[s], segments, contract_cols(branch_one, w["out"][s]).astype(bf16))
        for s in range(4)
    ]
    grad_in = sum(contract_cols(grad_mixed[s], w["qkv"][s]) for s in range(4)) + grad_first
    if not weights_too:
        return grad_in
    common = [
        jnp.sum(grad_first, 0),
        jnp.sum(grad_hidden * normed_one, 0),
        jnp.sum(grad_hidden, 0),
        jnp.sum(grad_second, 0),
        jnp.sum(grad_output * normed, 0),
        jnp.sum(grad_output, 0),
    ]
    grads = []
    for s in range(4):
        width = attended[s].shape[1]
        from_mixed = jnp.sum(grad_mixed[s], 0, dtype=f32)
        from_qv = jnp.concatenate([from_mixed[:width], from_mixed[2 * width :]])
        from_qv = jnp.pad(from_qv, (0, rows.shape[1] - 2 * width))
        from_up = jnp.sum(grad_upward[s], 0, dtype=f32)
        grads.append(
            (
                contract_rows(gelu_value(upward[s]).astype(bf16), branch_two).astype(bf16),
                contract_rows(hidden_low, grad_upward[s]).astype(bf16),
                contract_rows(attended[s], branch_one).astype(bf16),
                contract_rows(rows, grad_mixed[s]).astype(bf16),
                jnp.stack([from_up, from_qv] + common),
            )
        )
    return grad_in, grads


def add(left, right):
    return (left.astype(f32) + right.astype(f32)).astype(left.dtype)


def sum_over_dp(part):
    return lax.psum(part, "dp")


def combine(parts):
    far = add(parts[2], to_partner(parts[3], 1))
    own = add(parts[0], to_partner(parts[1], 1))
    return sum_over_dp(add(own, to_partner(far, 2)))


def body(
    ends_in,
    segment_ids,
    w_qkv,
    bias_qv,
    w_out,
    bias_out,
    gain_one,
    shift_one,
    w_up,
    bias_up,
    w_down,
    bias_down,
    gain_two,
    shift_two,
):
    section = lax.axis_index("section")
    place = lax.axis_index("tensor")
    _, micro, count, length, width = ends_in.shape
    share = count // lax.axis_size("tensor")
    own = lax.dynamic_slice_in_dim(ends_in[0], place * share, share, 1)
    own = own.reshape(micro * share * length, width)
    segments = lax.dynamic_slice_in_dim(segment_ids, place * share, share, 1)
    segments = segments.reshape(micro * share, length)
    third = w_qkv.shape[3]
    biases = gather(jnp.concatenate([bias_qv[0, 0], bias_qv[0, 1], bias_up[0]])[None])
    biases = [b[0].astype(f32) for b in biases]
    none = jnp.zeros((third,), f32)
    w = {
        "qkv": gather(w_qkv[0].reshape(width, 3 * third)),
        "out": gather(w_out[0]),
        "up": gather(w_up[0]),
        "down": gather(w_down[0]),
        "bias_mixed": [jnp.concatenate([b[:third], none, b[third : 2 * third]]) for b in biases],
        "bias_up": [b[2 * third :] for b in biases],
        "bias_out": bias_out[0].astype(f32),
        "gain_one": gain_one[0].astype(f32),
        "shift_one": shift_one[0].astype(f32),
        "bias_down": bias_down[0].astype(f32),
        "gain_two": gain_two[0].astype(f32),
        "shift_two": shift_two[0].astype(f32),
    }
    out, _ = forward(own, segments, w)
    received = lax.ppermute(out.astype(bf16), "section", [(0, 1)])
    rows = jnp.where(section == 0, own, received)
    out, kept = forward(rows, segments, w)
    grad_in = backward(own.astype(f32), segments, kept, w, False)
    returned = lax.ppermute(grad_in.astype(bf16), "section", [(1, 0)])
    cotangent = jnp.where(section == 1, own, returned).astype(f32)
    grad_in, grads = backward(cotangent, segments, kept, w, True)

    down, up, outer, qkv, small = [
        combine([grads[s][i] for s in range(4)]) for i in range(5)
    ]
    ends = jnp.where(section == 1, out, grad_in).astype(bf16)
    ends = ends.reshape(micro, share, length, width)
    ends = lax.all_gather(ends, "tensor", axis=1, tiled=True)
    small = small.astype(f32)
    from_qv = jnp.stack([small[1, :third], small[1, third : 2 * third]])
    results = (
        ends,
        qkv.reshape(width, 3, third),
        from_qv,
        outer,
        small[2],
        small[3],
        small[4],
        up,
        small[0],
        down,
        small[5],
        small[6],
        small[7],
    )
    return tuple(item.astype(f32)[None] for item in results)


def solution(mesh):
    return jax.shard_map(
        body,
        mesh=mesh,
        in_specs=(
            P("section", None, "dp", None, None),
            P(None, "dp", None),
            P("section", None, None, "tensor"),
            P("section", None, "tensor"),
            P("section", "tensor", None),
            P("section", None),
            P("section", None),
            P("section", None),
            P("section", None, "tensor"),
            P("section", "tensor"),
            P("section", "tensor", None),
            P("section", None),
            P("section", None),
            P("section", None),
        ),
        out_specs=(
            P("section", None, "dp", None, None),
            P("section", None, None, "tensor"),
            P("section", None, "tensor"),
            P("section", "tensor", None),
            P("section", None),
            P("section", None),
            P("section", None),
            P("section", None, "tensor"),
            P("section", "tensor"),
            P("section", "tensor", None),
            P("section", None),
            P("section", None),
            P("section", None),
        ),
        check_vma=False,
    )
```

time: 1070 us -> 639 us (0.60)
  waiting for transfers between devices: 656 us -> 251 us
  other arithmetic: 128 us -> 40.8 us
  matrix products: 141 us -> 217 us
  local copies, waits for them, and re-layouts: 84.8 us -> 58 us
    psum x17 -> x1, waiting for transfers between devices: 583 us -> 104 us  [sum_over_dp(): return lax.psum(part, 'dp')]
    ppermute x6 -> x32, waiting for transfers between devices: 72.5 us -> 148 us  [the longest x30 120 us: to_partner(): return lax.ppermute(x, 'tensor', [(i, i ^ bits) for i in range(size)])]
    dot_general x40 -> x64, matrix products: 47.1 us -> 116 us  [the longest x28 80.7 us: dot(): return jnp.dot(left, right, preferred_element_type=f32)]
    reduce_sum x30 -> x8, other arithmetic: 57.4 us -> 7.89 us  [the longest x4 3.2 us: backward(): from_mixed = jnp.sum(grad_mixed[s], 0, dtype=f32)]
    dot_general x16, matrix products: 64.2 us -> 18.5 us  [contract_rows(): lax.dot_general(left, right, (((0,), (0,)), ((), ())), preferred_element_...]
    dot_general x16 -> x28, matrix products: 28.4 us -> 65.8 us  [contract_cols(): lax.dot_general(left, right, (((1,), (1,)), ((), ())), preferred_element_...]
    unnamed x447 -> x379, local copies, waits for them, and re-layouts: 39 us -> 15.4 us
    another operation x8 -> x4, other arithmetic: 18.4 us -> 0.21 us  [attend_back(): stacked = jnp.stack([grad_query, grad_keys, grad_value], 2)]
  transfers between devices with their start and end apart: 23 -> 34, of which waited for: 23 -> 12; matrix products, arithmetic and copies ran while one was open for 12% -> 13% of each run, Pallas kernels for 0% -> 0%
where the time goes in v1:
time: 639 us; the launch traced here: 631 us
  waiting for transfers between devices  251 us (39%)
  matrix products  217 us (34%)
  local copies, waits for them, and re-layouts  58 us (9%)
  other arithmetic  40.8 us (6%)
  starting transfers between devices  24.6 us (4%)
  blocking collectives  20.3 us (3%)
  between operations  18.4 us (3%)
    ppermute x30, waiting for transfers between devices, to_partner(): return lax.ppermute(x, 'tensor', [(i, i ^ bits) for i in range(size)])  120 us
    psum x1, waiting for transfers between devices, sum_over_dp(): return lax.psum(part, 'dp')  104 us
    dot_general x28, matrix products, dot(): return jnp.dot(left, right, preferred_element_type=f32)  80.7 us
    dot_general x28, matrix products, contract_cols(): lax.dot_general(left, right, (((1,), (1,)), ((), ())), preferred_element_...  65.8 us
    psum x1, blocking collectives, sum_over_dp(): return lax.psum(part, 'dp')  20.3 us
    ppermute x30, starting transfers between devices, to_partner(): return lax.ppermute(x, 'tensor', [(i, i ^ bits) for i in range(size)])  19.3 us
    dot_general x16, matrix products, contract_rows(): lax.dot_general(left, right, (((0,), (0,)), ((), ())), preferred_element_...  18.5 us
    ppermute x1, waiting for transfers between devices, body(): returned = lax.ppermute(grad_in.astype(bf16), 'section', [(1, 0)])  15.4 us
  transfers between devices with their start and end apart: 34, of which 12 were waited for; matrix products, arithmetic and copies ran while one was open for 13% of the time, Pallas kernels for 0%

profile of v1, /device:TPU:0, one launch (start us, length us, event | category | flops | bytes accessed | tf_op | source)
XLA Modules:
  0.0 630.9 jit_solution(16838593031795549325)
XLA Ops:
  9.7 3.0 collective-permute-start.4
  30.3 2.6 fusion.45
  37.8 4.9 collective-permute-done.3
  42.7 2.6 fusion.46
  56.3 11.7 %collective-permute-done.12 = bf16[768,768]{1,0:T(8,128)(2,1)} collective-permute-done((bf16[768,768]{1,0:T(8,128)(2,1)}, bf16[768,768]{1,0:T(8,128)(2,1)}, u32[]{:S(2)}, u32[]{:S(2)}) %collective-permute-start.12) | collective-permute-done | bytes 1179680 | tf_op jit(solution)/shard_map/ppermute | solution.py:14
  68.0 25.0 %collective-permute-done.11 = bf16[768,768]{1,0:T(8,128)(2,1)} collective-permute-done((bf16[768,768]{1,0:T(8,128)(2,1)}, bf16[768,768]{1,0:T(8,128)(2,1)}, u32[]{:S(2)}, u32[]{:S(2)}) %collective-permute-start.11) | collective-permute-done | bytes 1179680 | tf_op jit(solution)/shard_map/ppermute | solution.py:14
  100.0 6.4 %fusion.184 = f32[384,768]{1,0:T(8,128)} fusion(f32[768]{0:T(1024)S(1)} %copy-done.180, bf16[1,768,768]{2,1,0:T(8,128)(2,1)} %param.24, bf16[1,768,768]{2,1,0:T(8,128)(2,1)} %param.22, f32[384,768]{1,0:T(8,128)S(1)} %get-tuple-element.100, f32[768]{0:T(1024)S(1)} %copy-done.150, f32[768]{0:T(1024)S(1)} %get-tuple-element.150, f32[384]{0:T(512)S(1)} %add_rsqrt_fusion.3, ...), kind=kOutput, calls=%fused_computation.384 | convolution fusion | flops 926908416 | bytes 4730880 | tf_op jit(solution)/shard_map/dot_general | solution.py:24
  106.4 7.2 %convolution_add_fusion.26 = f32[384,768]{1,0:T(8,128)} fusion(f32[384,768]{1,0:T(8,128)} %fusion.184, bf16[768,768]{1,0:T(8,128)(2,1)} %collective-permute-done.10, bf16[768,768]{1,0:T(8,128)(2,1)} %collective-permute-done.9, f32[768]{0:T(1024)S(1)} %copy-done.174, f32[384,768]{1,0:T(8,128)S(1)} %get-tuple-element.100, f32[768]{0:T(1024)S(1)} %copy-done.150, ...), kind=kOutput, calls=%fused_computation.98 | convolution fusion | flops 927203328 | bytes 5910528 | tf_op jit(solution)/shard_map/dot_general | solution.py:24
  113.6 6.8 %convolution_add_fusion.24 = f32[384,768]{1,0:T(8,128)} fusion(f32[384,768]{1,0:T(8,128)} %convolution_add_fusion.26, bf16[768,768]{1,0:T(8,128)(2,1)} %collective-permute-done.12, bf16[768,768]{1,0:T(8,128)(2,1)} %collective-permute-done.11, f32[768]{0:T(1024)S(1)} %copy-done.176, f32[384,768]{1,0:T(8,128)S(1)} %get-tuple-element.100, ...), kind=kOutput, calls=%fused_computation.96 | convolution fusion | flops 927203328 | bytes 5910528 | tf_op jit(solution)/shard_map/dot_general | solution.py:24
  120.4 6.8 %fusion.636 = (f32[384]{0:T(512)S(1)}, f32[384,768]{1,0:T(8,128)}) fusion(f32[768]{0:T(1024)S(1)} %copy-done.150, f32[768]{0:T(1024)S(1)} %get-tuple-element.150, f32[384]{0:T(512)S(1)} %add_rsqrt_fusion.3, f32[384,768]{1,0:T(8,128)S(1)} %get-tuple-element.100, f32[384]{0:T(512)S(1)} %broadcast_multiply_fusion.10, f32[768]{0:T(1024)S(1)} %copy-done.171, ...), kind=kOutput, calls=%fused_computation.948 | convolution fusion | flops 929267328 | bytes 5915136 | tf_op jit(solution)/shard_map/dot_general | solution.py:24
  129.1 3.7 collective-permute-start.15
  133.5 12.1 %collective-permute-done.15 = bf16[384,768]{1,0:T(8,128)(2,1)S(1)} collective-permute-done((bf16[384,768]{1,0:T(8,128)(2,1)S(1)}, bf16[384,768]{1,0:T(8,128)(2,1)S(1)}, u32[]{:S(2)}, u32[]{:S(2)}) %collective-permute-start.15) | collective-permute-done | bytes 589856 | tf_op jit(solution)/shard_map/ppermute | solution.py:221
  152.1 2.6 fusion.49
  154.7 2.3 reshape.324
  159.1 2.2 fusion.640
  163.5 2.6 fusion.50
  170.3 2.2 fusion.641
  174.1 2.7 fusion.51
  180.9 2.2 fusion.642
  187.0 5.3 fusion.91
  194.5 5.1 fusion.94
  199.6 5.3 fusion.97
  204.9 5.7 fusion.100
  219.5 4.5 fusion.68
  224.0 4.8 convolution_add_fusion.11
  228.8 4.8 convolution_add_fusion.10
  233.6 5.9 fusion.607
  254.1 2.2 fusion.202
  262.1 2.2 fusion.203
  281.8 2.9 fusion.30
  286.0 15.4 %collective-permute-done.16 = bf16[384,768]{1,0:T(8,128)(2,1)} collective-permute-done((bf16[384,768]{1,0:T(8,128)(2,1)}, bf16[384,768]{1,0:T(8,128)(2,1)}, u32[]{:S(2)}, u32[]{:S(2)}) %collective-permute-start.16) | collective-permute-done | bytes 589856 | tf_op jit(solution)/shard_map/ppermute | solution.py:225
  301.4 2.3 fusion.117
  306.0 2.7 convert_reduce_fusion.4
  310.9 2.8 convert_reduce_fusion.3
  313.8 3.0 convert_reduce_fusion.2
  316.7 2.9 convert_reduce_fusion.1
  323.8 2.9 multiply_reduce_fusion
  379.8 2.8 fusion.35
  390.6 9.3 %collective-permute-done.25 = bf16[192,768]{1,0:T(8,128)(2,1)S(1)} collective-permute-done((bf16[192,768]{1,0:T(8,128)(2,1)S(1)}, bf16[192,768]{1,0:T(8,128)(2,1)S(1)}, u32[]{:S(2)}, u32[]{:S(2)}) %collective-permute-start.25) | collective-permute-done | bytes 294944 | tf_op jit(solution)/shard_map/ppermute | solution.py:14
  401.5 2.5 collective-permute-start.19
  409.6 19.1 %collective-permute-done.19 = bf16[768,576]{0,1:T(8,128)(2,1)S(1)} collective-permute-done((bf16[768,576]{0,1:T(8,128)(2,1)S(1)}, bf16[768,576]{0,1:T(8,128)(2,1)S(1)}, u32[]{:S(2)}, u32[]{:S(2)}) %collective-permute-start.19) | collective-permute-done | bytes 884768 | tf_op jit(solution)/shard_map/ppermute | solution.py:14
  429.9 24.0 %collective-permute-done.28 = bf16[768,768]{1,0:T(8,128)(2,1)S(1)} collective-permute-done((bf16[768,768]{1,0:T(8,128)(2,1)S(1)}, bf16[768,768]{1,0:T(8,128)(2,1)S(1)}, u32[]{:S(2)}, u32[]{:S(2)}) %collective-permute-start.28) | collective-permute-done | bytes 1179680 | tf_op jit(solution)/shard_map/ppermute | solution.py:14
  455.3 23.7 %collective-permute-done.31 = bf16[768,768]{1,0:T(8,128)(2,1)S(1)} collective-permute-done((bf16[768,768]{1,0:T(8,128)(2,1)S(1)}, bf16[768,768]{1,0:T(8,128)(2,1)S(1)}, u32[]{:S(2)}, u32[]{:S(2)}) %collective-permute-start.31) | collective-permute-done | bytes 1179680 | tf_op jit(solution)/shard_map/ppermute | solution.py:14
  484.6 2.2 collective-permute-done.22
  486.8 20.3 %psum.36 = f32[8,768]{1,0:T(8,128)S(1)} all-reduce(f32[8,768]{1,0:T(8,128)S(1)} %add_add_fusion), channel_id=1, replica_groups=mesh['section'=2,'dp'=4,'tensor'=4] {'dp'}, use_global_device_ids=true, to_apply=%region_55.56 | all-reduce | flops 6144 | bytes 49152 | tf_op jit(solution)/shard_map/psum | solution.py:169
  508.4 4.3 bitcast_convert_fusion
  512.7 103.6 %all-reduce.7.cloned.1.call-done = (bf16[1,768,3,192]{1,3,2,0:T(8,128)(2,1)}, bf16[1,192,768]{2,1,0:T(8,128)(2,1)}, bf16[1,768,768]{2,1,0:T(8,128)(2,1)}, bf16[1,768,768]{2,1,0:T(8,128)(2,1)}) async-done(((bf16[1,768,3,192]{1,3,2,0:T(8,128)(2,1)}, bf16[1,192,768]{2,1,0:T(8,128)(2,1)}, bf16[1,768,768]{2,1,0:T(8,128)(2,1)}, bf16[1,768,768]{2,1,0:T(8,128)(2,1)}), (bf16[1,768,3,192]{1,3,2,0:T(8,128)(2,1)}, ...) | async-done | bytes 3538960 | tf_op jit(solution)/shard_map/psum | solution.py:169
  616.3 2.6 convert_element_type.641
  (686 shorter events, 207.8 us)
Async XLA Ops:
  8.0 500.3 %all-gather.2.cloned.1.call-start = ((), (), s32[]{:S(2)}) async-start(), calls=%async_computation | async-start | bytes 2949120 | tf_op jit(solution)/shard_map/all_gather | solution.py:234
  9.7 12.8 %collective-permute-start.4 = (bf16[1,1152]{1,0:T(2,128)(2,1)S(1)}, bf16[1,1152]{1,0:T(2,128)(2,1)S(1)}, u32[]{:S(2)}, u32[]{:S(2)}) collective-permute-start(bf16[1,1152]{1,0:T(2,128)(2,1)S(1)} %broadcast_in_dim.101), channel_id=1, source_target_pairs={{0,2},{1,3},{2,0},{3,1},{4,6},{5,7},{6,4},{7,5},{8,10},{9,11},{10,... | collective-permute-start | bytes 6920 | tf_op jit(solution)/shard_map/ppermute | solution.py:14
  12.6 7.2 %collective-permute-start.1 = (bf16[1,1152]{1,0:T(2,128)(2,1)S(1)}, bf16[1,1152]{1,0:T(2,128)(2,1)S(1)}, u32[]{:S(2)}, u32[]{:S(2)}) collective-permute-start(bf16[1,1152]{1,0:T(2,128)(2,1)S(1)} %broadcast_in_dim.101), channel_id=1, source_target_pairs={{0,1},{1,0},{2,3},{3,2},{4,5},{5,4},{6,7},{7,6},{8,9},{9,8},{10,11... | collective-permute-start | bytes 6920 | tf_op jit(solution)/shard_map/ppermute | solution.py:14
  12.6 41.2 %collective-permute-start.2 = (bf16[192,768]{1,0:T(8,128)(2,1)}, bf16[192,768]{1,0:T(8,128)(2,1)S(1)}, u32[]{:S(2)}, u32[]{:S(2)}) collective-permute-start(bf16[192,768]{1,0:T(8,128)(2,1)} %bitcast.674), channel_id=1, source_target_pairs={{0,1},{1,0},{2,3},{3,2},{4,5},{5,4},{6,7},{7,6},{8,9},{9,8},{10,11... | collective-permute-start | bytes 884744 | tf_op jit(solution)/shard_map/ppermute | solution.py:14
  13.1 41.7 %collective-permute-start.5 = (bf16[192,768]{1,0:T(8,128)(2,1)}, bf16[192,768]{1,0:T(8,128)(2,1)S(1)}, u32[]{:S(2)}, u32[]{:S(2)}) collective-permute-start(bf16[192,768]{1,0:T(8,128)(2,1)} %bitcast.675), channel_id=1, source_target_pairs={{0,2},{1,3},{2,0},{3,1},{4,6},{5,7},{6,4},{7,5},{8,10},{9,11},{10,... | collective-permute-start | bytes 884744 | tf_op jit(solution)/shard_map/ppermute | solution.py:14
  13.2 15.1 %collective-permute-start = (bf16[768,576]{0,1:T(8,128)(2,1)}, bf16[768,576]{0,1:T(8,128)(2,1)}, u32[]{:S(2)}, u32[]{:S(2)}) collective-permute-start(bf16[768,576]{0,1:T(8,128)(2,1)} %bitcast.1), channel_id=1, source_target_pairs={{0,1},{1,0},{2,3},{3,2},{4,5},{5,4},{6,7},{7,6},{8,9},{9,8},{10,11... | collective-permute-start | bytes 2654216 | tf_op jit(solution)/shard_map/ppermute | solution.py:14
  14.7 36.5 %copy-start.43 = (pred[3,128,128]{1,2,0:T(8,128)(4,1)}, pred[3,128,128]{1,2,0:T(8,128)(4,1)S(1)}, u32[]{:S(2)}) copy-start(pred[3,128,128]{1,2,0:T(8,128)(4,1)S(1)} %broadcast_compare_fusion) | copy-start | bytes 147460
  16.1 198.6 %copy-start.126 = (f32[768]{0:T(1024)}, f32[768]{0:T(1024)S(1)}, u32[]{:S(2)}) copy-start(f32[768]{0:T(1024)S(1)} %get-tuple-element.150) | copy-start | bytes 9220
  16.8 112.1 %copy-start.128 = (f32[768]{0:T(1024)}, f32[768]{0:T(1024)S(1)}, u32[]{:S(2)}) copy-start(f32[768]{0:T(1024)S(1)} %get-tuple-element.151) | copy-start | bytes 9220
  19.9 22.8 %collective-permute-start.3 = (bf16[768,576]{0,1:T(8,128)(2,1)}, bf16[768,576]{0,1:T(8,128)(2,1)}, u32[]{:S(2)}, u32[]{:S(2)}) collective-permute-start(bf16[768,576]{0,1:T(8,128)(2,1)} %bitcast.1), channel_id=1, source_target_pairs={{0,2},{1,3},{2,0},{3,1},{4,6},{5,7},{6,4},{7,5},{8,10},{9,11},{10,... | collective-permute-start | bytes 2654216 | tf_op jit(solution)/shard_map/ppermute | solution.py:14
  22.5 1.2 collective-permute-start.7
  23.7 44.3 %collective-permute-start.12 = (bf16[768,768]{1,0:T(8,128)(2,1)}, bf16[768,768]{1,0:T(8,128)(2,1)}, u32[]{:S(2)}, u32[]{:S(2)}) collective-permute-start(bf16[768,768]{1,0:T(8,128)(2,1)} %bitcast.26), channel_id=1, source_target_pairs={{0,2},{1,3},{2,0},{3,1},{4,6},{5,7},{6,4},{7,5},{8,10},{9,11},{10,... | collective-permute-start | bytes 3538952 | tf_op jit(solution)/shard_map/ppermute | solution.py:14
  24.0 18.7 %copy-start.162 = (f32[576]{0:T(1024)}, f32[576]{0:T(1024)S(1)}, u32[]{:S(2)}) copy-start(f32[576]{0:T(1024)S(1)} %get-tuple-element.97) | copy-start | bytes 6916
  24.0 69.5 %copy-start.160 = (f32[576]{0:T(1024)}, f32[576]{0:T(1024)S(1)}, u32[]{:S(2)}) copy-start(f32[576]{0:T(1024)S(1)} %get-tuple-element.95) | copy-start | bytes 6916
  28.3 64.7 %collective-permute-start.11 = (bf16[768,768]{1,0:T(8,128)(2,1)}, bf16[768,768]{1,0:T(8,128)(2,1)}, u32[]{:S(2)}, u32[]{:S(2)}) collective-permute-start(bf16[768,768]{1,0:T(8,128)(2,1)} %bitcast.25), channel_id=1, source_target_pairs={{0,2},{1,3},{2,0},{3,1},{4,6},{5,7},{6,4},{7,5},{8,10},{9,11},{10,... | collective-permute-start | bytes 3538952 | tf_op jit(solution)/shard_map/ppermute | solution.py:14
  49.6 43.4 %collective-permute-start.6 = (bf16[768,576]{0,1:T(8,128)(2,1)}, bf16[768,576]{0,1:T(8,128)(2,1)}, u32[]{:S(2)}, u32[]{:S(2)}) collective-permute-start(bf16[768,576]{0,1:T(8,128)(2,1)} %collective-permute-done.3), channel_id=1, source_target_pairs={{0,1},{1,0},{2,3},{3,2},{4,5},{5,4},{6,7},{7,6},{8,9},{9,8},{10,11... | collective-permute-start | bytes 2654216 | tf_op jit(solution)/shard_map/ppermute | solution.py:14
  53.9 130.8 %copy-start.21 = (bf16[192,768]{1,0:T(8,128)(2,1)}, bf16[192,768]{1,0:T(8,128)(2,1)S(1)}, u32[]{:S(2)}) copy-start(bf16[192,768]{1,0:T(8,128)(2,1)S(1)} %collective-permute-done.2) | copy-start | bytes 884740
  53.9 52.5 %collective-permute-start.10 = (bf16[768,768]{1,0:T(8,128)(2,1)}, bf16[768,768]{1,0:T(8,128)(2,1)}, u32[]{:S(2)}, u32[]{:S(2)}) collective-permute-start(bf16[768,768]{1,0:T(8,128)(2,1)} %bitcast.26), channel_id=1, source_target_pairs={{0,1},{1,0},{2,3},{3,2},{4,5},{5,4},{6,7},{7,6},{8,9},{9,8},{10,11... | collective-permute-start | bytes 3538952 | tf_op jit(solution)/shard_map/ppermute | solution.py:14
  54.8 130.3 %copy-start.18 = (bf16[192,768]{1,0:T(8,128)(2,1)}, bf16[192,768]{1,0:T(8,128)(2,1)S(1)}, u32[]{:S(2)}) copy-start(bf16[192,768]{1,0:T(8,128)(2,1)S(1)} %collective-permute-done.5) | copy-start | bytes 884740
  54.9 51.5 %collective-permute-start.9 = (bf16[768,768]{1,0:T(8,128)(2,1)}, bf16[768,768]{1,0:T(8,128)(2,1)}, u32[]{:S(2)}, u32[]{:S(2)}) collective-permute-start(bf16[768,768]{1,0:T(8,128)(2,1)} %bitcast.25), channel_id=1, source_target_pairs={{0,1},{1,0},{2,3},{3,2},{4,5},{5,4},{6,7},{7,6},{8,9},{9,8},{10,11... | collective-permute-start | bytes 3538952 | tf_op jit(solution)/shard_map/ppermute | solution.py:14
  68.0 29.3 %collective-permute-start.8 = (bf16[192,768]{1,0:T(8,128)(2,1)S(1)}, bf16[192,768]{1,0:T(8,128)(2,1)S(1)}, u32[]{:S(2)}, u32[]{:S(2)}) collective-permute-start(bf16[192,768]{1,0:T(8,128)(2,1)S(1)} %collective-permute-done.5), channel_id=1, source_target_pairs={{0,1},{1,0},{2,3},{3,2},{4,5},{5,4},{6,7},{7,6},{8,9},{9,8},{10,11... | collective-permute-start | bytes 884744 | tf_op jit(solution)/shard_map/ppermute | solution.py:14
  93.0 27.4 %collective-permute-start.14 = (bf16[768,768]{1,0:T(8,128)(2,1)}, bf16[768,768]{1,0:T(8,128)(2,1)}, u32[]{:S(2)}, u32[]{:S(2)}) collective-permute-start(bf16[768,768]{1,0:T(8,128)(2,1)} %collective-permute-done.12), channel_id=1, source_target_pairs={{0,1},{1,0},{2,3},{3,2},{4,5},{5,4},{6,7},{7,6},{8,9},{9,8},{10,11... | collective-permute-start | bytes 3538952 | tf_op jit(solution)/shard_map/ppermute | solution.py:14
  93.0 27.4 %collective-permute-start.13 = (bf16[768,768]{1,0:T(8,128)(2,1)}, bf16[768,768]{1,0:T(8,128)(2,1)}, u32[]{:S(2)}, u32[]{:S(2)}) collective-permute-start(bf16[768,768]{1,0:T(8,128)(2,1)} %collective-permute-done.11), channel_id=1, source_target_pairs={{0,1},{1,0},{2,3},{3,2},{4,5},{5,4},{6,7},{7,6},{8,9},{9,8},{10,11... | collective-permute-start | bytes 3538952 | tf_op jit(solution)/shard_map/ppermute | solution.py:14
  97.3 88.2 %copy-start.10 = (bf16[192,768]{1,0:T(8,128)(2,1)}, bf16[192,768]{1,0:T(8,128)(2,1)S(1)}, u32[]{:S(2)}) copy-start(bf16[192,768]{1,0:T(8,128)(2,1)S(1)} %collective-permute-done.8) | copy-start | bytes 884740
  129.1 16.5 %copy-start.167 = (f32[576]{0:T(1024)S(1)}, f32[576]{0:T(1024)}, u32[]{:S(2)}) copy-start(f32[576]{0:T(1024)} %copy-done.166) | copy-start | bytes 6916
  129.1 16.4 %collective-permute-start.15 = (bf16[384,768]{1,0:T(8,128)(2,1)S(1)}, bf16[384,768]{1,0:T(8,128)(2,1)S(1)}, u32[]{:S(2)}, u32[]{:S(2)}) collective-permute-start(bf16[384,768]{1,0:T(8,128)(2,1)S(1)} %add_convert_fusion.9), channel_id=1, source_target_pairs={{0,16},{1,17},{2,18},{3,19},{4,20},{5,21},{6,22},{7,23},{8,24},{9,... | collective-permute-start | bytes 1769480 | tf_op jit(solution)/shard_map/ppermute | solution.py:221
  187.0 17.9 %copy-start.8 = (bf16[384,768]{1,0:T(8,128)(2,1)}, bf16[384,768]{1,0:T(8,128)(2,1)S(1)}, u32[]{:S(2)}) copy-start(bf16[384,768]{1,0:T(8,128)(2,1)S(1)} %fusion.213) | copy-start | bytes 1769476
  199.6 11.1 %copy-start.93 = (bf16[384,768]{1,0:T(8,128)(2,1)}, bf16[384,768]{1,0:T(8,128)(2,1)S(1)}, u32[]{:S(2)}) copy-start(bf16[384,768]{1,0:T(8,128)(2,1)S(1)} %get-tuple-element.115) | copy-start | bytes 1769476
  284.7 16.7 %collective-permute-start.16 = (bf16[384,768]{1,0:T(8,128)(2,1)}, bf16[384,768]{1,0:T(8,128)(2,1)}, u32[]{:S(2)}, u32[]{:S(2)}) collective-permute-start(bf16[384,768]{1,0:T(8,128)(2,1)} %fusion.30), channel_id=1, source_target_pairs={{16,0},{17,1},{18,2},{19,3},{20,4},{21,5},{22,6},{23,7},{24,8},{25... | collective-permute-start | bytes 1769480 | tf_op jit(solution)/shard_map/ppermute | solution.py:225
  286.0 17.8 %copy-start.124 = (f32[384]{0:T(512)S(1)}, f32[384]{0:T(512)}, u32[]{:S(2)}) copy-start(f32[384]{0:T(512)} %copy-done.123) | copy-start | bytes 4612
  376.0 10.1 %collective-permute-start.24 = (bf16[192,768]{1,0:T(8,128)(2,1)}, bf16[192,768]{1,0:T(8,128)(2,1)}, u32[]{:S(2)}, u32[]{:S(2)}) collective-permute-start(bf16[192,768]{1,0:T(8,128)(2,1)} %convolution_convert_fusion.12), channel_id=1, source_target_pairs={{0,1},{1,0},{2,3},{3,2},{4,5},{5,4},{6,7},{7,6},{8,9},{9,8},{10,11... | collective-permute-start | bytes 884744 | tf_op jit(solution)/shard_map/ppermute | solution.py:14
  383.7 232.5 %all-reduce.7.cloned.1.call-start = ((), (), s32[]{:S(2)}) async-start(), calls=%async_computation.1 | async-start | bytes 7077888 | tf_op jit(solution)/shard_map/psum | solution.py:169
  384.0 16.7 %collective-permute-start.18 = (bf16[768,576]{0,1:T(8,128)(2,1)}, bf16[768,576]{0,1:T(8,128)(2,1)S(1)}, u32[]{:S(2)}, u32[]{:S(2)}) collective-permute-start(bf16[768,576]{0,1:T(8,128)(2,1)} %convolution_convert_fusion.8), channel_id=1, source_target_pairs={{0,1},{1,0},{2,3},{3,2},{4,5},{5,4},{6,7},{7,6},{8,9},{9,8},{10,11... | collective-permute-start | bytes 2654216 | tf_op jit(solution)/shard_map/ppermute | solution.py:14
  384.6 5.5 collective-permute-start.23
  384.7 16.8 %collective-permute-start.27 = (bf16[768,768]{1,0:T(8,128)(2,1)}, bf16[768,768]{1,0:T(8,128)(2,1)S(1)}, u32[]{:S(2)}, u32[]{:S(2)}) collective-permute-start(bf16[768,768]{1,0:T(8,128)(2,1)} %convolution_convert_fusion.4), channel_id=1, source_target_pairs={{0,1},{1,0},{2,3},{3,2},{4,5},{5,4},{6,7},{7,6},{8,9},{9,8},{10,11... | collective-permute-start | bytes 3538952 | tf_op jit(solution)/shard_map/ppermute | solution.py:14
  385.1 19.8 %collective-permute-start.30 = (bf16[768,768]{1,0:T(8,128)(2,1)}, bf16[768,768]{1,0:T(8,128)(2,1)S(1)}, u32[]{:S(2)}, u32[]{:S(2)}) collective-permute-start(bf16[768,768]{1,0:T(8,128)(2,1)} %convolution_convert_fusion), channel_id=1, source_target_pairs={{0,1},{1,0},{2,3},{3,2},{4,5},{5,4},{6,7},{7,6},{8,9},{9,8},{10,11... | collective-permute-start | bytes 3538952 | tf_op jit(solution)/shard_map/ppermute | solution.py:14
  387.4 12.5 %collective-permute-start.25 = (bf16[192,768]{1,0:T(8,128)(2,1)S(1)}, bf16[192,768]{1,0:T(8,128)(2,1)S(1)}, u32[]{:S(2)}, u32[]{:S(2)}) collective-permute-start(bf16[192,768]{1,0:T(8,128)(2,1)S(1)} %add_convert_fusion.11), channel_id=1, source_target_pairs={{0,2},{1,3},{2,0},{3,1},{4,6},{5,7},{6,4},{7,5},{8,10},{9,11},{10,... | collective-permute-start | bytes 884744 | tf_op jit(solution)/shard_map/ppermute | solution.py:14
  390.1 11.1 %copy-start.25 = (bf16[768,576]{0,1:T(8,128)(2,1)S(1)}, bf16[768,576]{0,1:T(8,128)(2,1)}, u32[]{:S(2)}) copy-start(bf16[768,576]{0,1:T(8,128)(2,1)} %convolution_convert_fusion.9) | copy-start | bytes 2654212
  390.5 19.1 %collective-permute-start.17 = (bf16[768,576]{0,1:T(8,128)(2,1)S(1)}, bf16[768,576]{0,1:T(8,128)(2,1)S(1)}, u32[]{:S(2)}, u32[]{:S(2)}) collective-permute-start(bf16[768,576]{0,1:T(8,128)(2,1)S(1)} %copy-done.77), channel_id=1, source_target_pairs={{0,1},{1,0},{2,3},{3,2},{4,5},{5,4},{6,7},{7,6},{8,9},{9,8},{10,11... | collective-permute-start | bytes 2654216 | tf_op jit(solution)/shard_map/ppermute | solution.py:14
  399.9 6.1 collective-permute-start.26
  400.7 8.0 %collective-permute-start.29 = (bf16[768,768]{1,0:T(8,128)(2,1)S(1)}, bf16[768,768]{1,0:T(8,128)(2,1)S(1)}, u32[]{:S(2)}, u32[]{:S(2)}) collective-permute-start(bf16[768,768]{1,0:T(8,128)(2,1)S(1)} %convolution_convert_fusion.2), channel_id=1, source_target_pairs={{0,1},{1,0},{2,3},{3,2},{4,5},{5,4},{6,7},{7,6},{8,9},{9,8},{10,11... | collective-permute-start | bytes 3538952 | tf_op jit(solution)/shard_map/ppermute | solution.py:14
  401.5 27.1 %collective-permute-start.19 = (bf16[768,576]{0,1:T(8,128)(2,1)S(1)}, bf16[768,576]{0,1:T(8,128)(2,1)S(1)}, u32[]{:S(2)}, u32[]{:S(2)}) collective-permute-start(bf16[768,576]{0,1:T(8,128)(2,1)S(1)} %add_convert_fusion.7), channel_id=1, source_target_pairs={{0,2},{1,3},{2,0},{3,1},{4,6},{5,7},{6,4},{7,5},{8,10},{9,11},{10,... | collective-permute-start | bytes 2654216 | tf_op jit(solution)/shard_map/ppermute | solution.py:14
  404.9 49.0 %collective-permute-start.28 = (bf16[768,768]{1,0:T(8,128)(2,1)S(1)}, bf16[768,768]{1,0:T(8,128)(2,1)S(1)}, u32[]{:S(2)}, u32[]{:S(2)}) collective-permute-start(bf16[768,768]{1,0:T(8,128)(2,1)S(1)} %add_convert_fusion.4), channel_id=1, source_target_pairs={{0,2},{1,3},{2,0},{3,1},{4,6},{5,7},{6,4},{7,5},{8,10},{9,11},{10,... | collective-permute-start | bytes 3538952 | tf_op jit(solution)/shard_map/ppermute | solution.py:14
  406.0 73.0 %collective-permute-start.31 = (bf16[768,768]{1,0:T(8,128)(2,1)S(1)}, bf16[768,768]{1,0:T(8,128)(2,1)S(1)}, u32[]{:S(2)}, u32[]{:S(2)}) collective-permute-start(bf16[768,768]{1,0:T(8,128)(2,1)S(1)} %add_convert_fusion.1), channel_id=1, source_target_pairs={{0,2},{1,3},{2,0},{3,1},{4,6},{5,7},{6,4},{7,5},{8,10},{9,11},{10,... | collective-permute-start | bytes 3538952 | tf_op jit(solution)/shard_map/ppermute | solution.py:14
  408.7 19.9 %copy-start.24 = (bf16[768,576]{0,1:T(8,128)(2,1)S(1)}, bf16[768,576]{0,1:T(8,128)(2,1)}, u32[]{:S(2)}) copy-start(bf16[768,576]{0,1:T(8,128)(2,1)} %convolution_convert_fusion.11) | copy-start | bytes 2654212
  481.6 1.3 collective-permute-start.21
  482.3 2.3 collective-permute-start.20
  482.9 3.9 collective-permute-start.22
  (175 other events, 400.8 us)
Sparse Core Ops, SparseCore 0:
  383.8 31.4 all-gather.1
Sparse Core Ops, SparseCore 1:
  480.5 135.7 all-reduce.6

commit v2 on v1

v2 whole, which is shorter than its diff:
```python
import functools
import jax
import jax.numpy as jnp
from jax import lax
from jax.experimental import pallas as pl
from jax.experimental.pallas import tpu as pltpu
from jax.sharding import PartitionSpec as P

HEAD = 64
LEN = 128
SHARDS = 4
SMALL = 16
epsilon = 1e-05
bf16 = jnp.bfloat16
f32 = jnp.float32
ANY = pl.BlockSpec(memory_space=pl.ANY)
VM = pl.BlockSpec(memory_space=pltpu.VMEM)


def nn(left, right):
    return lax.dot_general(left, right, (((1,), (0,)), ((), ())), preferred_element_type=f32)


def nt(left, right):
    return lax.dot_general(left, right, (((1,), (1,)), ((), ())), preferred_element_type=f32)


def tn(left, right):
    return lax.dot_general(left, right, (((0,), (0,)), ((), ())), preferred_element_type=f32)


def standardize(summed):
    center = summed - jnp.mean(summed, -1, keepdims=True)
    inverse = lax.rsqrt(jnp.mean(center * center, -1, keepdims=True) + epsilon)
    return center * inverse, inverse


def norm_back(normed, inverse, gain, grad_output):
    scaled = grad_output * gain
    return inverse * (
        scaled
        - jnp.mean(scaled, -1, keepdims=True)
        - normed * jnp.mean(scaled * normed, -1, keepdims=True)
    )


def begin(sources, held, sems):
    copies = [
        pltpu.make_async_copy(src, held.at[i], sems.at[i]) for i, src in enumerate(sources)
    ]
    for copy in copies:
        copy.start()
    return copies


def attention_forward(keep, count, *refs):
    (rows, seg_row, seg_col, bias_mixed, bias_out, *rest) = refs
    qkv, rest = rest[:SHARDS], rest[SHARDS:]
    outer, rest = rest[:SHARDS], rest[SHARDS:]
    if keep:
        first, mixed_out, probs_out, att_out, held_qkv, held_out, sem_qkv, sem_out = rest
    else:
        first, held_qkv, held_out, sem_qkv, sem_out = rest
    load_qkv = begin(qkv, held_qkv, sem_qkv)
    load_out = begin(outer, held_out, sem_out)
    x = rows[...]
    first[...] = x.astype(f32) + bias_out[...]
    same = [seg_col[i] == seg_row[i] for i in range(count)]
    for s in range(SHARDS):
        load_qkv[s].wait()
        mixed = (nt(held_qkv[s], x) + bias_mixed[:, s : s + 1]).astype(bf16)
        if keep:
            mixed_out[s] = mixed
        width = mixed.shape[0] // 3
        heads = []
        for h in range(width // HEAD):
            lines = []
            for i in range(count):
                cols = slice(i * LEN, (i + 1) * LEN)
                at = h * HEAD
                query = mixed[at : at + HEAD, cols]
                keys = mixed[width + at : width + at + HEAD, cols]
                value = mixed[2 * width + at : 2 * width + at + HEAD, cols]
                scores = jnp.where(same[i], tn(keys, query) * HEAD**-0.5, -1e9)
                top = jnp.max(scores, 0, keepdims=True)
                probs = jnp.exp(scores - top)
                probs = probs / jnp.sum(probs, 0, keepdims=True)
                if keep:
                    probs_out[s, h, i] = probs
                lines.append(nn(value, probs.astype(bf16)).astype(bf16))
            heads.append(jnp.concatenate(lines, 1))
        attended = jnp.concatenate(heads, 0)
        if keep:
            att_out[s] = attended
        load_out[s].wait()
        first[...] += tn(attended, held_out[s])


def mlp_forward(keep, *refs):
    (first, gain_one, shift_one, gain_two, shift_two, bias_up, bias_down, *rest) = refs
    up, rest = rest[:SHARDS], rest[SHARDS:]
    down, rest = rest[:SHARDS], rest[SHARDS:]
    if keep:
        out, hidden_out, active_out, slope_out, second, held_up, held_down, sem_up, sem_down = rest
    else:
        out, second, held_up, held_down, sem_up, sem_down = rest
    load_up = begin(up, held_up, sem_up)
    load_down = begin(down, held_down, sem_down)
    normed, _ = standardize(first[...])
    hidden = normed * gain_one[...] + shift_one[...]
    hidden_low = hidden.astype(bf16)
    second[...] = hidden + bias_down[...]
    if keep:
        hidden_out[...] = hidden_low
    for s in range(SHARDS):
        load_up[s].wait()
        upward = nn(hidden_low, held_up[s]) + bias_up[s]
        normal = 0.5 * (1.0 + lax.erf(upward * 0.7071067811865476))
        active = (upward * normal).astype(bf16)
        if keep:
            density = jnp.exp(-0.5 * upward * upward) * 0.3989422804014327
            active_out[s] = active
            slope_out[s] = (normal + upward * density).astype(bf16)
        load_down[s].wait()
        second[...] += nn(active, held_down[s])
    normed, _ = standardize(second[...])
    out[...] = (normed * gain_two[...] + shift_two[...]).astype(bf16)


def store(parts, s, value):
    half = value.shape[0] // 2
    for i in range(2):
        parts[2 * i + s % 2][s // 2] = value[i * half : (i + 1) * half]


def down_grads(*refs):
    grad_output, second, gain_two, active, *parts, branch_two, grad_second, sums = refs
    g = grad_output[...].astype(f32)
    normed, inverse = standardize(second[...])
    back = norm_back(normed, inverse, gain_two[...], g)
    grad_second[...] = back
    low = back.astype(bf16)
    branch_two[...] = low
    sums[0:1] = jnp.sum(back, 0, keepdims=True)
    sums[1:2] = jnp.sum(g * normed, 0, keepdims=True)
    sums[2:3] = jnp.sum(g, 0, keepdims=True)
    for s in range(SHARDS):
        store(parts, s, tn(active[s], low).astype(bf16))


def mlp_backward(full, *refs):
    if full:
        branch_two, grad_second, slope, hidden_low, first, gain_one, *rest = refs
    else:
        grad_output, second, gain_two, slope, first, gain_one, *rest = refs
    up, rest = rest[:SHARDS], rest[SHARDS:]
    down, rest = rest[:SHARDS], rest[SHARDS:]
    if full:
        *parts, grad_bias_up, grad_first, branch_one, sums = rest[:8]
        rest = rest[8:]
    else:
        grad_first, branch_one, *rest = rest
    total, held_up, held_down, sem_up, sem_down = rest
    load_down = begin(down, held_down, sem_down)
    load_up = begin(up, held_up, sem_up)
    if full:
        low = branch_two[...]
        total[...] = grad_second[...]
        x = hidden_low[...]
    else:
        normed, inverse = standardize(second[...])
        back = norm_back(normed, inverse, gain_two[...], grad_output[...].astype(f32))
        low = back.astype(bf16)
        total[...] = back
    for s in range(SHARDS):
        load_down[s].wait()
        grad_upward = (nt(low, held_down[s]) * slope[s].astype(f32)).astype(bf16)
        if full:
            store(parts, s, tn(x, grad_upward).astype(bf16))
            grad_bias_up[s] = jnp.sum(grad_upward.astype(f32), 0, keepdims=True)
        load_up[s].wait()
        total[...] += nt(grad_upward, held_up[s])
    grad_hidden = total[...]
    normed, inverse = standardize(first[...])
    back = norm_back(normed, inverse, gain_one[...], grad_hidden)
    grad_first[...] = back
    branch_one[...] = back.astype(bf16)
    if full:
        sums[0:1] = jnp.sum(back, 0, keepdims=True)
        sums[1:2] = jnp.sum(grad_hidden * normed, 0, keepdims=True)
        sums[2:3] = jnp.sum(grad_hidden, 0, keepdims=True)


def attention_backward(full, count, *refs):
    branch_one, grad_first, mixed_in, probs_in, *rest = refs
    if full:
        rows, attended, sums_two, sums_one, grad_bias_up, *rest = rest
    qkv, rest = rest[:SHARDS], rest[SHARDS:]
    outer, rest = rest[:SHARDS], rest[SHARDS:]
    if full:
        grad_in, *parts = rest[:5]
        rest = rest[5:]
        ones = jnp.ones((16, rows.shape[0]), bf16)
    else:
        grad_in, *rest = rest
    total, held_qkv, held_out, sem_qkv, sem_out = rest
    load_out = begin(outer, held_out, sem_out)
    load_qkv = begin(qkv, held_qkv, sem_qkv)
    branch = branch_one[...]
    total[...] = grad_first[...]
    scale = HEAD**-0.5
    for s in range(SHARDS):
        load_out[s].wait()
        if full:
            parts[s % 2][s // 2, : attended.shape[1]] = nn(attended[s], branch).astype(bf16)
        grad_att = nt(held_out[s], branch).astype(bf16)
        width = grad_att.shape[0]
        pieces = ([], [], [])
        for h in range(width // HEAD):
            lines = ([], [], [])
            for i in range(count):
                cols = slice(i * LEN, (i + 1) * LEN)
                at = h * HEAD
                query = mixed_in[s, at : at + HEAD, cols]
                keys = mixed_in[s, width + at : width + at + HEAD, cols]
                value = mixed_in[s, 2 * width + at : 2 * width + at + HEAD, cols]
                probs = probs_in[s, h, i]
                grad_head = grad_att[at : at + HEAD, cols]
                grad_probs = tn(value, grad_head)
                lines[2].append(nt(grad_head, probs.astype(bf16)).astype(bf16))
                inner = jnp.sum(probs * grad_probs, 0, keepdims=True)
                grad_scores = (probs * (grad_probs - inner)).astype(bf16)
                lines[0].append((nn(keys, grad_scores) * scale).astype(bf16))
                lines[1].append((nt(query, grad_scores) * scale).astype(bf16))
            for piece, line in zip(pieces, lines):
                piece.append(jnp.concatenate(line, 1))
        grad_mixed = jnp.concatenate([p for piece in pieces for p in piece], 0)
        load_qkv[s].wait()
        if full:
            grad_qkv = nn(grad_mixed, rows[...]).astype(bf16)
            parts[s % 2][s // 2, width:] = grad_qkv[:width]
            last = parts[2 + s % 2]
            last[s // 2, : 2 * width] = grad_qkv[width:]
            columns = nt(ones, grad_mixed)
            blank = jnp.zeros((1, last.shape[2] - width), f32)
            small = [
                grad_bias_up[s],
                jnp.concatenate([columns[:1, :width], blank], 1),
                jnp.concatenate([columns[:1, 2 * width :], blank], 1),
                sums_two[...],
                sums_one[...],
                jnp.zeros((SMALL - 9, last.shape[2]), f32),
            ]
            last[s // 2, 2 * width :] = jnp.concatenate(small, 0).astype(bf16)
        total[...] += tn(grad_mixed, held_qkv[s])
    grad_in[...] = total[...].astype(bf16)


def shape(dims, dtype):
    return jax.ShapeDtypeStruct(dims, dtype)


def launch(kernel, name, operands, weights, outputs, scratch):
    many = len(weights)
    return pl.pallas_call(
        kernel,
        name=name,
        out_shape=outputs,
        in_specs=[VM] * len(operands) + [ANY] * many,
        out_specs=[VM] * len(outputs),
        scratch_shapes=list(scratch)
        + [pltpu.VMEM((SHARDS,) + weights[i].shape, bf16) for i in range(0, many, SHARDS)]
        + [pltpu.SemaphoreType.DMA((SHARDS,)) for _ in range(0, many, SHARDS)],
        compiler_params=pltpu.CompilerParams(vmem_limit_bytes=56 << 20),
    )(*operands, *weights)


def run_attention_forward(keep, rows, seg, w):
    size, width = rows.shape
    third, count = w["out"][0].shape[0], size // LEN
    outputs = [shape((size, width), f32)]
    if keep:
        outputs += [
            shape((SHARDS, 3 * third, size), bf16),
            shape((SHARDS, third // HEAD, count, LEN, LEN), f32),
            shape((SHARDS, third, size), bf16),
        ]
    return launch(
        functools.partial(attention_forward, keep, count),
        "attention_forward",
        [rows, *seg, w["bias_mixed"], w["bias_out"]],
        w["qkv"] + w["out"],
        outputs,
        [],
    )


def run_mlp_forward(keep, first, w):
    size, width = first.shape
    units = w["up"][0].shape[1]
    outputs = [shape((size, width), bf16)]
    if keep:
        outputs += [
            shape((size, width), bf16),
            shape((SHARDS, size, units), bf16),
            shape((SHARDS, size, units), bf16),
            shape((size, width), f32),
        ]
    return launch(
        functools.partial(mlp_forward, keep),
        "mlp_forward",
        [first, w["gain_one"], w["shift_one"], w["gain_two"], w["shift_two"], w["bias_up"], w["bias_down"]],
        w["up"] + w["down"],
        outputs,
        [] if keep else [pltpu.VMEM((size, width), f32)],
    )


def run_down_grads(grad_output, second, active, w):
    size, width = second.shape
    units = active.shape[2]
    return launch(
        down_grads,
        "down_grads",
        [grad_output, second, w["gain_two"], active],
        [],
        [
            *[shape((SHARDS // 2, units // 2, width), bf16)] * 4,
            shape((size, width), bf16),
            shape((size, width), f32),
            shape((3, width), f32),
        ],
        [],
    )


def run_mlp_backward(full, operands, w):
    units = w["up"][0].shape[1]
    size, width = operands[0].shape
    outputs = [shape((size, width), f32), shape((size, width), bf16)]
    if full:
        outputs = [
            *[shape((SHARDS // 2, width // 2, units), bf16)] * 4,
            shape((SHARDS, 1, units), f32),
            *outputs,
            shape((3, width), f32),
        ]
    return launch(
        functools.partial(mlp_backward, full),
        "mlp_backward",
        operands,
        w["up"] + w["down"],
        outputs,
        [pltpu.VMEM((size, width), f32)],
    )


def run_attention_backward(full, operands, w):
    size, width = operands[0].shape
    third = w["out"][0].shape[0]
    outputs = [shape((size, width), bf16)]
    if full:
        outputs += [
            *[shape((SHARDS // 2, 2 * third, width), bf16)] * 2,
            *[shape((SHARDS // 2, 2 * third + SMALL, width), bf16)] * 2,
        ]
    return launch(
        functools.partial(attention_backward, full, size // LEN),
        "attention_backward",
        operands,
        w["qkv"] + w["out"],
        outputs,
        [pltpu.VMEM((size, width), f32)],
    )


def to_partner(x, bits):
    size = lax.axis_size("tensor")
    return lax.ppermute(x, "tensor", [(i, i ^ bits) for i in range(size)])


def gather(x):
    near = to_partner(x, 1)
    far = to_partner(x, 2)
    return [x, near, far, to_partner(far, 1)]


def add(*items):
    return sum(item.astype(f32) for item in items).astype(bf16)


def over_dp(part):
    size = lax.axis_size("dp")
    if size != 4:
        return lax.psum(part, "dp")
    pair = add(part, lax.ppermute(part, "dp", [(0, 1), (3, 2)]))
    total = add(pair, lax.ppermute(pair, "dp", [(1, 2), (2, 1)]))
    back = lax.ppermute(total, "dp", [(1, 0), (2, 3)])
    place = lax.axis_index("dp")
    return jnp.where((place == 1) | (place == 2), total, back)


def over_devices(keep, send):
    near = to_partner(send, 1)
    far = to_partner(add(keep[1], near[1]), 2)
    return over_dp(add(keep[0], near[0], far))


def all_rows(own):
    place = lax.axis_index("tensor")
    low, high = place % 2 == 1, place // 2 == 1
    own, near, far, both = gather(own)
    first = [jnp.where(low, near, own), jnp.where(low, own, near)]
    second = [jnp.where(low, both, far), jnp.where(low, far, both)]
    return [jnp.where(high, b, a) for a, b in zip(first, second)] + [
        jnp.where(high, a, b) for a, b in zip(first, second)
    ]


def body(
    ends_in,
    segment_ids,
    w_qkv,
    bias_qv,
    w_out,
    bias_out,
    gain_one,
    shift_one,
    w_up,
    bias_up,
    w_down,
    bias_down,
    gain_two,
    shift_two,
):
    section = lax.axis_index("section")
    place = lax.axis_index("tensor")
    _, micro, count, length, width = ends_in.shape
    share = count // lax.axis_size("tensor")
    own = lax.dynamic_slice_in_dim(ends_in[0], place * share, share, 1)
    own = own.reshape(micro * share * length, width)
    segments = lax.dynamic_slice_in_dim(segment_ids, place * share, share, 1)
    segments = segments.reshape(micro * share, length)
    seg = (segments[:, None, :], segments[:, :, None])
    third = w_qkv.shape[3]
    biases = gather(jnp.concatenate([bias_qv[0, 0], bias_qv[0, 1], bias_up[0]])[None])
    biases = jnp.concatenate(biases, 0).astype(f32)
    none = jnp.zeros((SHARDS, third), f32)
    w = {
        "qkv": gather(w_qkv[0].reshape(width, 3 * third).T),
        "out": gather(w_out[0]),
        "up": gather(w_up[0]),
        "down": gather(w_down[0]),
        "bias_mixed": jnp.concatenate([biases[:, :third], none, biases[:, third : 2 * third]], 1).T,
        "bias_up": biases[:, None, 2 * third :],
        "bias_out": bias_out.astype(f32),
        "gain_one": gain_one.astype(f32),
        "shift_one": shift_one.astype(f32),
        "bias_down": bias_down.astype(f32),
        "gain_two": gain_two.astype(f32),
        "shift_two": shift_two.astype(f32),
    }
    (first,) = run_attention_forward(False, own, seg, w)
    (out,) = run_mlp_forward(False, first, w)
    received = lax.ppermute(out, "section", [(0, 1)])
    rows = jnp.where(section == 0, own, received)
    first, mixed, probs, attended = run_attention_forward(True, rows, seg, w)
    out, hidden, active, slope, second = run_mlp_forward(True, first, w)
    grad_first, branch_one = run_mlp_backward(
        False, [own, second, w["gain_two"], slope, first, w["gain_one"]], w
    )
    (grad_in,) = run_attention_backward(False, [branch_one, grad_first, mixed, probs], w)
    returned = lax.ppermute(grad_in, "section", [(1, 0)])
    cotangent = jnp.where(section == 1, own, returned)

    *parts, branch_two, grad_second, sums_two = run_down_grads(cotangent, second, active, w)
    down = [over_devices(*parts[:2]), over_devices(*parts[2:])]
    *parts, grad_bias_up, grad_first, branch_one, sums_one = run_mlp_backward(
        True, [branch_two, grad_second, slope, hidden, first, w["gain_one"]], w
    )
    up = [over_devices(*parts[:2]), over_devices(*parts[2:])]
    grad_in, *parts = run_attention_backward(
        True,
        [branch_one, grad_first, mixed, probs, rows, attended, sums_two, sums_one, grad_bias_up],
        w,
    )
    mixer = [over_devices(*parts[:2]), over_devices(*parts[2:])]
    ends = all_rows(jnp.where(section == 1, out, grad_in).reshape(micro, share, length, width))
    qkv = jnp.concatenate([mixer[0][third:], mixer[1][: 2 * third]], 0)
    small = mixer[1][2 * third :]
    results = (
        jnp.concatenate(ends, 1),
        qkv.T.reshape(width, 3, third),
        small[1:3, :third],
        mixer[0][:third],
        small[6],
        small[7],
        small[8],
        jnp.concatenate(up, 0),
        small[0],
        jnp.concatenate(down, 0),
        small[3],
        small[4],
        small[5],
    )
    return tuple(item.astype(f32)[None] for item in results)


def solution(mesh):
    return jax.shard_map(
        body,
        mesh=mesh,
        in_specs=(
            P("section", None, "dp", None, None),
            P(None, "dp", None),
            P("section", None, None, "tensor"),
            P("section", None, "tensor"),
            P("section", "tensor", None),
            P("section", None),
            P("section", None),
            P("section", None),
            P("section", None, "tensor"),
            P("section", "tensor"),
            P("section", "tensor", None),
            P("section", None),
            P("section", None),
            P("section", None),
        ),
        out_specs=(
            P("section", None, "dp", None, None),
            P("section", None, None, "tensor"),
            P("section", None, "tensor"),
            P("section", "tensor", None),
            P("section", None),
            P("section", None),
            P("section", None),
            P("section", None, "tensor"),
            P("section", "tensor"),
            P("section", "tensor", None),
            P("section", None),
            P("section", None),
            P("section", None),
        ),
        check_vma=False,
    )
```

time: 639 us -> 487 us (0.76)
  matrix products: 217 us -> 0 us
  Pallas kernels: 0 us -> 117 us
  local copies, waits for them, and re-layouts: 58 us -> 9.63 us
  starting transfers between devices: 24.6 us -> 56.6 us
  blocking collectives: 20.3 us -> 0 us
  between operations: 18.4 us -> 1.78 us
  waiting for transfers between devices: 251 us -> 259 us
  other arithmetic: 40.8 us -> 34.2 us
    dot_general x116 -> x0, matrix products: 207 us -> none  [the longest x28 80.7 us: dot(): return jnp.dot(left, right, preferred_element_type=f32)]
    pallas_call x0 -> x9, Pallas kernels: none -> 117 us  [launch(): pl.pallas_call(kernel, name=name, out_shape=outputs, in_specs=[VM] * len(...]
    psum x1 -> x0, waiting for transfers between devices: 104 us -> none  [sum_over_dp(): return lax.psum(part, 'dp')]
    ppermute x2 -> x20, waiting for transfers between devices: 27.5 us -> 119 us  [the longest x6 70.4 us: over_dp(): back = lax.ppermute(total, 'dp', [(1, 0), (2, 3)])]
    ppermute x2 -> x20, starting transfers between devices: 4.99 us -> 36.3 us  [the longest x6 18.8 us: over_dp(): pair = add(part, lax.ppermute(part, 'dp', [(0, 1), (3, 2)]))]
    reshape x16 -> x0, local copies, waits for them, and re-layouts: 23 us -> none  [the longest x8 13.1 us: attend_back(): grad_heads = grad_result.reshape(query.shape)]
    psum x1 -> x0, blocking collectives: 20.3 us -> none  [sum_over_dp(): return lax.psum(part, 'dp')]
    ppermute x30, waiting for transfers between devices: 120 us -> 140 us  [to_partner(): return lax.ppermute(x, 'tensor', [(i, i ^ bits) for i in range(size)])]
  transfers between devices with their start and end apart: 34 -> 50, of which waited for: 12 -> 23; matrix products, arithmetic and copies ran while one was open for 13% -> 8% of each run, Pallas kernels for 0% -> 3%
where the time goes in v2:
time: 487 us; the launch traced here: 478 us
  waiting for transfers between devices  259 us (53%)
  Pallas kernels  117 us (24%)
  starting transfers between devices  56.6 us (12%)
  other arithmetic  34.2 us (7%)
  local copies, waits for them, and re-layouts  9.63 us (2%)
    ppermute x30, waiting for transfers between devices, to_partner(): return lax.ppermute(x, 'tensor', [(i, i ^ bits) for i in range(size)])  140 us
    pallas_call x9, Pallas kernels, launch(): pl.pallas_call(kernel, name=name, out_shape=outputs, in_specs=[VM] * len(...  117 us
    ppermute x6, waiting for transfers between devices, over_dp(): back = lax.ppermute(total, 'dp', [(1, 0), (2, 3)])  70.4 us
    ppermute x30, starting transfers between devices, to_partner(): return lax.ppermute(x, 'tensor', [(i, i ^ bits) for i in range(size)])  20.2 us
    ppermute x6, waiting for transfers between devices, over_dp(): pair = add(part, lax.ppermute(part, 'dp', [(0, 1), (3, 2)]))  19.8 us
    ppermute x6, starting transfers between devices, over_dp(): pair = add(part, lax.ppermute(part, 'dp', [(0, 1), (3, 2)]))  18.8 us
    ppermute x1, waiting for transfers between devices, body(): returned = lax.ppermute(grad_in, 'section', [(1, 0)])  15.4 us
    ppermute x1, waiting for transfers between devices, body(): received = lax.ppermute(out, 'section', [(0, 1)])  13.1 us
  transfers between devices with their start and end apart: 50, of which 23 were waited for; matrix products, arithmetic and copies ran while one was open for 8% of the time, Pallas kernels for 3%

profile of v2, /device:TPU:0, one launch (start us, length us, event | category | flops | bytes accessed | tf_op | source)
XLA Modules:
  0.0 477.9 jit_solution(16350401788527361047)
XLA Ops:
  0.7 3.0 collective-permute-start.10
  3.7 1.9 collective-permute-start.7
  7.3 2.0 collective-permute-start.1
  9.3 71.2 %collective-permute-done.1 = bf16[1,1152]{1,0:T(2,128)(2,1)S(1)} collective-permute-done((bf16[1,1152]{1,0:T(2,128)(2,1)S(1)}, bf16[1,1152]{1,0:T(2,128)(2,1)S(1)}, u32[]{:S(2)}, u32[]{:S(2)}) %collective-permute-start.1) | collective-permute-done | bytes 2336 | tf_op jit(solution)/shard_map/ppermute | solution.py:379
  85.0 1.6 collective-permute-done.8.refs_12_.refs_11_.refs_16_
  89.2 1.5 copy.32.refs_2_
  103.5 12.7 %attention_forward.2.refs_0_ = f32[384,768]{1,0:T(8,128)} custom-call(bf16[384,768]{1,0:T(8,128)(2,1)} %bitcast.97, s32[3,1,128]{2,1,0:T(1,128)} %constant_dynamic-slice_fusion.refs_1_, s32[3,128,1]{2,1,0:T(8,128)} %copy.32.refs_2_, f32[576,4]{1,0:T(8,128)} %copy.33.refs_3_, f32[1,768]{1,0:T(1,128)} %convert_element_type.374.refs_4_, ...), custom_call_target="tpu_custom_call" | custom-call | tf_op jit(solution)/shard_map/attention_forward/pallas_call | solution.py:265
  116.2 10.0 %mlp_forward.2 = bf16[384,768]{1,0:T(8,128)(2,1)} custom-call(f32[384,768]{1,0:T(8,128)} %attention_forward.2.refs_0_, f32[1,768]{1,0:T(1,128)} %convert_element_type.375.refs_1_.refs_5_, f32[1,768]{1,0:T(1,128)} %convert_element_type.376.refs_2_, f32[1,768]{1,0:T(1,128)} %convert_element_type.377.refs_3_.refs_2_, f32[1,768]{1,0:T(1,128)} %convert_element_type.378.refs_4_, ...), custom_call_target="tpu_custom_call" | custom-call | tf_op jit(solution)/shard_map/mlp_forward/pallas_call | solution.py:265
  126.2 3.9 collective-permute-start.15
  130.2 13.1 %collective-permute-done.15 = bf16[384,768]{1,0:T(8,128)(2,1)S(1)} collective-permute-done((bf16[384,768]{1,0:T(8,128)(2,1)}, bf16[384,768]{1,0:T(8,128)(2,1)S(1)}, u32[]{:S(2)}, u32[]{:S(2)}) %collective-permute-start.15) | collective-permute-done | bytes 589856 | tf_op jit(solution)/shard_map/ppermute | solution.py:465
  144.2 13.9 %attention_forward.3 = (f32[384,768]{1,0:T(8,128)}, bf16[4,576,384]{2,1,0:T(8,128)(2,1)}, f32[4,3,3,128,128]{4,3,2,1,0:T(8,128)}, bf16[4,192,384]{2,1,0:T(8,128)(2,1)}) custom-call(bf16[384,768]{1,0:T(8,128)(2,1)} %broadcast_select_fusion.2.refs_0_.refs_4_, s32[3,1,128]{2,1,0:T(1,128)} %constant_dynamic-slice_fusion.refs_1_, s32[3,128,1]{2,1,0:T(8,128)} %copy.32.refs_2_, ...), custom_call_target="tpu_custom_call" | custom-call | tf_op jit(solution)/shard_map/attention_forward/pallas_call | solution.py:265
  158.2 11.8 %mlp_forward.3 = (bf16[384,768]{1,0:T(8,128)(2,1)}, bf16[384,768]{1,0:T(8,128)(2,1)}, bf16[4,384,768]{2,1,0:T(8,128)(2,1)}, bf16[4,384,768]{2,1,0:T(8,128)(2,1)}, f32[384,768]{1,0:T(8,128)}) custom-call(f32[384,768]{1,0:T(8,128)} %get-tuple-element.44.refs_0_.refs_4_, f32[1,768]{1,0:T(1,128)} %convert_element_type.375.refs_1_.refs_5_, ...), custom_call_target="tpu_custom_call" | custom-call | tf_op jit(solution)/shard_map/mlp_forward/pallas_call | solution.py:265
  170.0 12.1 %mlp_backward.2 = (f32[384,768]{1,0:T(8,128)}, bf16[384,768]{1,0:T(8,128)(2,1)}) custom-call(bf16[384,768]{1,0:T(8,128)(2,1)} %bitcast.98, f32[384,768]{1,0:T(8,128)} %get-tuple-element.46.refs_1_, f32[1,768]{1,0:T(1,128)} %convert_element_type.377.refs_3_.refs_2_, bf16[4,384,768]{2,1,0:T(8,128)(2,1)} %get-tuple-element.47.refs_3_.refs_2_, ...), custom_call_target="tpu_custom_call" | custom-call | tf_op jit(solution)/shard_map/mlp_backward/pallas_call | solution.py:265
  182.2 14.7 %attention_backward.2 = bf16[384,768]{1,0:T(8,128)(2,1)} custom-call(bf16[384,768]{1,0:T(8,128)(2,1)} %get-tuple-element.48.refs_0_, f32[384,768]{1,0:T(8,128)} %get-tuple-element.49.refs_1_, bf16[4,576,384]{2,1,0:T(8,128)(2,1)} %get-tuple-element.50.refs_2_, f32[4,3,3,128,128]{4,3,2,1,0:T(8,128)} %get-tuple-element.51.refs_3_, bf16[576,768]{1,0:T(8,128)(2,1)} %bitcast.103, ...), custom_call_target="tpu_custom_call" | custom-call | tf_op jit(solution)/shard_map/attention_backward/pallas_call | solution.py:265
  196.9 1.5 collective-permute-start.16
  198.3 15.4 %collective-permute-done.16 = bf16[384,768]{1,0:T(8,128)(2,1)S(1)} collective-permute-done((bf16[384,768]{1,0:T(8,128)(2,1)}, bf16[384,768]{1,0:T(8,128)(2,1)S(1)}, u32[]{:S(2)}, u32[]{:S(2)}) %collective-permute-start.16) | collective-permute-done | bytes 589856 | tf_op jit(solution)/shard_map/ppermute | solution.py:473
  214.7 7.6 %down_grads.1 = (bf16[2,384,768]{2,1,0:T(8,128)(2,1)}, bf16[2,384,768]{2,1,0:T(8,128)(2,1)}, bf16[2,384,768]{2,1,0:T(8,128)(2,1)}, bf16[2,384,768]{2,1,0:T(8,128...) custom-call(bf16[384,768]{1,0:T(8,128)(2,1)} %broadcast_select_fusion.4.refs_0_, ...), custom_call_target="tpu_custom_call" | custom-call | tf_op jit(solution)/shard_map/down_grads/pallas_call | solution.py:265
  222.3 15.2 %mlp_backward.3 = (bf16[2,384,768]{2,1,0:T(8,128)(2,1)}, bf16[2,384,768]{2,1,0:T(8,128)(2,1)}, bf16[2,384,768]{2,1,0:T(8,128)(2,1)}, bf16[2,384,768]{2,1,0:T(8,1...) custom-call(bf16[384,768]{1,0:T(8,128)(2,1)} %get-tuple-element.53.refs_0_, ...), custom_call_target="tpu_custom_call" | custom-call | tf_op jit(solution)/shard_map/mlp_backward/pallas_call | solution.py:265
  237.5 18.5 %attention_backward.3 = (bf16[384,768]{1,0:T(8,128)(2,1)}, bf16[2,384,768]{2,1,0:T(8,128)(2,1)}, bf16[2,384,768]{2,1,0:T(8,128)(2,1)}, bf16[2,400,768]{2,1,0:T(8,128)(2,1)}, bf16[2,400,768]{2,1,0:T(8,128)(2,1)}) custom-call(bf16[384,768]{1,0:T(8,128)(2,1)} %get-tuple-element.56.refs_0_, f32[384,768]{1,0:T(8,128)} %get-tuple-element.57.refs_1_, ...), custom_call_target="tpu_custom_call" | custom-call | tf_op jit(solution)/shard_map/attention_backward/pallas_call | solution.py:265
  257.2 1.6 collective-permute-start.17
  259.3 11.9 %collective-permute-done.17 = bf16[3,1,128,768]{3,2,0,1:T(8,128)(2,1)S(1)} collective-permute-done((bf16[3,1,128,768]{3,2,0,1:T(8,128)(2,1)S(1)}, bf16[3,1,128,768]{3,2,0,1:T(8,128)(2,1)S(1)}, u32[]{:S(2)}, u32[]{:S(2)}) %collective-permute-start.17) | collective-permute-done | bytes 589856 | tf_op jit(solution)/shard_map/ppermute | solution.py:379
  272.2 1.8 collective-permute-done.18
  276.4 2.6 maximum_convert_fusion
  280.6 1.6 collective-permute-start.41
  285.3 1.6 collective-permute-start.31
  287.7 1.6 collective-permute-start.21
  289.4 7.4 %collective-permute-done.41 = bf16[384,768]{1,0:T(8,128)(2,1)S(1)} collective-permute-done((bf16[384,768]{1,0:T(8,128)(2,1)S(1)}, bf16[384,768]{1,0:T(8,128)(2,1)S(1)}, u32[]{:S(2)}, u32[]{:S(2)}) %collective-permute-start.41) | collective-permute-done | bytes 589856 | tf_op jit(solution)/shard_map/ppermute | solution.py:379
  296.9 1.5 collective-permute-start.26
  299.7 9.8 %collective-permute-done.46 = bf16[384,768]{1,0:T(8,128)(2,1)S(1)} collective-permute-done((bf16[384,768]{1,0:T(8,128)(2,1)S(1)}, bf16[384,768]{1,0:T(8,128)(2,1)S(1)}, u32[]{:S(2)}, u32[]{:S(2)}) %collective-permute-start.46) | collective-permute-done | bytes 589856 | tf_op jit(solution)/shard_map/ppermute | solution.py:379
  309.5 3.5 collective-permute-start.42
  314.3 7.8 %collective-permute-done.31 = bf16[384,768]{1,0:T(8,128)(2,1)S(1)} collective-permute-done((bf16[384,768]{1,0:T(8,128)(2,1)S(1)}, bf16[384,768]{1,0:T(8,128)(2,1)S(1)}, u32[]{:S(2)}, u32[]{:S(2)}) %collective-permute-start.31) | collective-permute-done | bytes 589856 | tf_op jit(solution)/shard_map/ppermute | solution.py:379
  322.1 3.5 collective-permute-start.47
  327.0 7.8 %collective-permute-done.36 = bf16[384,768]{1,0:T(8,128)(2,1)S(1)} collective-permute-done((bf16[384,768]{1,0:T(8,128)(2,1)S(1)}, bf16[384,768]{1,0:T(8,128)(2,1)S(1)}, u32[]{:S(2)}, u32[]{:S(2)}) %collective-permute-start.36) | collective-permute-done | bytes 589856 | tf_op jit(solution)/shard_map/ppermute | solution.py:379
  334.8 3.5 collective-permute-start.32
  338.5 8.9 %collective-permute-done.21 = bf16[384,768]{1,0:T(8,128)(2,1)S(1)} collective-permute-done((bf16[384,768]{1,0:T(8,128)(2,1)S(1)}, bf16[384,768]{1,0:T(8,128)(2,1)S(1)}, u32[]{:S(2)}, u32[]{:S(2)}) %collective-permute-start.21) | collective-permute-done | bytes 589856 | tf_op jit(solution)/shard_map/ppermute | solution.py:379
  347.4 3.5 collective-permute-start.37
  351.2 8.7 %collective-permute-done.26 = bf16[400,768]{1,0:T(8,128)(2,1)S(1)} collective-permute-done((bf16[400,768]{1,0:T(8,128)(2,1)S(1)}, bf16[400,768]{1,0:T(8,128)(2,1)S(1)}, u32[]{:S(2)}, u32[]{:S(2)}) %collective-permute-start.26) | collective-permute-done | bytes 614432 | tf_op jit(solution)/shard_map/ppermute | solution.py:379
  359.9 3.5 collective-permute-start.22
  368.0 9.1 %collective-permute-done.22 = bf16[384,768]{1,0:T(8,128)(2,1)S(1)} collective-permute-done((bf16[384,768]{1,0:T(8,128)(2,1)S(1)}, bf16[384,768]{1,0:T(8,128)(2,1)S(1)}, u32[]{:S(2)}, u32[]{:S(2)}) %collective-permute-start.22) | collective-permute-done | bytes 589856 | tf_op jit(solution)/shard_map/ppermute | solution.py:396
  378.0 10.7 %collective-permute-done.27 = bf16[400,768]{1,0:T(8,128)(2,1)S(1)} collective-permute-done((bf16[400,768]{1,0:T(8,128)(2,1)S(1)}, bf16[400,768]{1,0:T(8,128)(2,1)S(1)}, u32[]{:S(2)}, u32[]{:S(2)}) %collective-permute-start.27) | collective-permute-done | bytes 614432 | tf_op jit(solution)/shard_map/ppermute | solution.py:396
  397.7 15.2 %collective-permute-done.44 = bf16[384,768]{1,0:T(8,128)(2,1)S(1)} collective-permute-done((bf16[384,768]{1,0:T(8,128)(2,1)S(1)}, bf16[384,768]{1,0:T(8,128)(2,1)S(1)}, u32[]{:S(2)}, u32[]{:S(2)}) %collective-permute-start.44) | collective-permute-done | bytes 589856 | tf_op jit(solution)/shard_map/ppermute | solution.py:398
  414.2 11.3 %collective-permute-done.49 = bf16[384,768]{1,0:T(8,128)(2,1)S(1)} collective-permute-done((bf16[384,768]{1,0:T(8,128)(2,1)S(1)}, bf16[384,768]{1,0:T(8,128)(2,1)S(1)}, u32[]{:S(2)}, u32[]{:S(2)}) %collective-permute-start.49) | collective-permute-done | bytes 589856 | tf_op jit(solution)/shard_map/ppermute | solution.py:398
  425.6 12.6 %collective-permute-done.34 = bf16[384,768]{1,0:T(8,128)(2,1)S(1)} collective-permute-done((bf16[384,768]{1,0:T(8,128)(2,1)S(1)}, bf16[384,768]{1,0:T(8,128)(2,1)S(1)}, u32[]{:S(2)}, u32[]{:S(2)}) %collective-permute-start.34) | collective-permute-done | bytes 589856 | tf_op jit(solution)/shard_map/ppermute | solution.py:398
  438.2 1.6 maximum_convert_fusion.2
  439.8 10.7 %collective-permute-done.39 = bf16[384,768]{1,0:T(8,128)(2,1)S(1)} collective-permute-done((bf16[384,768]{1,0:T(8,128)(2,1)S(1)}, bf16[384,768]{1,0:T(8,128)(2,1)S(1)}, u32[]{:S(2)}, u32[]{:S(2)}) %collective-permute-start.39) | collective-permute-done | bytes 589856 | tf_op jit(solution)/shard_map/ppermute | solution.py:398
  450.6 1.6 maximum_convert_fusion.1
  452.2 11.0 %collective-permute-done.24 = bf16[384,768]{1,0:T(8,128)(2,1)S(1)} collective-permute-done((bf16[384,768]{1,0:T(8,128)(2,1)S(1)}, bf16[384,768]{1,0:T(8,128)(2,1)S(1)}, u32[]{:S(2)}, u32[]{:S(2)}) %collective-permute-start.24) | collective-permute-done | bytes 589856 | tf_op jit(solution)/shard_map/ppermute | solution.py:398
  464.1 9.7 %collective-permute-done.29 = bf16[400,768]{1,0:T(8,128)(2,1)S(1)} collective-permute-done((bf16[400,768]{1,0:T(8,128)(2,1)S(1)}, bf16[400,768]{1,0:T(8,128)(2,1)S(1)}, u32[]{:S(2)}, u32[]{:S(2)}) %collective-permute-start.29) | collective-permute-done | bytes 614432 | tf_op jit(solution)/shard_map/ppermute | solution.py:398
  (162 shorter events, 58.9 us)
Async XLA Ops:
  0.7 86.5 %collective-permute-start.10 = (bf16[768,768]{1,0:T(8,128)(2,1)}, bf16[768,768]{1,0:T(8,128)(2,1)S(1)}, u32[]{:S(2)}, u32[]{:S(2)}) collective-permute-start(bf16[768,768]{1,0:T(8,128)(2,1)} %bitcast.85), channel_id=1, source_target_pairs={{0,2},{1,3},{2,0},{3,1},{4,6},{5,7},{6,4},{7,5},{8,10},{9,11},{10,... | collective-permute-start | bytes 3538952 | tf_op jit(solution)/shard_map/ppermute | solution.py:379
  3.7 83.7 %collective-permute-start.13 = (bf16[768,768]{1,0:T(8,128)(2,1)}, bf16[768,768]{1,0:T(8,128)(2,1)}, u32[]{:S(2)}, u32[]{:S(2)}) collective-permute-start(bf16[768,768]{1,0:T(8,128)(2,1)} %bitcast.91), channel_id=1, source_target_pairs={{0,2},{1,3},{2,0},{3,1},{4,6},{5,7},{6,4},{7,5},{8,10},{9,11},{10,... | collective-permute-start | bytes 3538952 | tf_op jit(solution)/shard_map/ppermute | solution.py:379
  3.7 79.5 %collective-permute-start.7 = (bf16[192,768]{1,0:T(8,128)(2,1)}, bf16[192,768]{1,0:T(8,128)(2,1)}, u32[]{:S(2)}, u32[]{:S(2)}) collective-permute-start(bf16[192,768]{1,0:T(8,128)(2,1)} %bitcast.105), channel_id=1, source_target_pairs={{0,2},{1,3},{2,0},{3,1},{4,6},{5,7},{6,4},{7,5},{8,10},{9,11},{10,... | collective-permute-start | bytes 884744 | tf_op jit(solution)/shard_map/ppermute | solution.py:379
  5.7 81.1 %collective-permute-start.4 = (bf16[576,768]{1,0:T(8,128)(2,1)}, bf16[576,768]{1,0:T(8,128)(2,1)}, u32[]{:S(2)}, u32[]{:S(2)}) collective-permute-start(bf16[576,768]{1,0:T(8,128)(2,1)} %bitcast.99), channel_id=1, source_target_pairs={{0,2},{1,3},{2,0},{3,1},{4,6},{5,7},{6,4},{7,5},{8,10},{9,11},{10,... | collective-permute-start | bytes 2654216 | tf_op jit(solution)/shard_map/ppermute | solution.py:379
  7.3 73.2 %collective-permute-start.1 = (bf16[1,1152]{1,0:T(2,128)(2,1)S(1)}, bf16[1,1152]{1,0:T(2,128)(2,1)S(1)}, u32[]{:S(2)}, u32[]{:S(2)}) collective-permute-start(bf16[1,1152]{1,0:T(2,128)(2,1)S(1)} %broadcast_in_dim.32), channel_id=1, source_target_pairs={{0,2},{1,3},{2,0},{3,1},{4,6},{5,7},{6,4},{7,5},{8,10},{9,11},{10,... | collective-permute-start | bytes 6920 | tf_op jit(solution)/shard_map/ppermute | solution.py:379
  83.0 1.8 collective-permute-start.6
  83.2 4.5 collective-permute-start.3
  84.8 1.8 collective-permute-start.8
  86.6 29.6 %collective-permute-start.12 = (bf16[768,768]{1,0:T(8,128)(2,1)}, bf16[768,768]{1,0:T(8,128)(2,1)}, u32[]{:S(2)}, u32[]{:S(2)}) collective-permute-start(bf16[768,768]{1,0:T(8,128)(2,1)} %bitcast.92), channel_id=1, source_target_pairs={{0,1},{1,0},{2,3},{3,2},{4,5},{5,4},{6,7},{7,6},{8,9},{9,8},{10,11... | collective-permute-start | bytes 3538952 | tf_op jit(solution)/shard_map/ppermute | solution.py:379
  86.8 29.4 %collective-permute-start.9 = (bf16[768,768]{1,0:T(8,128)(2,1)}, bf16[768,768]{1,0:T(8,128)(2,1)}, u32[]{:S(2)}, u32[]{:S(2)}) collective-permute-start(bf16[768,768]{1,0:T(8,128)(2,1)} %bitcast.86), channel_id=1, source_target_pairs={{0,1},{1,0},{2,3},{3,2},{4,5},{5,4},{6,7},{7,6},{8,9},{9,8},{10,11... | collective-permute-start | bytes 3538952 | tf_op jit(solution)/shard_map/ppermute | solution.py:379
  87.1 29.1 %collective-permute-start.11 = (bf16[768,768]{1,0:T(8,128)(2,1)S(1)}, bf16[768,768]{1,0:T(8,128)(2,1)}, u32[]{:S(2)}, u32[]{:S(2)}) collective-permute-start(bf16[768,768]{1,0:T(8,128)(2,1)S(1)} %collective-permute-done.10.refs_9_.refs_8_), channel_id=1, source_target_pairs={{0,1},{1,0},{2,3},{3,2},{4,5},{5,4},{6,7},{7,6},{8,9},{9,8},{10,11... | collective-permute-start | bytes 3538952 | tf_op jit(solution)/shard_map/ppermute | solution.py:379
  87.4 28.8 %collective-permute-start.14 = (bf16[768,768]{1,0:T(8,128)(2,1)}, bf16[768,768]{1,0:T(8,128)(2,1)}, u32[]{:S(2)}, u32[]{:S(2)}) collective-permute-start(bf16[768,768]{1,0:T(8,128)(2,1)} %collective-permute-done.13.refs_13_.refs_12_), channel_id=1, source_target_pairs={{0,1},{1,0},{2,3},{3,2},{4,5},{5,4},{6,7},{7,6},{8,9},{9,8},{10,11... | collective-permute-start | bytes 3538952 | tf_op jit(solution)/shard_map/ppermute | solution.py:379
  87.7 15.8 %collective-permute-start.5 = (bf16[576,768]{1,0:T(8,128)(2,1)}, bf16[576,768]{1,0:T(8,128)(2,1)}, u32[]{:S(2)}, u32[]{:S(2)}) collective-permute-start(bf16[576,768]{1,0:T(8,128)(2,1)} %collective-permute-done.4.refs_7_.refs_6_.refs_11_), channel_id=1, source_target_pairs={{0,1},{1,0},{2,3},{3,2},{4,5},{5,4},{6,7},{7,6},{8,9},{9,8},{10,11... | collective-permute-start | bytes 2654216 | tf_op jit(solution)/shard_map/ppermute | solution.py:379
  126.2 17.1 %collective-permute-start.15 = (bf16[384,768]{1,0:T(8,128)(2,1)}, bf16[384,768]{1,0:T(8,128)(2,1)S(1)}, u32[]{:S(2)}, u32[]{:S(2)}) collective-permute-start(bf16[384,768]{1,0:T(8,128)(2,1)} %mlp_forward.2), channel_id=1, source_target_pairs={{0,16},{1,17},{2,18},{3,19},{4,20},{5,21},{6,22},{7,23},{8,24},{9,... | collective-permute-start | bytes 1769480 | tf_op jit(solution)/shard_map/ppermute | solution.py:465
  196.9 16.9 %collective-permute-start.16 = (bf16[384,768]{1,0:T(8,128)(2,1)}, bf16[384,768]{1,0:T(8,128)(2,1)S(1)}, u32[]{:S(2)}, u32[]{:S(2)}) collective-permute-start(bf16[384,768]{1,0:T(8,128)(2,1)} %attention_backward.2), channel_id=1, source_target_pairs={{16,0},{17,1},{18,2},{19,3},{20,4},{21,5},{22,6},{23,7},{24,8},{25... | collective-permute-start | bytes 1769480 | tf_op jit(solution)/shard_map/ppermute | solution.py:473
  257.2 13.9 %collective-permute-start.17 = (bf16[3,1,128,768]{3,2,0,1:T(8,128)(2,1)S(1)}, bf16[3,1,128,768]{3,2,0,1:T(8,128)(2,1)S(1)}, u32[]{:S(2)}, u32[]{:S(2)}) collective-permute-start(bf16[3,1,128,768]{3,2,0,1:T(8,128)(2,1)S(1)} %bitcast.111), channel_id=1, source_target_pairs={{0,2},{1,3},{2,0},{3,1},{4,6},{5,7},{6,4},{7,5},{8,10},{9,11},{10,... | collective-permute-start | bytes 1769480 | tf_op jit(solution)/shard_map/ppermute | solution.py:379
  258.8 20.2 %collective-permute-start.40 = (bf16[2,384,768]{2,1,0:T(8,128)(2,1)}, bf16[2,384,768]{2,1,0:T(8,128)(2,1)}, u32[]{:S(2)}, u32[]{:S(2)}) collective-permute-start(bf16[2,384,768]{2,1,0:T(8,128)(2,1)} %get-tuple-element.72), channel_id=1, source_target_pairs={{0,1},{1,0},{2,3},{3,2},{4,5},{5,4},{6,7},{7,6},{8,9},{9,8},{10,11... | collective-permute-start | bytes 3538952 | tf_op jit(solution)/shard_map/ppermute | solution.py:379
  258.8 12.9 %collective-permute-start.19 = (bf16[3,1,128,768]{3,2,0,1:T(8,128)(2,1)S(1)}, bf16[3,1,128,768]{3,2,0,1:T(8,128)(2,1)S(1)}, u32[]{:S(2)}, u32[]{:S(2)}) collective-permute-start(bf16[3,1,128,768]{3,2,0,1:T(8,128)(2,1)S(1)} %bitcast.112), channel_id=1, source_target_pairs={{0,1},{1,0},{2,3},{3,2},{4,5},{5,4},{6,7},{7,6},{8,9},{9,8},{10,11... | collective-permute-start | bytes 1769480 | tf_op jit(solution)/shard_map/ppermute | solution.py:379
  271.1 2.8 collective-permute-start.18
  271.1 9.5 %collective-permute-start.45 = (bf16[2,384,768]{2,1,0:T(8,128)(2,1)}, bf16[2,384,768]{2,1,0:T(8,128)(2,1)}, u32[]{:S(2)}, u32[]{:S(2)}) collective-permute-start(bf16[2,384,768]{2,1,0:T(8,128)(2,1)} %get-tuple-element.74), channel_id=1, source_target_pairs={{0,1},{1,0},{2,3},{3,2},{4,5},{5,4},{6,7},{7,6},{8,9},{9,8},{10,11... | collective-permute-start | bytes 3538952 | tf_op jit(solution)/shard_map/ppermute | solution.py:379
  271.7 11.8 %collective-permute-start.30 = (bf16[2,384,768]{2,1,0:T(8,128)(2,1)}, bf16[2,384,768]{2,1,0:T(8,128)(2,1)}, u32[]{:S(2)}, u32[]{:S(2)}) collective-permute-start(bf16[2,384,768]{2,1,0:T(8,128)(2,1)} %get-tuple-element.68), channel_id=1, source_target_pairs={{0,1},{1,0},{2,3},{3,2},{4,5},{5,4},{6,7},{7,6},{8,9},{9,8},{10,11... | collective-permute-start | bytes 3538952 | tf_op jit(solution)/shard_map/ppermute | solution.py:379
  271.7 13.6 %collective-permute-start.35 = (bf16[2,384,768]{2,1,0:T(8,128)(2,1)}, bf16[2,384,768]{2,1,0:T(8,128)(2,1)S(1)}, u32[]{:S(2)}, u32[]{:S(2)}) collective-permute-start(bf16[2,384,768]{2,1,0:T(8,128)(2,1)} %get-tuple-element.70), channel_id=1, source_target_pairs={{0,1},{1,0},{2,3},{3,2},{4,5},{5,4},{6,7},{7,6},{8,9},{9,8},{10,11... | collective-permute-start | bytes 3538952 | tf_op jit(solution)/shard_map/ppermute | solution.py:379
  274.8 12.2 %collective-permute-start.20 = (bf16[2,384,768]{2,1,0:T(8,128)(2,1)}, bf16[2,384,768]{2,1,0:T(8,128)(2,1)S(1)}, u32[]{:S(2)}, u32[]{:S(2)}) collective-permute-start(bf16[2,384,768]{2,1,0:T(8,128)(2,1)} %get-tuple-element.64), channel_id=1, source_target_pairs={{0,1},{1,0},{2,3},{3,2},{4,5},{5,4},{6,7},{7,6},{8,9},{9,8},{10,11... | collective-permute-start | bytes 3538952 | tf_op jit(solution)/shard_map/ppermute | solution.py:379
  279.0 8.8 %collective-permute-start.25 = (bf16[2,400,768]{2,1,0:T(8,128)(2,1)S(1)}, bf16[2,400,768]{2,1,0:T(8,128)(2,1)S(1)}, u32[]{:S(2)}, u32[]{:S(2)}) collective-permute-start(bf16[2,400,768]{2,1,0:T(8,128)(2,1)S(1)} %copy-done.18), channel_id=1, source_target_pairs={{0,1},{1,0},{2,3},{3,2},{4,5},{5,4},{6,7},{7,6},{8,9},{9,8},{10,11... | collective-permute-start | bytes 3686408 | tf_op jit(solution)/shard_map/ppermute | solution.py:379
  280.6 16.2 %collective-permute-start.41 = (bf16[384,768]{1,0:T(8,128)(2,1)S(1)}, bf16[384,768]{1,0:T(8,128)(2,1)S(1)}, u32[]{:S(2)}, u32[]{:S(2)}) collective-permute-start(bf16[384,768]{1,0:T(8,128)(2,1)S(1)} %fusion.10), channel_id=1, source_target_pairs={{0,2},{1,3},{2,0},{3,1},{4,6},{5,7},{6,4},{7,5},{8,10},{9,11},{10,... | collective-permute-start | bytes 1769480 | tf_op jit(solution)/shard_map/ppermute | solution.py:379
  283.4 26.1 %collective-permute-start.46 = (bf16[384,768]{1,0:T(8,128)(2,1)S(1)}, bf16[384,768]{1,0:T(8,128)(2,1)S(1)}, u32[]{:S(2)}, u32[]{:S(2)}) collective-permute-start(bf16[384,768]{1,0:T(8,128)(2,1)S(1)} %fusion.11), channel_id=1, source_target_pairs={{0,2},{1,3},{2,0},{3,1},{4,6},{5,7},{6,4},{7,5},{8,10},{9,11},{10,... | collective-permute-start | bytes 1769480 | tf_op jit(solution)/shard_map/ppermute | solution.py:379
  285.3 36.9 %collective-permute-start.31 = (bf16[384,768]{1,0:T(8,128)(2,1)S(1)}, bf16[384,768]{1,0:T(8,128)(2,1)S(1)}, u32[]{:S(2)}, u32[]{:S(2)}) collective-permute-start(bf16[384,768]{1,0:T(8,128)(2,1)S(1)} %fusion.8), channel_id=1, source_target_pairs={{0,2},{1,3},{2,0},{3,1},{4,6},{5,7},{6,4},{7,5},{8,10},{9,11},{10,... | collective-permute-start | bytes 1769480 | tf_op jit(solution)/shard_map/ppermute | solution.py:379
  287.0 47.8 %collective-permute-start.36 = (bf16[384,768]{1,0:T(8,128)(2,1)S(1)}, bf16[384,768]{1,0:T(8,128)(2,1)S(1)}, u32[]{:S(2)}, u32[]{:S(2)}) collective-permute-start(bf16[384,768]{1,0:T(8,128)(2,1)S(1)} %fusion.9), channel_id=1, source_target_pairs={{0,2},{1,3},{2,0},{3,1},{4,6},{5,7},{6,4},{7,5},{8,10},{9,11},{10,... | collective-permute-start | bytes 1769480 | tf_op jit(solution)/shard_map/ppermute | solution.py:379
  287.7 59.7 %collective-permute-start.21 = (bf16[384,768]{1,0:T(8,128)(2,1)S(1)}, bf16[384,768]{1,0:T(8,128)(2,1)S(1)}, u32[]{:S(2)}, u32[]{:S(2)}) collective-permute-start(bf16[384,768]{1,0:T(8,128)(2,1)S(1)} %fusion.7), channel_id=1, source_target_pairs={{0,2},{1,3},{2,0},{3,1},{4,6},{5,7},{6,4},{7,5},{8,10},{9,11},{10,... | collective-permute-start | bytes 1769480 | tf_op jit(solution)/shard_map/ppermute | solution.py:379
  296.9 63.0 %collective-permute-start.26 = (bf16[400,768]{1,0:T(8,128)(2,1)S(1)}, bf16[400,768]{1,0:T(8,128)(2,1)S(1)}, u32[]{:S(2)}, u32[]{:S(2)}) collective-permute-start(bf16[400,768]{1,0:T(8,128)(2,1)S(1)} %fusion.6), channel_id=1, source_target_pairs={{0,2},{1,3},{2,0},{3,1},{4,6},{5,7},{6,4},{7,5},{8,10},{9,11},{10,... | collective-permute-start | bytes 1843208 | tf_op jit(solution)/shard_map/ppermute | solution.py:379
  309.5 54.2 %collective-permute-start.42 = (bf16[384,768]{1,0:T(8,128)(2,1)S(1)}, bf16[384,768]{1,0:T(8,128)(2,1)S(1)}, u32[]{:S(2)}, u32[]{:S(2)}) collective-permute-start(bf16[384,768]{1,0:T(8,128)(2,1)S(1)} %fusion.2), channel_id=1, source_target_pairs={{0,4},{12,8},{1,5},{13,9},{2,6},{14,10},{3,7},{15,11},{16,20},{28,... | collective-permute-start | bytes 1769480 | tf_op jit(solution)/shard_map/ppermute | solution.py:396
  322.1 43.0 %collective-permute-start.47 = (bf16[384,768]{1,0:T(8,128)(2,1)S(1)}, bf16[384,768]{1,0:T(8,128)(2,1)S(1)}, u32[]{:S(2)}, u32[]{:S(2)}) collective-permute-start(bf16[384,768]{1,0:T(8,128)(2,1)S(1)} %fusion.1), channel_id=1, source_target_pairs={{0,4},{12,8},{1,5},{13,9},{2,6},{14,10},{3,7},{15,11},{16,20},{28,... | collective-permute-start | bytes 1769480 | tf_op jit(solution)/shard_map/ppermute | solution.py:396
  334.8 31.2 %collective-permute-start.32 = (bf16[384,768]{1,0:T(8,128)(2,1)S(1)}, bf16[384,768]{1,0:T(8,128)(2,1)S(1)}, u32[]{:S(2)}, u32[]{:S(2)}) collective-permute-start(bf16[384,768]{1,0:T(8,128)(2,1)S(1)} %fusion.4), channel_id=1, source_target_pairs={{0,4},{12,8},{1,5},{13,9},{2,6},{14,10},{3,7},{15,11},{16,20},{28,... | collective-permute-start | bytes 1769480 | tf_op jit(solution)/shard_map/ppermute | solution.py:396
  347.4 19.7 %collective-permute-start.37 = (bf16[384,768]{1,0:T(8,128)(2,1)S(1)}, bf16[384,768]{1,0:T(8,128)(2,1)S(1)}, u32[]{:S(2)}, u32[]{:S(2)}) collective-permute-start(bf16[384,768]{1,0:T(8,128)(2,1)S(1)} %fusion.3), channel_id=1, source_target_pairs={{0,4},{12,8},{1,5},{13,9},{2,6},{14,10},{3,7},{15,11},{16,20},{28,... | collective-permute-start | bytes 1769480 | tf_op jit(solution)/shard_map/ppermute | solution.py:396
  359.9 17.2 %collective-permute-start.22 = (bf16[384,768]{1,0:T(8,128)(2,1)S(1)}, bf16[384,768]{1,0:T(8,128)(2,1)S(1)}, u32[]{:S(2)}, u32[]{:S(2)}) collective-permute-start(bf16[384,768]{1,0:T(8,128)(2,1)S(1)} %fusion.5), channel_id=1, source_target_pairs={{0,4},{12,8},{1,5},{13,9},{2,6},{14,10},{3,7},{15,11},{16,20},{28,... | collective-permute-start | bytes 1769480 | tf_op jit(solution)/shard_map/ppermute | solution.py:396
  363.7 25.0 %collective-permute-start.27 = (bf16[400,768]{1,0:T(8,128)(2,1)S(1)}, bf16[400,768]{1,0:T(8,128)(2,1)S(1)}, u32[]{:S(2)}, u32[]{:S(2)}) collective-permute-start(bf16[400,768]{1,0:T(8,128)(2,1)S(1)} %fusion), channel_id=1, source_target_pairs={{0,4},{12,8},{1,5},{13,9},{2,6},{14,10},{3,7},{15,11},{16,20},{28,... | collective-permute-start | bytes 1843208 | tf_op jit(solution)/shard_map/ppermute | solution.py:396
  365.2 24.4 %collective-permute-start.43 = (bf16[384,768]{1,0:T(8,128)(2,1)S(1)}, bf16[384,768]{1,0:T(8,128)(2,1)S(1)}, u32[]{:S(2)}, u32[]{:S(2)}) collective-permute-start(bf16[384,768]{1,0:T(8,128)(2,1)S(1)} %add_convert_fusion.7), channel_id=1, source_target_pairs={{4,8},{8,4},{5,9},{9,5},{6,10},{10,6},{7,11},{11,7},{20,24},{24,20... | collective-permute-start | bytes 1769480 | tf_op jit(solution)/shard_map/ppermute | solution.py:397
  366.0 24.4 %collective-permute-start.48 = (bf16[384,768]{1,0:T(8,128)(2,1)S(1)}, bf16[384,768]{1,0:T(8,128)(2,1)S(1)}, u32[]{:S(2)}, u32[]{:S(2)}) collective-permute-start(bf16[384,768]{1,0:T(8,128)(2,1)S(1)} %add_convert_fusion.4), channel_id=1, source_target_pairs={{4,8},{8,4},{5,9},{9,5},{6,10},{10,6},{7,11},{11,7},{20,24},{24,20... | collective-permute-start | bytes 1769480 | tf_op jit(solution)/shard_map/ppermute | solution.py:397
  367.2 24.7 %collective-permute-start.33 = (bf16[384,768]{1,0:T(8,128)(2,1)S(1)}, bf16[384,768]{1,0:T(8,128)(2,1)S(1)}, u32[]{:S(2)}, u32[]{:S(2)}) collective-permute-start(bf16[384,768]{1,0:T(8,128)(2,1)S(1)} %add_convert_fusion.13), channel_id=1, source_target_pairs={{4,8},{8,4},{5,9},{9,5},{6,10},{10,6},{7,11},{11,7},{20,24},{24,20... | collective-permute-start | bytes 1769480 | tf_op jit(solution)/shard_map/ppermute | solution.py:397
  377.1 16.2 %collective-permute-start.38 = (bf16[384,768]{1,0:T(8,128)(2,1)S(1)}, bf16[384,768]{1,0:T(8,128)(2,1)S(1)}, u32[]{:S(2)}, u32[]{:S(2)}) collective-permute-start(bf16[384,768]{1,0:T(8,128)(2,1)S(1)} %add_convert_fusion.10), channel_id=1, source_target_pairs={{4,8},{8,4},{5,9},{9,5},{6,10},{10,6},{7,11},{11,7},{20,24},{24,20... | collective-permute-start | bytes 1769480 | tf_op jit(solution)/shard_map/ppermute | solution.py:397
  388.7 6.1 %collective-permute-start.23 = (bf16[384,768]{1,0:T(8,128)(2,1)S(1)}, bf16[384,768]{1,0:T(8,128)(2,1)S(1)}, u32[]{:S(2)}, u32[]{:S(2)}) collective-permute-start(bf16[384,768]{1,0:T(8,128)(2,1)S(1)} %add_convert_fusion.16), channel_id=1, source_target_pairs={{4,8},{8,4},{5,9},{9,5},{6,10},{10,6},{7,11},{11,7},{20,24},{24,20... | collective-permute-start | bytes 1769480 | tf_op jit(solution)/shard_map/ppermute | solution.py:397
  389.6 6.7 %collective-permute-start.28 = (bf16[400,768]{1,0:T(8,128)(2,1)S(1)}, bf16[400,768]{1,0:T(8,128)(2,1)S(1)}, u32[]{:S(2)}, u32[]{:S(2)}) collective-permute-start(bf16[400,768]{1,0:T(8,128)(2,1)S(1)} %add_convert_fusion.1), channel_id=1, source_target_pairs={{4,8},{8,4},{5,9},{9,5},{6,10},{10,6},{7,11},{11,7},{20,24},{24,20... | collective-permute-start | bytes 1843208 | tf_op jit(solution)/shard_map/ppermute | solution.py:397
  390.4 22.4 %collective-permute-start.44 = (bf16[384,768]{1,0:T(8,128)(2,1)S(1)}, bf16[384,768]{1,0:T(8,128)(2,1)S(1)}, u32[]{:S(2)}, u32[]{:S(2)}) collective-permute-start(bf16[384,768]{1,0:T(8,128)(2,1)S(1)} %add_convert_fusion.6), channel_id=1, source_target_pairs={{4,0},{8,12},{5,1},{9,13},{6,2},{10,14},{7,3},{11,15},{20,16},{24,... | collective-permute-start | bytes 1769480 | tf_op jit(solution)/shard_map/ppermute | solution.py:398
  391.9 33.6 %collective-permute-start.49 = (bf16[384,768]{1,0:T(8,128)(2,1)S(1)}, bf16[384,768]{1,0:T(8,128)(2,1)S(1)}, u32[]{:S(2)}, u32[]{:S(2)}) collective-permute-start(bf16[384,768]{1,0:T(8,128)(2,1)S(1)} %add_convert_fusion.3), channel_id=1, source_target_pairs={{4,0},{8,12},{5,1},{9,13},{6,2},{10,14},{7,3},{11,15},{20,16},{24,... | collective-permute-start | bytes 1769480 | tf_op jit(solution)/shard_map/ppermute | solution.py:398
  393.3 44.8 %collective-permute-start.34 = (bf16[384,768]{1,0:T(8,128)(2,1)S(1)}, bf16[384,768]{1,0:T(8,128)(2,1)S(1)}, u32[]{:S(2)}, u32[]{:S(2)}) collective-permute-start(bf16[384,768]{1,0:T(8,128)(2,1)S(1)} %add_convert_fusion.12), channel_id=1, source_target_pairs={{4,0},{8,12},{5,1},{9,13},{6,2},{10,14},{7,3},{11,15},{20,16},{24,... | collective-permute-start | bytes 1769480 | tf_op jit(solution)/shard_map/ppermute | solution.py:398
  394.8 55.7 %collective-permute-start.39 = (bf16[384,768]{1,0:T(8,128)(2,1)S(1)}, bf16[384,768]{1,0:T(8,128)(2,1)S(1)}, u32[]{:S(2)}, u32[]{:S(2)}) collective-permute-start(bf16[384,768]{1,0:T(8,128)(2,1)S(1)} %add_convert_fusion.9), channel_id=1, source_target_pairs={{4,0},{8,12},{5,1},{9,13},{6,2},{10,14},{7,3},{11,15},{20,16},{24,... | collective-permute-start | bytes 1769480 | tf_op jit(solution)/shard_map/ppermute | solution.py:398
  396.3 66.9 %collective-permute-start.24 = (bf16[384,768]{1,0:T(8,128)(2,1)S(1)}, bf16[384,768]{1,0:T(8,128)(2,1)S(1)}, u32[]{:S(2)}, u32[]{:S(2)}) collective-permute-start(bf16[384,768]{1,0:T(8,128)(2,1)S(1)} %add_convert_fusion.15), channel_id=1, source_target_pairs={{4,0},{8,12},{5,1},{9,13},{6,2},{10,14},{7,3},{11,15},{20,16},{24,... | collective-permute-start | bytes 1769480 | tf_op jit(solution)/shard_map/ppermute | solution.py:398
  412.9 60.9 %collective-permute-start.29 = (bf16[400,768]{1,0:T(8,128)(2,1)S(1)}, bf16[400,768]{1,0:T(8,128)(2,1)S(1)}, u32[]{:S(2)}, u32[]{:S(2)}) collective-permute-start(bf16[400,768]{1,0:T(8,128)(2,1)S(1)} %add_convert_fusion), channel_id=1, source_target_pairs={{4,0},{8,12},{5,1},{9,13},{6,2},{10,14},{7,3},{11,15},{20,16},{24,... | collective-permute-start | bytes 1843208 | tf_op jit(solution)/shard_map/ppermute | solution.py:398
  (21 other events, 247.0 us)

commit v3 on v2

v3 whole, which is shorter than its diff:
```python
import functools
import jax
import jax.numpy as jnp
from jax import lax
from jax.experimental import pallas as pl
from jax.experimental.pallas import tpu as pltpu
from jax.sharding import PartitionSpec as P

HEAD = 64
LEN = 128
SHARDS = 4
SMALL = 16
NEAR_PAIR, FAR_PAIR, ALL = (0, 1), (2, 3), (0, 1, 2, 3)
epsilon = 1e-05
bf16 = jnp.bfloat16
f32 = jnp.float32
ANY = pl.BlockSpec(memory_space=pl.ANY)
VM = pl.BlockSpec(memory_space=pltpu.VMEM)
SM = pl.BlockSpec(memory_space=pltpu.SMEM)


def nn(left, right):
    return lax.dot_general(left, right, (((1,), (0,)), ((), ())), preferred_element_type=f32)


def nt(left, right):
    return lax.dot_general(left, right, (((1,), (1,)), ((), ())), preferred_element_type=f32)


def tn(left, right):
    return lax.dot_general(left, right, (((0,), (0,)), ((), ())), preferred_element_type=f32)


def standardize(summed):
    center = summed - jnp.mean(summed, -1, keepdims=True)
    inverse = lax.rsqrt(jnp.mean(center * center, -1, keepdims=True) + epsilon)
    return center * inverse, inverse


def norm_back(normed, inverse, gain, grad_output):
    scaled = grad_output * gain
    return inverse * (
        scaled
        - jnp.mean(scaled, -1, keepdims=True)
        - normed * jnp.mean(scaled * normed, -1, keepdims=True)
    )


def wide(ref):
    return ref[...].astype(f32)


def load(sources, held, sems):
    copies = [
        pltpu.make_async_copy(src, held.at[n], sems.at[n]) for n, src in enumerate(sources)
    ]
    for copy in copies:
        copy.start()
    return copies


def load_mlp(kinds, refs, rotation, held_up, held_down, sems, up_first):
    refs = list(refs)
    ups, downs = [], []
    for n, kind in enumerate(kinds):
        first = refs.pop(0)
        half = first.shape[0]
        up = [pltpu.make_async_copy(first, held_up.at[n, pl.ds(0, half)], sems.at[n, 0])]
        down = []
        if kind == 1:
            down.append(pltpu.make_async_copy(refs.pop(0), held_down.at[n], sems.at[n, 1]))
        else:
            size = held_down.shape[1] // kind
            rest = (held_up.shape[1] - half) // kind
            for turn in range(kind):
                piece = refs.pop(0)
                place = lax.rem(rotation[0] + (kind - turn), kind)
                at = pl.ds(pl.multiple_of(place * size, 16), size)
                down.append(
                    pltpu.make_async_copy(
                        piece.at[pl.ds(0, size)], held_down.at[n, at], sems.at[n, 1 + turn]
                    )
                )
                at = pl.ds(pl.multiple_of(half + place * rest, 16), rest)
                up.append(
                    pltpu.make_async_copy(
                        piece.at[pl.ds(size, rest)], held_up.at[n, at], sems.at[n, 1 + kind + turn]
                    )
                )
        for copy in up + down if up_first else down + up:
            copy.start()
        ups.append(up)
        downs.append(down)
    return ups, downs


def wait(copies):
    for copy in copies:
        copy.wait()


def by_sequence(count, value):
    return jnp.concatenate([value(slice(i * LEN, (i + 1) * LEN)) for i in range(count)], 1)


def attention_forward(which, more, keep, *refs):
    rows, segments, start, *rest = refs
    count = segments.shape[0]
    many = len(which)
    mixers, rest = rest[:many], rest[many:]
    if keep:
        first, mixed_out, probs_out, att_out, held, sems = rest
    else:
        first, held, sems = rest
    copies = load(mixers, held, sems)
    x = rows[...]
    first[...] = start[...] if more else x.astype(f32) + wide(start)
    ids = segments[...].astype(f32)
    ids_down = jnp.concatenate([ids, jnp.zeros((8 - count, LEN), f32)], 0).T
    same = jnp.concatenate([ids_down[:, i : i + 1] == ids[i : i + 1] for i in range(count)], 1)
    for n in range(many):
        copies[n].wait()
        third = (held.shape[1] - SMALL) // 4
        bias = held[n, 4 * third :].astype(f32)[:8].T[: 3 * third, :1]
        mixed = (nt(held[n, : 3 * third], x) + bias).astype(bf16)
        query, keys, value = mixed[:third] * HEAD**-0.5, mixed[third : 2 * third], mixed[2 * third :]
        if keep:
            mixed_out[n, :third] = query
            mixed_out[n, third:] = mixed[third:]
        heads = []
        for h in range(third // HEAD):
            at = slice(h * HEAD, (h + 1) * HEAD)
            scores = by_sequence(count, lambda cols: tn(keys[at, cols], query[at, cols]))
            scores = jnp.where(same, scores, -1e9)
            probs = jnp.exp(scores - jnp.max(scores, 0, keepdims=True))
            probs = probs * (1.0 / jnp.sum(probs, 0, keepdims=True))
            if keep:
                probs_out[n, h] = probs
            low = probs.astype(bf16)
            heads.append(by_sequence(count, lambda cols: nn(value[at, cols], low[:, cols])))
        attended = jnp.concatenate(heads, 0).astype(bf16)
        if keep:
            att_out[n] = attended
        first[...] += tn(attended, held[n, 3 * third : 4 * third])


def mlp_forward(kinds, more, last, keep, *refs):
    rotation, first, gain_one, shift_one, gain_two, shift_two, bias_down, *rest = refs
    if more:
        start, *rest = rest
    many = len(kinds)
    *rest, held_up, held_down, held_tail, sems, sem_tail = rest
    outs = 5 if keep else 2 if last else 1
    rest, outs = rest[:-outs], rest[-outs:]
    mixers, weights = rest[:many], rest[many:]
    edge = mixers[0].shape[0] - SMALL
    tails = load([item.at[pl.ds(edge, SMALL)] for item in mixers], held_tail, sem_tail)
    ups, downs = load_mlp(kinds, weights, rotation, held_up, held_down, sems, True)
    second = outs[-1]
    normed, _ = standardize(first[...])
    hidden = normed * wide(gain_one) + wide(shift_one)
    hidden_low = hidden.astype(bf16)
    second[...] = start[...] if more else hidden + wide(bias_down)
    if keep:
        out, hidden_out, active_out, slope_out, _ = outs
        hidden_out[...] = hidden_low
    wait(tails)
    for n in range(many):
        wait(ups[n])
        upward = nn(hidden_low, held_up[n]) + held_tail[n].astype(f32)[1:2]
        normal = 0.5 * (1.0 + lax.erf(upward * 0.7071067811865476))
        active = (upward * normal).astype(bf16)
        if keep:
            density = jnp.exp(-0.5 * upward * upward) * 0.3989422804014327
            active_out[n] = active
            slope_out[n] = (normal + upward * density).astype(bf16)
        wait(downs[n])
        second[...] += nn(active, held_down[n])
    if last:
        normed, _ = standardize(second[...])
        outs[0][...] = (normed * wide(gain_two) + wide(shift_two)).astype(bf16)


def down_grads(which, *refs):
    if which == FAR_PAIR:
        grad_output, second, gain_two, active, *parts, branch_two, grad_second, sums = refs
        g = wide(grad_output)
        normed, inverse = standardize(second[...])
        back = norm_back(normed, inverse, wide(gain_two), g)
        grad_second[...] = back
        low = back.astype(bf16)
        branch_two[...] = low
        sums[0:1] = jnp.sum(back, 0, keepdims=True)
        sums[1:2] = jnp.sum(g * normed, 0, keepdims=True)
        sums[2:3] = jnp.sum(g, 0, keepdims=True)
    else:
        branch_two, active, *parts = refs
        low = branch_two[...]
    for n, s in enumerate(which):
        parts[n][...] = tn(active[s], low).astype(bf16)


def mlp_backward(which, kinds, last, full, *refs):
    if full:
        rotation, branch_two, start, slope, hidden_low, first, gain_one, *rest = refs
    else:
        rotation, grad_output, second, gain_two, slope, first, gain_one, *rest = refs
    *rest, held_up, held_down, sems = rest
    many = len(which)
    ins = sum(1 + kind for kind in kinds)
    weights, rest = rest[:ins], rest[ins:]
    ups, downs = load_mlp(kinds, weights, rotation, held_up, held_down, sems, False)
    if full:
        parts, grad_bias_up, rest = rest[:many], rest[many], rest[many + 1 :]
    if last:
        grad_first, branch_one, *rest = rest
        sums = rest[0] if full else None
    total = rest[-1]
    if full:
        low = branch_two[...]
        total[...] = start[...]
        x = hidden_low[...]
    else:
        normed, inverse = standardize(second[...])
        back = norm_back(normed, inverse, wide(gain_two), wide(grad_output))
        low = back.astype(bf16)
        total[...] = back
    for n, s in enumerate(which):
        wait(downs[n])
        grad_upward = (nt(low, held_down[n]) * slope[s].astype(f32)).astype(bf16)
        if full:
            parts[n][...] = tn(x, grad_upward).astype(bf16)
            grad_bias_up[n] = jnp.sum(grad_upward.astype(f32), 0, keepdims=True)
        wait(ups[n])
        total[...] += nt(grad_upward, held_up[n])
    if not last:
        return
    grad_hidden = total[...]
    normed, inverse = standardize(first[...])
    back = norm_back(normed, inverse, wide(gain_one), grad_hidden)
    grad_first[...] = back
    branch_one[...] = back.astype(bf16)
    if full:
        sums[0:1] = jnp.sum(back, 0, keepdims=True)
        sums[1:2] = jnp.sum(grad_hidden * normed, 0, keepdims=True)
        sums[2:3] = jnp.sum(grad_hidden, 0, keepdims=True)


def attention_backward(which, last, full, count, *refs):
    branch_one, start, mixed_in, probs_in, *rest = refs
    if full:
        rows, attended, sums_two, sums_one, grad_bias_up, *rest = rest
        ones = jnp.ones((16, rows.shape[0]), bf16)
    many = len(which)
    *rest, held, sems = rest
    mixers, rest = rest[:many], rest[many:]
    copies = load(mixers, held, sems)
    total = rest[-1]
    if full:
        parts = rest[:many]
    if last:
        grad_in = rest[-2]
    branch = branch_one[...]
    total[...] = start[...]
    scale = HEAD**-0.5
    for n, s in enumerate(which):
        copies[n].wait()
        third = (held.shape[1] - SMALL) // 4
        if full:
            parts[n][:third] = nn(attended[s], branch).astype(bf16)
        grad_att = nt(held[n, 3 * third : 4 * third], branch).astype(bf16)
        pieces = ([], [], [])
        for h in range(third // HEAD):
            at = slice(h * HEAD, (h + 1) * HEAD)
            query = mixed_in[s, at]
            keys = mixed_in[s, third + at.start : third + at.stop]
            value = mixed_in[s, 2 * third + at.start : 2 * third + at.stop]
            probs = probs_in[s, h]
            low = probs.astype(bf16)
            grads = grad_att[at]
            grad_probs = by_sequence(count, lambda cols: tn(value[:, cols], grads[:, cols]))
            inner = jnp.sum(probs * grad_probs, 0, keepdims=True)
            grad_scores = (probs * (grad_probs - inner)).astype(bf16)
            pieces[0].append(
                by_sequence(count, lambda cols: nn(keys[:, cols], grad_scores[:, cols])) * scale
            )
            pieces[1].append(
                by_sequence(count, lambda cols: nt(query[:, cols], grad_scores[:, cols]))
            )
            pieces[2].append(by_sequence(count, lambda cols: nt(grads[:, cols], low[:, cols])))
        grad_mixed = jnp.concatenate([p for piece in pieces for p in piece], 0).astype(bf16)
        if full:
            parts[n][third : 4 * third] = nn(grad_mixed, rows[...]).astype(bf16)
            columns = nt(ones, grad_mixed)
            blank = jnp.zeros((1, rows.shape[1] - third), f32)
            small = [
                grad_bias_up[n],
                jnp.concatenate([columns[:1, :third], blank], 1),
                jnp.concatenate([columns[:1, 2 * third :], blank], 1),
                sums_two[...],
                sums_one[...],
                jnp.zeros((SMALL - 9, rows.shape[1]), f32),
            ]
            parts[n][4 * third :] = jnp.concatenate(small, 0).astype(bf16)
        total[...] += tn(grad_mixed, held[n, : 3 * third])
    if last:
        grad_in[...] = total[...].astype(bf16)


def pack(count, rotation, bias_qv, bias_up, qkv, outer, up, down, *refs):
    third = outer.shape[0]
    mixer, *refs = refs
    copies = [
        (qkv, mixer.at[pl.ds(0, 3 * third)]),
        (outer, mixer.at[pl.ds(3 * third, third)]),
    ]
    if count > 1:
        piece, *refs = refs
        size, half = down.shape[0] // count, up.shape[0] // 2
        part = half // count
        at = pl.multiple_of(rotation[0] * size, 16)
        copies.append((down.at[pl.ds(at, size)], piece.at[pl.ds(0, size)]))
        at = pl.multiple_of(half + rotation[0] * part, 16)
        copies.append((up.at[pl.ds(at, part)], piece.at[pl.ds(size, part)]))
    copies = [pltpu.make_async_copy(*pair, refs[0].at[n]) for n, pair in enumerate(copies)]
    for copy in copies:
        copy.start()
    none = jnp.zeros((1, third), f32)
    biases = jnp.concatenate([wide(bias_qv)[:1], none, wide(bias_qv)[1:], none], 1)
    rest = jnp.zeros((SMALL - 2, biases.shape[1]), f32)
    mixer[4 * third :] = jnp.concatenate([biases, wide(bias_up), rest], 0).astype(bf16)
    wait(copies)


def run_pack(count, rotation, bias_qv, bias_up, qkv, outer, up, down):
    third, width = outer.shape
    outputs = [shape((4 * third + SMALL, width), bf16)]
    if count > 1:
        outputs += [shape((down.shape[0] // count + up.shape[0] // 2 // count, width), bf16)]
    return pl.pallas_call(
        functools.partial(pack, count),
        name="pack",
        out_shape=outputs,
        in_specs=[SM, VM, VM, ANY, ANY, ANY, ANY],
        out_specs=[VM] * len(outputs),
        scratch_shapes=[pltpu.SemaphoreType.DMA((4,))],
    )(rotation, bias_qv, bias_up, qkv, outer, up, down)


def shape(dims, dtype):
    return jax.ShapeDtypeStruct(dims, dtype)


def launch(kernel, name, operands, weights, outputs, scratch, flops, scalars=0):
    size = sum(item.size * item.dtype.itemsize for item in [*operands, *weights, *outputs])
    return pl.pallas_call(
        kernel,
        name=name,
        out_shape=outputs,
        in_specs=[SM] * scalars + [VM] * (len(operands) - scalars) + [ANY] * len(weights),
        out_specs=[VM] * len(outputs),
        scratch_shapes=scratch,
        compiler_params=pltpu.CompilerParams(vmem_limit_bytes=56 << 20),
        cost_estimate=pl.CostEstimate(flops=flops, bytes_accessed=size, transcendentals=0),
    )(*operands, *weights)


def mixer_scratch(many, mixer):
    return [pltpu.VMEM((many,) + mixer.shape, bf16), pltpu.SemaphoreType.DMA((many,))]


def mlp_scratch(w, which):
    size = w["mlp"][0][0].shape
    most = max(len(w["mlp"][s]) - 1 for s in which)
    return [
        pltpu.VMEM((len(which),) + size, bf16),
        pltpu.VMEM((len(which),) + size[::-1], bf16),
        pltpu.SemaphoreType.DMA((len(which), 1 + 2 * most)),
    ]


def kinds_of(w, which):
    return tuple(len(w["mlp"][s]) - 1 for s in which)


def take(items, which):
    return [items[s] for s in which]


def flat(items, which):
    return [item for s in which for item in items[s]]


def run_attention_forward(which, keep, rows, segments, w, start=None):
    size, width = rows.shape
    many = len(which)
    third = (w["mix"][0].shape[0] - SMALL) // 4
    outputs = [shape((size, width), f32)]
    if keep:
        outputs += [
            shape((many, 3 * third, size), bf16),
            shape((many, third // HEAD, LEN, size), f32),
            shape((many, third, size), bf16),
        ]
    more = start is not None
    return launch(
        functools.partial(attention_forward, which, more, keep),
        "attention_forward",
        [rows, segments, start if more else w["bias_out"]],
        take(w["mix"], which),
        outputs,
        mixer_scratch(many, w["mix"][0]),
        8 * many * size * third * width,
    )


def run_mlp_forward(which, last, keep, first, w, start=None):
    size, width = first.shape
    units, many = w["mlp"][0][0].shape[1], len(which)
    outputs = [shape((size, width), bf16)] if last else []
    if keep:
        outputs += [
            shape((size, width), bf16),
            shape((many, size, units), bf16),
            shape((many, size, units), bf16),
        ]
    outputs += [shape((size, width), f32)]
    names = ("gain_one", "shift_one", "gain_two", "shift_two", "bias_down")
    operands = [w["rotation"], first, *[w[name] for name in names]]
    more = start is not None
    if more:
        operands += [start]
    held_up, held_down, sems = mlp_scratch(w, which)
    return launch(
        functools.partial(mlp_forward, kinds_of(w, which), more, last, keep),
        "mlp_forward",
        operands,
        take(w["mix"], which) + flat(w["mlp"], which),
        outputs,
        [
            held_up,
            held_down,
            pltpu.VMEM((many, SMALL, width), bf16),
            sems,
            pltpu.SemaphoreType.DMA((many,)),
        ],
        4 * many * size * units * width,
        1,
    )


def run_down_grads(which, operands):
    size, width = operands[0].shape
    units = operands[-1].shape[2]
    outputs = [shape((units, width), bf16)] * len(which)
    if which == FAR_PAIR:
        outputs += [shape((size, width), bf16), shape((size, width), f32), shape((3, width), f32)]
    return launch(
        functools.partial(down_grads, which),
        "down_grads",
        operands,
        [],
        outputs,
        [],
        4 * size * units * width,
    )


def run_mlp_backward(which, last, full, operands, w):
    units, many = w["mlp"][0][0].shape[1], len(which)
    size, width = operands[0].shape
    outputs = []
    if full:
        outputs = [shape((width, units), bf16)] * many + [shape((many, 1, units), f32)]
    if last:
        outputs += [shape((size, width), f32), shape((size, width), bf16)]
        if full:
            outputs += [shape((3, width), f32)]
    outputs += [shape((size, width), f32)]
    return launch(
        functools.partial(mlp_backward, which, kinds_of(w, which), last, full),
        "mlp_backward",
        [w["rotation"], *operands],
        flat(w["mlp"], which),
        outputs,
        mlp_scratch(w, which),
        (6 if full else 4) * many * size * units * width,
        1,
    )


def run_attention_backward(which, last, full, operands, w):
    size, width = operands[0].shape
    many = len(which)
    third = (w["mix"][0].shape[0] - SMALL) // 4
    outputs = []
    if full:
        outputs = [shape((4 * third + SMALL, width), bf16)] * many
    if last:
        outputs += [shape((size, width), bf16)]
    outputs += [shape((size, width), f32)]
    return launch(
        functools.partial(attention_backward, which, last, full, size // LEN),
        "attention_backward",
        operands,
        take(w["mix"], which),
        outputs,
        mixer_scratch(many, w["mix"][0]),
        (16 if full else 8) * many * size * third * width,
    )


def to_partner(x, bits):
    size = lax.axis_size("tensor")
    return lax.ppermute(x, "tensor", [(i, i ^ bits) for i in range(size)])


def add(*items):
    return sum(item.astype(f32) for item in items).astype(bf16)


def tie(value, *others):
    return lax.optimization_barrier((value, *others))[0]


class Line:
    lag = 3

    def __init__(self):
        self.size = lax.axis_size("dp")
        place = lax.axis_index("dp")
        self.middle = (place == 1) | (place == 2)
        self.parts, self.sent, self.pairs, self.totals, self.done = [], [], [], [], []
        self.last = jnp.zeros((8, 128), bf16)

    def add(self, *items):
        *items, _ = lax.optimization_barrier((*items, self.last))
        self.last = add(*items)
        return self.last

    def exchange(self, *fresh):
        if self.size != 4:
            if fresh:
                self.done.append(lax.psum(self.add(*fresh), "dp"))
            return
        routes, items = [], []
        step = len(self.sent)
        back = step - self.lag
        if back >= 0:
            items += list(self.pairs[back])
            routes += [(1, 0), (2, 3)]
        if fresh:
            routes += [(0, 1), (3, 2)]
        *values, _ = lax.optimization_barrier((*items, *fresh, self.last))
        total = add(*values[:2]) if back >= 0 else None
        part = add(*values[len(items) :]) if fresh else None
        if back >= 0:
            self.totals.append(total)
        if fresh:
            self.parts.append(values[len(items) :])
        if total is None or part is None:
            operand = part if total is None else total
        else:
            rows = max(total.shape[0], part.shape[0])
            total, part = [jnp.pad(v, ((0, rows - v.shape[0]), (0, 0))) for v in (total, part)]
            operand = jnp.where(self.middle, total, part)
        self.last = operand
        received = lax.ppermute(operand, "dp", routes)
        self.sent.append(received)
        if back >= 0:
            total = self.totals[back]
            self.done.append(jnp.where(self.middle, total, received[: total.shape[0]]))

    def inner(self):
        if self.size != 4:
            return
        part = self.parts[len(self.pairs)]
        received = self.sent[len(self.pairs)]
        pair = self.add(*part, received[: part[0].shape[0]])
        self.pairs.append((pair, lax.ppermute(pair, "dp", [(1, 2), (2, 1)])))


def all_rows(own, near, far, both):
    place = lax.axis_index("tensor")
    low, high = place % 2 == 1, place // 2 == 1
    first = [jnp.where(low, near, own), jnp.where(low, own, near)]
    second = [jnp.where(low, both, far), jnp.where(low, far, both)]
    return [jnp.where(high, b, a) for a, b in zip(first, second)] + [
        jnp.where(high, a, b) for a, b in zip(first, second)
    ]


def body(
    ends_in,
    segment_ids,
    w_qkv,
    bias_qv,
    w_out,
    bias_out,
    gain_one,
    shift_one,
    w_up,
    bias_up,
    w_down,
    bias_down,
    gain_two,
    shift_two,
):
    section = lax.axis_index("section")
    place = lax.axis_index("tensor")
    _, micro, count, length, width = ends_in.shape
    share = count // lax.axis_size("tensor")
    own = lax.dynamic_slice_in_dim(ends_in[0], place * share, share, 1)
    own = own.reshape(micro * share * length, width)
    segments = lax.dynamic_slice_in_dim(segment_ids, place * share, share, 1)
    segments = segments.reshape(micro * share, length)
    third = w_qkv.shape[3]
    rotation = lax.axis_index("dp").astype(jnp.int32).reshape(1)
    w = {
        "rotation": rotation,
        "bias_out": bias_out,
        "gain_one": gain_one,
        "shift_one": shift_one,
        "bias_down": bias_down,
        "gain_two": gain_two,
        "shift_two": shift_two,
    }
    up, down = w_up[0], w_down[0]
    turns = lax.axis_size("dp") if lax.axis_size("dp") == 4 else 1
    mixer, *pieces = run_pack(
        turns, rotation, bias_qv[0], bias_up, w_qkv[0].reshape(width, -1).T, w_out[0], up, down
    )
    pieces = [to_partner(item, 2) for item in pieces]
    mixer_near, up_near, down_near = [to_partner(item, 1) for item in (mixer, up, down)]
    mixer_far = to_partner(mixer, 2)
    w["mix"] = [mixer, mixer_near]
    w["mlp"] = [[up, down], [up_near, down_near]]
    (first,) = run_attention_forward(NEAR_PAIR, False, own, segments, w)
    if turns > 1:
        pieces[0] = tie(pieces[0], first, up_near, down_near)
        near_pieces = [to_partner(pieces[0], 1)]
        for turn in range(1, turns):
            pairs = [(i, (i + turn) % turns) for i in range(turns)]
            pieces.append(lax.ppermute(pieces[0], "dp", pairs))
        rest = [up[: up.shape[0] // 2]]
    else:
        near_pieces, rest = [], [up, down]
    mixer_far = tie(mixer_far, first, *near_pieces)
    w["mix"] += [mixer_far, to_partner(mixer_far, 1)]
    rest = [to_partner(tie(item, mixer_far), 2) for item in rest]
    (first,) = run_attention_forward(FAR_PAIR, False, own, segments, w, first)
    (second,) = run_mlp_forward(NEAR_PAIR, False, False, first, w)
    far = rest + pieces
    *far, _ = lax.optimization_barrier((*far, second))
    near = [to_partner(item, 1) for item in far]
    w["mlp"] += [far, near[: len(rest)] + (near_pieces or []) + near[len(rest) + len(near_pieces) :]]
    out, _ = run_mlp_forward(FAR_PAIR, True, False, first, w, second)
    received = lax.ppermute(out, "section", [(0, 1)])
    rows = jnp.where(section == 0, own, received)
    first, mixed, probs, attended = run_attention_forward(ALL, True, rows, segments, w)
    out, hidden, active, slope, second = run_mlp_forward(ALL, True, True, first, w)
    grad_first, branch_one, _ = run_mlp_backward(
        ALL, True, False, [own, second, gain_two, slope, first, gain_one], w
    )
    grad_in, _ = run_attention_backward(
        ALL, True, False, [branch_one, grad_first, mixed, probs], w
    )
    returned = lax.ppermute(grad_in, "section", [(1, 0)])
    cotangent = jnp.where(section == 1, own, returned)

    line = Line()

    def swap(send):
        return to_partner(tie(send, line.last), 1)

    def halves(keep):
        half = keep.shape[0] // 2 // 16 * 16
        return slice(0, half), slice(half, None)

    def cross(keep, received):
        return [to_partner(line.add(keep[cut], received[cut]), 2) for cut in halves(keep)]

    def chunks(keep, received, far):
        return [(keep[cut], received[cut], item) for cut, item in zip(halves(keep), far)]

    keep, send, branch_two, grad_second, sums_two = run_down_grads(
        FAR_PAIR, [cotangent, second, gain_two, active]
    )
    line.last = branch_two
    received = swap(send)
    keep_near, send_near = run_down_grads(NEAR_PAIR, [branch_two, active])
    line.last = keep_near
    far = cross(keep, received)
    received = swap(send_near)
    keep, send, bias_far, total = run_mlp_backward(
        FAR_PAIR,
        False,
        True,
        [tie(branch_two, line.last), grad_second, slope, hidden, first, gain_one],
        w,
    )
    line.last = total
    down = chunks(keep_near, received, far)
    line.exchange(*down[0])
    received = swap(send)
    keep_near, send_near, bias_near, grad_first, branch_one, sums_one, line.last = run_mlp_backward(
        NEAR_PAIR,
        True,
        True,
        [tie(branch_two, line.last), total, slope, hidden, first, gain_one],
        w,
    )
    line.exchange(*down[1])
    line.inner()
    far = cross(keep, received)
    received = swap(send_near)
    keep, send, total = run_attention_backward(
        FAR_PAIR,
        False,
        True,
        [
            tie(branch_one, line.last),
            *(grad_first, mixed, probs, rows, attended, sums_two, sums_one, bias_far),
        ],
        w,
    )
    line.last = total
    up = chunks(keep_near, received, far)
    line.exchange(*up[0])
    line.inner()
    received = swap(send)
    keep_near, send_near, grad_in, line.last = run_attention_backward(
        NEAR_PAIR,
        True,
        True,
        [
            tie(branch_one, line.last),
            *(total, mixed, probs, rows, attended, sums_two, sums_one, bias_near),
        ],
        w,
    )
    line.exchange(*up[1])
    line.inner()
    far = cross(keep, received)
    mixer = chunks(keep_near, swap(send_near), far)
    mine = jnp.where(section == 1, out, grad_in).reshape(micro, share, length, width)
    line.exchange(*mixer[0])
    line.inner()
    line.exchange(*mixer[1])
    mine = tie(mine, line.last)
    mine_far = to_partner(mine, 2)
    line.inner()
    line.exchange()
    line.inner()
    line.exchange()
    mine, mine_far, _ = lax.optimization_barrier((mine, mine_far, line.last))
    near = to_partner(mine, 1), to_partner(mine_far, 1)
    line.exchange()
    mine, near, mine_far, both, _ = lax.optimization_barrier(
        (mine, near[0], mine_far, near[1], line.last)
    )
    ends = all_rows(mine, near, mine_far, both)
    down, up, mixer = line.done[:2], line.done[2:4], line.done[4:]
    half = mixer[0].shape[0]
    qkv = jnp.concatenate([mixer[0][third:], mixer[1][: 4 * third - half]], 0)
    small = mixer[1][4 * third - half :]
    results = (
        jnp.concatenate(ends, 1),
        qkv.T.reshape(width, 3, third),
        small[1:3, :third],
        mixer[0][:third],
        small[6],
        small[7],
        small[8],
        jnp.concatenate(up, 0),
        small[0],
        jnp.concatenate(down, 0),
        small[3],
        small[4],
        small[5],
    )
    return tuple(item.astype(f32)[None] for item in results)


def solution(mesh):
    return jax.shard_map(
        body,
        mesh=mesh,
        in_specs=(
            P("section", None, "dp", None, None),
            P(None, "dp", None),
            P("section", None, None, "tensor"),
            P("section", None, "tensor"),
            P("section", "tensor", None),
            P("section", None),
            P("section", None),
            P("section", None),
            P("section", None, "tensor"),
            P("section", "tensor"),
            P("section", "tensor", None),
            P("section", None),
            P("section", None),
            P("section", None),
        ),
        out_specs=(
            P("section", None, "dp", None, None),
            P("section", None, None, "tensor"),
            P("section", None, "tensor"),
            P("section", "tensor", None),
            P("section", None),
            P("section", None),
            P("section", None),
            P("section", None, "tensor"),
            P("section", "tensor"),
            P("section", "tensor", None),
            P("section", None),
            P("section", None),
            P("section", None),
        ),
        check_vma=False,
    )
```

time: 487 us -> 390 us (0.80)
  waiting for transfers between devices: 259 us -> 146 us
  Pallas kernels: 117 us -> 138 us
  local copies, waits for them, and re-layouts: 9.63 us -> 19.1 us
  other arithmetic: 34.2 us -> 28.3 us
  starting transfers between devices: 56.6 us -> 51.6 us
    ppermute x30 -> x27, waiting for transfers between devices: 140 us -> 51.9 us  [to_partner(): return lax.ppermute(x, 'tensor', [(i, i ^ bits) for i in range(size)])]
    ppermute x18, waiting for transfers between devices: 90.3 us -> 66.3 us  [the longest x9 45.1 us: exchange(): received = lax.ppermute(operand, 'dp', routes)]
    pallas_call x9 -> x15, Pallas kernels: 117 us -> 138 us  [the longest x14 134 us: launch(): pl.pallas_call(kernel, name=name, out_shape=outputs, in_specs=[SM] * scal...]
    slice x2 -> x18, local copies, waits for them, and re-layouts: 0.81 us -> 11.4 us  [the longest x4 3.28 us: chunks(): keep[cut]]
    convert_element_type x7 -> x0, other arithmetic: 8.32 us -> none  [the longest x1 1.28 us: body(): bias_out.astype(f32)]
    ppermute x30 -> x27, starting transfers between devices: 20.2 us -> 13.7 us  [to_partner(): return lax.ppermute(x, 'tensor', [(i, i ^ bits) for i in range(size)])]
    convert_element_type x24 -> x19, other arithmetic: 10.4 us -> 9.63 us  [add(): return sum((item.astype(f32) for item in items)).astype(bf16)]
  transfers between devices with their start and end apart: 50 -> 47, of which waited for: 23 -> 19; matrix products, arithmetic and copies ran while one was open for 8% -> 9% of each run, Pallas kernels for 3% -> 18%
where the time goes in v3:
time: 390 us; the launch traced here: 385 us
  waiting for transfers between devices  146 us (37%)
  Pallas kernels  138 us (35%)
  starting transfers between devices  51.6 us (13%)
  other arithmetic  28.3 us (7%)
  local copies, waits for them, and re-layouts  19.1 us (5%)
    pallas_call x14, Pallas kernels, launch(): pl.pallas_call(kernel, name=name, out_shape=outputs, in_specs=[SM] * scal...  134 us
    ppermute x27, waiting for transfers between devices, to_partner(): return lax.ppermute(x, 'tensor', [(i, i ^ bits) for i in range(size)])  51.9 us
    ppermute x9, waiting for transfers between devices, exchange(): received = lax.ppermute(operand, 'dp', routes)  45.1 us
    ppermute x9, starting transfers between devices, exchange(): received = lax.ppermute(operand, 'dp', routes)  22.3 us
    ppermute x3, waiting for transfers between devices, body(): pieces.append(lax.ppermute(pieces[0], 'dp', pairs))  21.2 us
    ppermute x1, waiting for transfers between devices, body(): returned = lax.ppermute(grad_in, 'section', [(1, 0)])  15.2 us
    ppermute x27, starting transfers between devices, to_partner(): return lax.ppermute(x, 'tensor', [(i, i ^ bits) for i in range(size)])  13.7 us
    ppermute x1, waiting for transfers between devices, body(): received = lax.ppermute(out, 'section', [(0, 1)])  12.9 us
  transfers between devices with their start and end apart: 47, of which 19 were waited for; matrix products, arithmetic and copies ran while one was open for 9% of the time, Pallas kernels for 18%

profile of v3, /device:TPU:0, one launch (start us, length us, event | category | flops | bytes accessed | tf_op | source)
XLA Modules:
  0.0 385.0 jit_solution(4782595975981541296)
XLA Ops:
  0.7 3.5 pack.1
  5.2 2.6 collective-permute-start.1
  9.9 7.0 %attention_forward.3.refs_2_ = f32[384,768]{1,0:T(8,128)} custom-call(bf16[384,768]{1,0:T(8,128)(2,1)} %bitcast.64, s32[3,128]{1,0:T(4,128)} %bitcast.73, bf16[1,768]{1,0:T(2,128)(2,1)} %refs_2_.9, bf16[784,768]{1,0:T(8,128)(2,1)} %get-tuple-element.142.refs_3_.refs_7_.refs_4_.refs_9_, bf16[784,768]{1,0:T(8,128)(2,1)} %collective-permute-done.refs_4_.refs_8_.refs_5_.refs_10_), custom_call_target="tpu_custom_call" | custom-call | flops 905969664 | bytes 4180992 | tf_op jit(solution)/shard_map/attention_forward/pallas_call | solution.py:356
  17.0 27.7 %collective-permute-done.2.refs_11_.refs_16_.refs_12_.refs_8_ = bf16[288,768]{1,0:T(8,128)(2,1)} collective-permute-done((bf16[288,768]{1,0:T(8,128)(2,1)}, bf16[288,768]{1,0:T(8,128)(2,1)}, u32[]{:S(2)}, u32[]{:S(2)}) %collective-permute-start.2) | collective-permute-done | bytes 442400 | tf_op jit(solution)/shard_map/ppermute | solution.py:515
  44.7 2.0 collective-permute-done.5.refs_16_.refs_21_.refs_17_.refs_13_
  46.8 1.8 collective-permute-start.7
  48.7 3.6 collective-permute-start.10
  54.5 7.4 %attention_forward.4.refs_1_ = f32[384,768]{1,0:T(8,128)} custom-call(bf16[384,768]{1,0:T(8,128)(2,1)} %bitcast.65, s32[3,128]{1,0:T(4,128)} %bitcast.74, f32[384,768]{1,0:T(8,128)} %attention_forward.3.refs_2_, bf16[784,768]{1,0:T(8,128)(2,1)} %collective-permute-done.1.refs_3_.refs_8_.refs_5_.refs_9_.refs_6_, bf16[784,768]{1,0:T(8,128)(2,1)} %copy-done.3), custom_call_target="tpu_custom_call" | custom-call | flops 905969664 | bytes 5359104 | tf_op jit(solution)/shard_map/attention_forward/pallas_call | solution.py:356
  61.9 7.4 %mlp_forward.3.refs_7_ = f32[384,768]{1,0:T(8,128)} custom-call(s32[1]{0:T(128)} %bitcast.rotation.refs_0_, f32[384,768]{1,0:T(8,128)} %attention_forward.4.refs_1_, bf16[1,768]{1,0:T(2,128)(2,1)} %refs_6_.11, bf16[1,768]{1,0:T(2,128)(2,1)} %refs_3_.6, bf16[1,768]{1,0:T(2,128)(2,1)} %refs_2_.11, bf16[1,768]{1,0:T(2,128)(2,1)} %refs_5_.5, ...), custom_call_target="tpu_custom_call" | custom-call | flops 1811939328 | bytes 9494020 | tf_op jit(solution)/shard_map/mlp_forward/pallas_call | solution.py:356
  69.3 21.2 %collective-permute-done.9.refs_13_.refs_18_.refs_14_.refs_10_ = bf16[288,768]{1,0:T(8,128)(2,1)S(1)} collective-permute-done((bf16[288,768]{1,0:T(8,128)(2,1)}, bf16[288,768]{1,0:T(8,128)(2,1)S(1)}, u32[]{:S(2)}, u32[]{:S(2)}) %collective-permute-start.9) | collective-permute-done | bytes 442400 | tf_op jit(solution)/shard_map/ppermute | solution.py:644
  91.6 1.6 collective-permute-done.12.refs_17_.refs_22_.refs_18_.refs_14_
  96.1 8.3 %mlp_forward.4 = (bf16[384,768]{1,0:T(8,128)(2,1)}, f32[384,768]{1,0:T(8,128)}) custom-call(s32[1]{0:T(128)} %bitcast.rotation.refs_0_, f32[384,768]{1,0:T(8,128)} %attention_forward.4.refs_1_, bf16[1,768]{1,0:T(2,128)(2,1)} %refs_6_.11, bf16[1,768]{1,0:T(2,128)(2,1)} %refs_3_.6, bf16[1,768]{1,0:T(2,128)(2,1)} %refs_2_.11, bf16[1,768]{1,0:T(2,128)(2,1)} %refs_5_.5, ...), custom_call_target="tpu_custom_call" | custom-call | flops 1811939328 | bytes 11263492 | tf_op jit(solution)/shard_map/mlp_forward/pallas_call | solution.py:356
  104.3 3.7 collective-permute-start.15
  108.0 12.9 %collective-permute-done.15 = bf16[384,768]{1,0:T(8,128)(2,1)S(1)} collective-permute-done((bf16[384,768]{1,0:T(8,128)(2,1)}, bf16[384,768]{1,0:T(8,128)(2,1)S(1)}, u32[]{:S(2)}, u32[]{:S(2)}) %collective-permute-start.15) | collective-permute-done | bytes 589856 | tf_op jit(solution)/shard_map/ppermute | solution.py:658
  121.9 11.6 %attention_forward.5 = (f32[384,768]{1,0:T(8,128)}, bf16[4,576,384]{2,1,0:T(8,128)(2,1)}, f32[4,3,128,384]{3,2,1,0:T(8,128)}, bf16[4,192,384]{2,1,0:T(8,128)(2,1)}) custom-call(bf16[384,768]{1,0:T(8,128)(2,1)} %broadcast_select_fusion.2.refs_0_.refs_4_, s32[3,128]{1,0:T(4,128)} %bitcast.75, bf16[1,768]{1,0:T(2,128)(2,1)} %refs_2_.9, ...), custom_call_target="tpu_custom_call" | custom-call | flops 1811939328 | bytes 11308032 | tf_op jit(solution)/shard_map/attention_forward/pallas_call | solution.py:356
  133.4 14.3 %mlp_forward.5 = (bf16[384,768]{1,0:T(8,128)(2,1)}, bf16[384,768]{1,0:T(8,128)(2,1)}, bf16[4,384,768]{2,1,0:T(8,128)(2,1)}, bf16[4,384,768]{2,1,0:T(8,128)(2,1)}, f32[384,768]{1,0:T(8,128)}) custom-call(s32[1]{0:T(128)} %bitcast.rotation.refs_0_, f32[384,768]{1,0:T(8,128)} %get-tuple-element.153.refs_1_.refs_5_, bf16[1,768]{1,0:T(2,128)(2,1)} %refs_6_.11, ...), custom_call_target="tpu_custom_call" | custom-call | flops 3623878656 | bytes 22519300 | tf_op jit(solution)/shard_map/mlp_forward/pallas_call | solution.py:356
  147.8 12.9 %mlp_backward.3 = (f32[384,768]{1,0:T(8,128)}, bf16[384,768]{1,0:T(8,128)(2,1)}, f32[384,768]{1,0:T(8,128)}) custom-call(s32[1]{0:T(128)} %bitcast.rotation.refs_0_, bf16[384,768]{1,0:T(8,128)(2,1)} %bitcast.66, f32[384,768]{1,0:T(8,128)} %get-tuple-element.155.refs_2_.refs_1_, bf16[1,768]{1,0:T(2,128)(2,1)} %refs_2_.11, ...), custom_call_target="tpu_custom_call" | custom-call | flops 3623878656 | bytes 17697796 | tf_op jit(solution)/shard_map/mlp_backward/pallas_call | solution.py:356
  160.7 13.6 %attention_backward.3 = (bf16[384,768]{1,0:T(8,128)(2,1)}, f32[384,768]{1,0:T(8,128)}) custom-call(bf16[384,768]{1,0:T(8,128)(2,1)} %get-tuple-element.157.refs_0_, f32[384,768]{1,0:T(8,128)} %get-tuple-element.158.refs_1_, bf16[4,576,384]{2,1,0:T(8,128)(2,1)} %get-tuple-element.159.refs_2_, f32[4,3,128,384]{3,2,1,0:T(8,128)} %get-tuple-element.160.refs_3_, ...), custom_call_target="tpu_custom_call" | custom-call | flops 1811939328 | bytes 12484608 | tf_op jit(solution)/shard_map/attention_backward/pallas_call | solution.py:356
  175.8 15.2 %collective-permute-done.16 = bf16[384,768]{1,0:T(8,128)(2,1)S(1)} collective-permute-done((bf16[384,768]{1,0:T(8,128)(2,1)}, bf16[384,768]{1,0:T(8,128)(2,1)S(1)}, u32[]{:S(2)}, u32[]{:S(2)}) %collective-permute-start.16) | collective-permute-done | bytes 589856 | tf_op jit(solution)/shard_map/ppermute | solution.py:668
  191.9 5.6 %down_grads.2 = (bf16[768,768]{1,0:T(8,128)(2,1)}, bf16[768,768]{1,0:T(8,128)(2,1)}, bf16[384,768]{1,0:T(8,128)(2,1)}, f32[384,768]{1,0:T(8,128)}, f32[3,768]{1,0:T(4,128)}) custom-call(bf16[384,768]{1,0:T(8,128)(2,1)} %broadcast_select_fusion.4.refs_0_, f32[384,768]{1,0:T(8,128)} %get-tuple-element.155.refs_2_.refs_1_, bf16[1,768]{1,0:T(2,128)(2,1)} %refs_2_.11, ...), custom_call_target="tpu_custom_call" | custom-call | flops 905969664 | bytes 8268288 | tf_op jit(solution)/shard_map/down_grads/pallas_call | solution.py:356
  197.5 4.4 %down_grads.3 = (bf16[768,768]{1,0:T(8,128)(2,1)}, bf16[768,768]{1,0:T(8,128)(2,1)}) custom-call(bf16[384,768]{1,0:T(8,128)(2,1)} %get-tuple-element.181.refs_0_.refs_1_, bf16[4,384,768]{2,1,0:T(8,128)(2,1)} %get-tuple-element.162.refs_3_.refs_1_), custom_call_target="tpu_custom_call" | custom-call | flops 905969664 | bytes 5308416 | tf_op jit(solution)/shard_map/down_grads/pallas_call | solution.py:356
  204.4 1.6 collective-permute-start.20
  205.9 9.8 %mlp_backward.4 = (bf16[768,768]{1,0:T(8,128)(2,1)}, bf16[768,768]{1,0:T(8,128)(2,1)}, f32[2,1,768]{2,1,0:T(1,128)}, f32[384,768]{1,0:T(8,128)}) custom-call(s32[1]{0:T(128)} %bitcast.rotation.refs_0_, bf16[384,768]{1,0:T(8,128)(2,1)} %get-tuple-element.181.refs_0_.refs_1_, f32[384,768]{1,0:T(8,128)} %get-tuple-element.175.refs_2_, ...), custom_call_target="tpu_custom_call" | custom-call | flops 2717908992 | bytes 14163460 | tf_op jit(solution)/shard_map/mlp_backward/pallas_call | solution.py:356
  215.8 4.1 %collective-permute-done.19 = bf16[384,768]{1,0:T(8,128)(2,1)S(1)} collective-permute-done((bf16[384,768]{1,0:T(8,128)(2,1)S(1)}, bf16[384,768]{1,0:T(8,128)(2,1)S(1)}, u32[]{:S(2)}, u32[]{:S(2)}) %collective-permute-start.19) | collective-permute-done | bytes 589856 | tf_op jit(solution)/shard_map/ppermute | solution.py:515
  220.3 3.1 collective-permute-start.23
  223.5 8.2 %collective-permute-done.20 = bf16[384,768]{1,0:T(8,128)(2,1)S(1)} collective-permute-done((bf16[384,768]{1,0:T(8,128)(2,1)S(1)}, bf16[384,768]{1,0:T(8,128)(2,1)S(1)}, u32[]{:S(2)}, u32[]{:S(2)}) %collective-permute-start.20) | collective-permute-done | bytes 589856 | tf_op jit(solution)/shard_map/ppermute | solution.py:515
  231.7 10.5 %mlp_backward.5 = (bf16[768,768]{1,0:T(8,128)(2,1)}, bf16[768,768]{1,0:T(8,128)(2,1)}, f32[2,1,768]{2,1,0:T(1,128)}, f32[384,768]{1,0:T(8,128)}, bf16[384,768]{1...) custom-call(s32[1]{0:T(128)} %bitcast.rotation.refs_0_, bf16[384,768]{1,0:T(8,128)(2,1)} %get-tuple-element.181.refs_0_.refs_1_, ...), custom_call_target="tpu_custom_call" | custom-call | flops 2717908992 | bytes 15942148 | tf_op jit(solution)/shard_map/mlp_backward/pallas_call | solution.py:356
  243.3 2.9 collective-permute-start.21
  247.7 1.5 collective-permute-start.27
  249.2 1.5 collective-permute-start.28
  250.7 10.6 %attention_backward.4 = (bf16[784,768]{1,0:T(8,128)(2,1)}, bf16[784,768]{1,0:T(8,128)(2,1)}, f32[384,768]{1,0:T(8,128)}) custom-call(bf16[384,768]{1,0:T(8,128)(2,1)} %get-tuple-element.214.refs_0_, f32[384,768]{1,0:T(8,128)} %get-tuple-element.201.refs_1_, bf16[4,576,384]{2,1,0:T(8,128)(2,1)} %get-tuple-element.159.refs_2_, ...), custom_call_target="tpu_custom_call" | custom-call | flops 1811939328 | bytes 13099008 | tf_op jit(solution)/shard_map/attention_backward/pallas_call | solution.py:356
  263.9 5.2 %collective-permute-start.26 = (bf16[384,768]{1,0:T(8,128)(2,1)}, bf16[384,768]{1,0:T(8,128)(2,1)}, u32[]{:S(2)}, u32[]{:S(2)}) collective-permute-start(bf16[384,768]{1,0:T(8,128)(2,1)} %add_convert_fusion.16), channel_id=1, source_target_pairs={{0,4},{12,8},{1,5},{13,9},{2,6},{14,10},{3,7},{15,11},{16,20},{28,... | collective-permute-start | bytes 1769480 | tf_op jit(solution)/shard_map/ppermute | solution.py:568
  271.4 3.0 collective-permute-done.28
  274.3 11.0 %attention_backward.5 = (bf16[784,768]{1,0:T(8,128)(2,1)}, bf16[784,768]{1,0:T(8,128)(2,1)}, bf16[384,768]{1,0:T(8,128)(2,1)}, f32[384,768]{1,0:T(8,128)}) custom-call(bf16[384,768]{1,0:T(8,128)(2,1)} %get-tuple-element.214.refs_0_, f32[384,768]{1,0:T(8,128)} %get-tuple-element.206.refs_1_, bf16[4,576,384]{2,1,0:T(8,128)(2,1)} %get-tuple-element.159.refs_2_, ...), custom_call_target="tpu_custom_call" | custom-call | flops 1811939328 | bytes 13688832 | tf_op jit(solution)/shard_map/attention_backward/pallas_call | solution.py:356
  285.4 2.5 fusion.1
  287.9 2.2 add_convert_fusion.12
  299.6 9.9 %collective-permute-done.33 = bf16[384,768]{1,0:T(8,128)(2,1)S(1)} collective-permute-done((bf16[384,768]{1,0:T(8,128)(2,1)}, bf16[384,768]{1,0:T(8,128)(2,1)S(1)}, u32[]{:S(2)}, u32[]{:S(2)}) %collective-permute-start.33) | collective-permute-done | bytes 589856 | tf_op jit(solution)/shard_map/ppermute | solution.py:568
  312.4 1.7 fusion.2
  314.1 3.8 collective-permute-start.37
  321.1 3.9 %collective-permute-done.32 = bf16[400,768]{1,0:T(8,128)(2,1)S(1)} collective-permute-done((bf16[400,768]{1,0:T(8,128)(2,1)S(1)}, bf16[400,768]{1,0:T(8,128)(2,1)S(1)}, u32[]{:S(2)}, u32[]{:S(2)}) %collective-permute-start.32) | collective-permute-done | bytes 614432 | tf_op jit(solution)/shard_map/ppermute | solution.py:515
  325.5 3.3 collective-permute-start.39
  335.0 1.6 maximum_convert_fusion.2
  336.6 7.0 %collective-permute-done.39 = bf16[400,768]{1,0:T(8,128)(2,1)S(1)} collective-permute-done((bf16[400,768]{1,0:T(8,128)(2,1)S(1)}, bf16[400,768]{1,0:T(8,128)(2,1)S(1)}, u32[]{:S(2)}, u32[]{:S(2)}) %collective-permute-start.39) | collective-permute-done | bytes 614432 | tf_op jit(solution)/shard_map/ppermute | solution.py:568
  346.8 9.4 %collective-permute-done.46 = bf16[384,768]{1,0:T(8,128)(2,1)S(1)} collective-permute-done((bf16[384,768]{1,0:T(8,128)(2,1)S(1)}, bf16[384,768]{1,0:T(8,128)(2,1)S(1)}, u32[]{:S(2)}, u32[]{:S(2)}) %collective-permute-start.46) | collective-permute-done | bytes 589856 | tf_op jit(solution)/shard_map/ppermute | solution.py:568
  356.3 1.6 maximum_convert_fusion.1
  359.6 2.6 maximum_convert_fusion
  362.2 6.7 %collective-permute-done.44 = bf16[384,768]{1,0:T(8,128)(2,1)S(1)} collective-permute-done((bf16[384,768]{1,0:T(8,128)(2,1)S(1)}, bf16[384,768]{1,0:T(8,128)(2,1)S(1)}, u32[]{:S(2)}, u32[]{:S(2)}) %collective-permute-start.44) | collective-permute-done | bytes 589856 | tf_op jit(solution)/shard_map/ppermute | solution.py:568
  369.8 11.3 %collective-permute-done.45 = bf16[400,768]{1,0:T(8,128)(2,1)S(1)} collective-permute-done((bf16[400,768]{1,0:T(8,128)(2,1)S(1)}, bf16[400,768]{1,0:T(8,128)(2,1)S(1)}, u32[]{:S(2)}, u32[]{:S(2)}) %collective-permute-start.45) | collective-permute-done | bytes 614432 | tf_op jit(solution)/shard_map/ppermute | solution.py:568
  (183 shorter events, 54.5 us)
Async XLA Ops:
  4.2 5.8 %collective-permute-start = (bf16[784,768]{1,0:T(8,128)(2,1)}, bf16[784,768]{1,0:T(8,128)(2,1)}, u32[]{:S(2)}, u32[]{:S(2)}) collective-permute-start(bf16[784,768]{1,0:T(8,128)(2,1)} %get-tuple-element.142.refs_3_.refs_7_.refs_4_.refs_9_), channel_id=1, source_target_pairs={{0,1},{1,0},{2,3},{3,2},{4,5},{5,4},{6,7},{7,6},{8,9},{9,8},{10,11... | collective-permute-start | bytes 3612680 | tf_op jit(solution)/shard_map/ppermute | solution.py:515
  4.7 40.0 %collective-permute-start.4 = (bf16[768,768]{1,0:T(8,128)(2,1)}, bf16[768,768]{1,0:T(8,128)(2,1)}, u32[]{:S(2)}, u32[]{:S(2)}) collective-permute-start(bf16[768,768]{1,0:T(8,128)(2,1)} %bitcast.59), channel_id=1, source_target_pairs={{0,1},{1,0},{2,3},{3,2},{4,5},{5,4},{6,7},{7,6},{8,9},{9,8},{10,11... | collective-permute-start | bytes 3538952 | tf_op jit(solution)/shard_map/ppermute | solution.py:515
  4.8 39.9 %collective-permute-start.3 = (bf16[768,768]{1,0:T(8,128)(2,1)S(1)}, bf16[768,768]{1,0:T(8,128)(2,1)}, u32[]{:S(2)}, u32[]{:S(2)}) collective-permute-start(bf16[768,768]{1,0:T(8,128)(2,1)S(1)} %bitcast.57), channel_id=1, source_target_pairs={{0,1},{1,0},{2,3},{3,2},{4,5},{5,4},{6,7},{7,6},{8,9},{9,8},{10,11... | collective-permute-start | bytes 3538952 | tf_op jit(solution)/shard_map/ppermute | solution.py:515
  5.2 39.5 %collective-permute-start.1 = (bf16[784,768]{1,0:T(8,128)(2,1)}, bf16[784,768]{1,0:T(8,128)(2,1)}, u32[]{:S(2)}, u32[]{:S(2)}) collective-permute-start(bf16[784,768]{1,0:T(8,128)(2,1)} %get-tuple-element.142.refs_3_.refs_7_.refs_4_.refs_9_), channel_id=1, source_target_pairs={{0,2},{1,3},{2,0},{3,1},{4,6},{5,7},{6,4},{7,5},{8,10},{9,11},{10,... | collective-permute-start | bytes 3612680 | tf_op jit(solution)/shard_map/ppermute | solution.py:515
  7.8 36.9 %collective-permute-start.2 = (bf16[288,768]{1,0:T(8,128)(2,1)}, bf16[288,768]{1,0:T(8,128)(2,1)}, u32[]{:S(2)}, u32[]{:S(2)}) collective-permute-start(bf16[288,768]{1,0:T(8,128)(2,1)} %get-tuple-element.143), channel_id=1, source_target_pairs={{0,2},{1,3},{2,0},{3,1},{4,6},{5,7},{6,4},{7,5},{8,10},{9,11},{10,... | collective-permute-start | bytes 1327112 | tf_op jit(solution)/shard_map/ppermute | solution.py:515
  44.7 2.0 collective-permute-start.5
  46.7 6.8 %collective-permute-start.6 = (bf16[784,768]{1,0:T(8,128)(2,1)}, bf16[784,768]{1,0:T(8,128)(2,1)S(1)}, u32[]{:S(2)}, u32[]{:S(2)}) collective-permute-start(bf16[784,768]{1,0:T(8,128)(2,1)} %collective-permute-done.1.refs_3_.refs_8_.refs_5_.refs_9_.refs_6_), channel_id=1, source_target_pairs={{0,1},{1,0},{2,3},{3,2},{4,5},{5,4},{6,7},{7,6},{8,9},{9,8},{10,11... | collective-permute-start | bytes 3612680 | tf_op jit(solution)/shard_map/ppermute | solution.py:515
  46.8 43.7 %collective-permute-start.7 = (bf16[384,768]{1,0:T(8,128)(2,1)S(1)}, bf16[384,768]{1,0:T(8,128)(2,1)S(1)}, u32[]{:S(2)}, u32[]{:S(2)}) collective-permute-start(bf16[384,768]{1,0:T(8,128)(2,1)S(1)} %slice_bitcast_fusion), channel_id=1, source_target_pairs={{0,2},{1,3},{2,0},{3,1},{4,6},{5,7},{6,4},{7,5},{8,10},{9,11},{10,... | collective-permute-start | bytes 1769480 | tf_op jit(solution)/shard_map/ppermute | solution.py:515
  48.7 20.6 %collective-permute-start.10 = (bf16[288,768]{1,0:T(8,128)(2,1)}, bf16[288,768]{1,0:T(8,128)(2,1)S(1)}, u32[]{:S(2)}, u32[]{:S(2)}) collective-permute-start(bf16[288,768]{1,0:T(8,128)(2,1)} %collective-permute-done.2.refs_11_.refs_16_.refs_12_.refs_8_), channel_id=1, source_target_pairs={{0,12},{4,0},{8,4},{12,8},{1,13},{5,1},{9,5},{13,9},{2,14},{6,2},{... | collective-permute-start | bytes 1327112 | tf_op jit(solution)/shard_map/ppermute | solution.py:644
  52.3 38.2 %collective-permute-start.9 = (bf16[288,768]{1,0:T(8,128)(2,1)}, bf16[288,768]{1,0:T(8,128)(2,1)S(1)}, u32[]{:S(2)}, u32[]{:S(2)}) collective-permute-start(bf16[288,768]{1,0:T(8,128)(2,1)} %collective-permute-done.2.refs_11_.refs_16_.refs_12_.refs_8_), channel_id=1, source_target_pairs={{0,8},{4,12},{8,0},{12,4},{1,9},{5,13},{9,1},{13,5},{2,10},{6,14},... | collective-permute-start | bytes 1327112 | tf_op jit(solution)/shard_map/ppermute | solution.py:644
  52.3 38.2 %collective-permute-start.8 = (bf16[288,768]{1,0:T(8,128)(2,1)}, bf16[288,768]{1,0:T(8,128)(2,1)S(1)}, u32[]{:S(2)}, u32[]{:S(2)}) collective-permute-start(bf16[288,768]{1,0:T(8,128)(2,1)} %collective-permute-done.2.refs_11_.refs_16_.refs_12_.refs_8_), channel_id=1, source_target_pairs={{0,4},{4,8},{8,12},{12,0},{1,5},{5,9},{9,13},{13,1},{2,6},{6,10},{... | collective-permute-start | bytes 1327112 | tf_op jit(solution)/shard_map/ppermute | solution.py:644
  69.3 51.7 %copy-start.4 = (bf16[1,3,1,128,768]{4,3,2,1,0:T(8,128)(2,1)S(1)}, bf16[1,3,1,128,768]{4,3,2,1,0:T(8,128)(2,1)}, u32[]{:S(2)}) copy-start(bf16[1,3,1,128,768]{4,3,2,1,0:T(8,128)(2,1)} %constant_dynamic-slice_fusion.1) | copy-start | bytes 1769476
  90.5 4.0 %collective-permute-start.11 = (bf16[384,768]{1,0:T(8,128)(2,1)S(1)}, bf16[384,768]{1,0:T(8,128)(2,1)S(1)}, u32[]{:S(2)}, u32[]{:S(2)}) collective-permute-start(bf16[384,768]{1,0:T(8,128)(2,1)S(1)} %collective-permute-done.7.refs_10_.refs_15_.refs_11_.refs_7_), channel_id=1, source_target_pairs={{0,1},{1,0},{2,3},{3,2},{4,5},{5,4},{6,7},{7,6},{8,9},{9,8},{10,11... | collective-permute-start | bytes 1769480 | tf_op jit(solution)/shard_map/ppermute | solution.py:515
  90.6 2.6 collective-permute-start.12
  91.1 2.8 collective-permute-start.13
  91.2 3.3 collective-permute-start.14
  104.3 16.6 %collective-permute-start.15 = (bf16[384,768]{1,0:T(8,128)(2,1)}, bf16[384,768]{1,0:T(8,128)(2,1)S(1)}, u32[]{:S(2)}, u32[]{:S(2)}) collective-permute-start(bf16[384,768]{1,0:T(8,128)(2,1)} %get-tuple-element.152), channel_id=1, source_target_pairs={{0,16},{1,17},{2,18},{3,19},{4,20},{5,21},{6,22},{7,23},{8,24},{9,... | collective-permute-start | bytes 1769480 | tf_op jit(solution)/shard_map/ppermute | solution.py:658
  174.3 16.7 %collective-permute-start.16 = (bf16[384,768]{1,0:T(8,128)(2,1)}, bf16[384,768]{1,0:T(8,128)(2,1)S(1)}, u32[]{:S(2)}, u32[]{:S(2)}) collective-permute-start(bf16[384,768]{1,0:T(8,128)(2,1)} %get-tuple-element.161), channel_id=1, source_target_pairs={{16,0},{17,1},{18,2},{19,3},{20,4},{21,5},{22,6},{23,7},{24,8},{25... | collective-permute-start | bytes 1769480 | tf_op jit(solution)/shard_map/ppermute | solution.py:668
  197.5 4.5 %collective-permute-start.17 = (bf16[768,768]{1,0:T(8,128)(2,1)}, bf16[768,768]{1,0:T(8,128)(2,1)S(1)}, u32[]{:S(2)}, u32[]{:S(2)}) collective-permute-start(bf16[768,768]{1,0:T(8,128)(2,1)} %get-tuple-element.168), channel_id=1, source_target_pairs={{0,1},{1,0},{2,3},{3,2},{4,5},{5,4},{6,7},{7,6},{8,9},{9,8},{10,11... | collective-permute-start | bytes 3538952 | tf_op jit(solution)/shard_map/ppermute | solution.py:515
  203.3 12.4 %collective-permute-start.18 = (bf16[768,768]{1,0:T(8,128)(2,1)S(1)}, bf16[768,768]{1,0:T(8,128)(2,1)S(1)}, u32[]{:S(2)}, u32[]{:S(2)}) collective-permute-start(bf16[768,768]{1,0:T(8,128)(2,1)S(1)} %copy-done.30), channel_id=1, source_target_pairs={{0,1},{1,0},{2,3},{3,2},{4,5},{5,4},{6,7},{7,6},{8,9},{9,8},{10,11... | collective-permute-start | bytes 3538952 | tf_op jit(solution)/shard_map/ppermute | solution.py:515
  203.8 16.2 %collective-permute-start.19 = (bf16[384,768]{1,0:T(8,128)(2,1)S(1)}, bf16[384,768]{1,0:T(8,128)(2,1)S(1)}, u32[]{:S(2)}, u32[]{:S(2)}) collective-permute-start(bf16[384,768]{1,0:T(8,128)(2,1)S(1)} %add_convert_fusion.23), channel_id=1, source_target_pairs={{0,2},{1,3},{2,0},{3,1},{4,6},{5,7},{6,4},{7,5},{8,10},{9,11},{10,... | collective-permute-start | bytes 1769480 | tf_op jit(solution)/shard_map/ppermute | solution.py:515
  204.4 27.4 %collective-permute-start.20 = (bf16[384,768]{1,0:T(8,128)(2,1)S(1)}, bf16[384,768]{1,0:T(8,128)(2,1)S(1)}, u32[]{:S(2)}, u32[]{:S(2)}) collective-permute-start(bf16[384,768]{1,0:T(8,128)(2,1)S(1)} %add_convert_fusion.22), channel_id=1, source_target_pairs={{0,2},{1,3},{2,0},{3,1},{4,6},{5,7},{6,4},{7,5},{8,10},{9,11},{10,... | collective-permute-start | bytes 1769480 | tf_op jit(solution)/shard_map/ppermute | solution.py:515
  220.2 22.6 %collective-permute-start.22 = (bf16[768,768]{1,0:T(8,128)(2,1)}, bf16[768,768]{1,0:T(8,128)(2,1)S(1)}, u32[]{:S(2)}, u32[]{:S(2)}) collective-permute-start(bf16[768,768]{1,0:T(8,128)(2,1)} %get-tuple-element.190), channel_id=1, source_target_pairs={{0,1},{1,0},{2,3},{3,2},{4,5},{5,4},{6,7},{7,6},{8,9},{9,8},{10,11... | collective-permute-start | bytes 3538952 | tf_op jit(solution)/shard_map/ppermute | solution.py:515
  220.3 22.2 %collective-permute-start.23 = (bf16[384,768]{1,0:T(8,128)(2,1)S(1)}, bf16[384,768]{1,0:T(8,128)(2,1)S(1)}, u32[]{:S(2)}, u32[]{:S(2)}) collective-permute-start(bf16[384,768]{1,0:T(8,128)(2,1)S(1)} %add_convert_fusion.21), channel_id=1, source_target_pairs={{0,4},{12,8},{1,5},{13,9},{2,6},{14,10},{3,7},{15,11},{16,20},{28,... | collective-permute-start | bytes 1769480 | tf_op jit(solution)/shard_map/ppermute | solution.py:568
  243.2 18.1 %collective-permute-start.24 = (bf16[768,768]{1,0:T(8,128)(2,1)}, bf16[768,768]{1,0:T(8,128)(2,1)S(1)}, u32[]{:S(2)}, u32[]{:S(2)}) collective-permute-start(bf16[768,768]{1,0:T(8,128)(2,1)} %get-tuple-element.199), channel_id=1, source_target_pairs={{0,1},{1,0},{2,3},{3,2},{4,5},{5,4},{6,7},{7,6},{8,9},{9,8},{10,11... | collective-permute-start | bytes 3538952 | tf_op jit(solution)/shard_map/ppermute | solution.py:515
  243.3 20.3 %collective-permute-start.21 = (bf16[384,768]{1,0:T(8,128)(2,1)S(1)}, bf16[384,768]{1,0:T(8,128)(2,1)S(1)}, u32[]{:S(2)}, u32[]{:S(2)}) collective-permute-start(bf16[384,768]{1,0:T(8,128)(2,1)S(1)} %add_convert_fusion.20), channel_id=1, source_target_pairs={{0,4},{12,8},{1,5},{13,9},{2,6},{14,10},{3,7},{15,11},{16,20},{28,... | collective-permute-start | bytes 1769480 | tf_op jit(solution)/shard_map/ppermute | solution.py:568
  246.2 16.2 %collective-permute-start.25 = (bf16[384,768]{1,0:T(8,128)(2,1)S(1)}, bf16[384,768]{1,0:T(8,128)(2,1)S(1)}, u32[]{:S(2)}, u32[]{:S(2)}) collective-permute-start(bf16[384,768]{1,0:T(8,128)(2,1)S(1)} %add_convert_fusion.18), channel_id=1, source_target_pairs={{0,2},{1,3},{2,0},{3,1},{4,6},{5,7},{6,4},{7,5},{8,10},{9,11},{10,... | collective-permute-start | bytes 1769480 | tf_op jit(solution)/shard_map/ppermute | solution.py:515
  247.7 23.7 %collective-permute-start.27 = (bf16[384,768]{1,0:T(8,128)(2,1)S(1)}, bf16[384,768]{1,0:T(8,128)(2,1)}, u32[]{:S(2)}, u32[]{:S(2)}) collective-permute-start(bf16[384,768]{1,0:T(8,128)(2,1)S(1)} %add_convert_fusion.19), channel_id=1, source_target_pairs={{4,8},{8,4},{5,9},{9,5},{6,10},{10,6},{7,11},{11,7},{20,24},{24,20... | collective-permute-start | bytes 1769480 | tf_op jit(solution)/shard_map/ppermute | solution.py:580
  249.2 25.1 %collective-permute-start.28 = (bf16[384,768]{1,0:T(8,128)(2,1)S(1)}, bf16[384,768]{1,0:T(8,128)(2,1)}, u32[]{:S(2)}, u32[]{:S(2)}) collective-permute-start(bf16[384,768]{1,0:T(8,128)(2,1)S(1)} %add_convert_fusion.17), channel_id=1, source_target_pairs={{0,2},{1,3},{2,0},{3,1},{4,6},{5,7},{6,4},{7,5},{8,10},{9,11},{10,... | collective-permute-start | bytes 1769480 | tf_op jit(solution)/shard_map/ppermute | solution.py:515
  263.8 26.3 %collective-permute-start.30 = (bf16[784,768]{1,0:T(8,128)(2,1)}, bf16[784,768]{1,0:T(8,128)(2,1)}, u32[]{:S(2)}, u32[]{:S(2)}) collective-permute-start(bf16[784,768]{1,0:T(8,128)(2,1)} %get-tuple-element.230), channel_id=1, source_target_pairs={{0,1},{1,0},{2,3},{3,2},{4,5},{5,4},{6,7},{7,6},{8,9},{9,8},{10,11... | collective-permute-start | bytes 3612680 | tf_op jit(solution)/shard_map/ppermute | solution.py:515
  263.9 24.0 %collective-permute-start.26 = (bf16[384,768]{1,0:T(8,128)(2,1)}, bf16[384,768]{1,0:T(8,128)(2,1)}, u32[]{:S(2)}, u32[]{:S(2)}) collective-permute-start(bf16[384,768]{1,0:T(8,128)(2,1)} %add_convert_fusion.16), channel_id=1, source_target_pairs={{0,4},{12,8},{1,5},{13,9},{2,6},{14,10},{3,7},{15,11},{16,20},{28,... | collective-permute-start | bytes 1769480 | tf_op jit(solution)/shard_map/ppermute | solution.py:568
  293.5 17.8 %collective-permute-start.31 = (bf16[784,768]{1,0:T(8,128)(2,1)}, bf16[784,768]{1,0:T(8,128)(2,1)}, u32[]{:S(2)}, u32[]{:S(2)}) collective-permute-start(bf16[784,768]{1,0:T(8,128)(2,1)} %get-tuple-element.235), channel_id=1, source_target_pairs={{0,1},{1,0},{2,3},{3,2},{4,5},{5,4},{6,7},{7,6},{8,9},{9,8},{10,11... | collective-permute-start | bytes 3612680 | tf_op jit(solution)/shard_map/ppermute | solution.py:515
  293.5 16.0 %collective-permute-start.33 = (bf16[384,768]{1,0:T(8,128)(2,1)}, bf16[384,768]{1,0:T(8,128)(2,1)S(1)}, u32[]{:S(2)}, u32[]{:S(2)}) collective-permute-start(bf16[384,768]{1,0:T(8,128)(2,1)} %fusion.1), channel_id=1, source_target_pairs={{4,0},{8,12},{0,4},{12,8},{5,1},{9,13},{1,5},{13,9},{6,2},{10,14},... | collective-permute-start | bytes 1769480 | tf_op jit(solution)/shard_map/ppermute | solution.py:568
  293.5 18.9 %collective-permute-start.34 = (bf16[384,768]{1,0:T(8,128)(2,1)S(1)}, bf16[384,768]{1,0:T(8,128)(2,1)}, u32[]{:S(2)}, u32[]{:S(2)}) collective-permute-start(bf16[384,768]{1,0:T(8,128)(2,1)S(1)} %add_convert_fusion.15), channel_id=1, source_target_pairs={{4,8},{8,4},{5,9},{9,5},{6,10},{10,6},{7,11},{11,7},{20,24},{24,20... | collective-permute-start | bytes 1769480 | tf_op jit(solution)/shard_map/ppermute | solution.py:580
  294.9 17.4 %collective-permute-start.35 = (bf16[384,768]{1,0:T(8,128)(2,1)S(1)}, bf16[384,768]{1,0:T(8,128)(2,1)}, u32[]{:S(2)}, u32[]{:S(2)}) collective-permute-start(bf16[384,768]{1,0:T(8,128)(2,1)S(1)} %add_convert_fusion.11), channel_id=1, source_target_pairs={{0,2},{1,3},{2,0},{3,1},{4,6},{5,7},{6,4},{7,5},{8,10},{9,11},{10,... | collective-permute-start | bytes 1769480 | tf_op jit(solution)/shard_map/ppermute | solution.py:515
  298.9 22.3 %collective-permute-start.29 = (bf16[384,768]{1,0:T(8,128)(2,1)S(1)}, bf16[384,768]{1,0:T(8,128)(2,1)S(1)}, u32[]{:S(2)}, u32[]{:S(2)}) collective-permute-start(bf16[384,768]{1,0:T(8,128)(2,1)S(1)} %copy-done.20), channel_id=1, source_target_pairs={{4,8},{8,4},{5,9},{9,5},{6,10},{10,6},{7,11},{11,7},{20,24},{24,20... | collective-permute-start | bytes 1769480 | tf_op jit(solution)/shard_map/ppermute | solution.py:580
  309.4 15.6 %collective-permute-start.32 = (bf16[400,768]{1,0:T(8,128)(2,1)S(1)}, bf16[400,768]{1,0:T(8,128)(2,1)S(1)}, u32[]{:S(2)}, u32[]{:S(2)}) collective-permute-start(bf16[400,768]{1,0:T(8,128)(2,1)S(1)} %copy-done.27), channel_id=1, source_target_pairs={{0,2},{1,3},{2,0},{3,1},{4,6},{5,7},{6,4},{7,5},{8,10},{9,11},{10,... | collective-permute-start | bytes 1843208 | tf_op jit(solution)/shard_map/ppermute | solution.py:515
  314.1 16.1 %collective-permute-start.37 = (bf16[384,768]{1,0:T(8,128)(2,1)S(1)}, bf16[384,768]{1,0:T(8,128)(2,1)S(1)}, u32[]{:S(2)}, u32[]{:S(2)}) collective-permute-start(bf16[384,768]{1,0:T(8,128)(2,1)S(1)} %fusion.2), channel_id=1, source_target_pairs={{4,0},{8,12},{0,4},{12,8},{5,1},{9,13},{1,5},{13,9},{6,2},{10,14},... | collective-permute-start | bytes 1769480 | tf_op jit(solution)/shard_map/ppermute | solution.py:568
  319.3 12.9 %collective-permute-start.40 = (bf16[384,768]{1,0:T(8,128)(2,1)S(1)}, bf16[384,768]{1,0:T(8,128)(2,1)S(1)}, u32[]{:S(2)}, u32[]{:S(2)}) collective-permute-start(bf16[384,768]{1,0:T(8,128)(2,1)S(1)} %add_convert_fusion.8), channel_id=1, source_target_pairs={{4,8},{8,4},{5,9},{9,5},{6,10},{10,6},{7,11},{11,7},{20,24},{24,20... | collective-permute-start | bytes 1769480 | tf_op jit(solution)/shard_map/ppermute | solution.py:580
  325.5 18.1 %collective-permute-start.39 = (bf16[400,768]{1,0:T(8,128)(2,1)S(1)}, bf16[400,768]{1,0:T(8,128)(2,1)S(1)}, u32[]{:S(2)}, u32[]{:S(2)}) collective-permute-start(bf16[400,768]{1,0:T(8,128)(2,1)S(1)} %fusion), channel_id=1, source_target_pairs={{4,0},{8,12},{0,4},{12,8},{5,1},{9,13},{1,5},{13,9},{6,2},{10,14},... | collective-permute-start | bytes 1843208 | tf_op jit(solution)/shard_map/ppermute | solution.py:568
  328.8 17.4 %collective-permute-start.36 = (bf16[3,1,128,768]{3,2,0,1:T(8,128)(2,1)S(1)}, bf16[3,1,128,768]{3,2,0,1:T(8,128)(2,1)S(1)}, u32[]{:S(2)}, u32[]{:S(2)}) collective-permute-start(bf16[3,1,128,768]{3,2,0,1:T(8,128)(2,1)S(1)} %bitcast.67), channel_id=1, source_target_pairs={{0,2},{1,3},{2,0},{3,1},{4,6},{5,7},{6,4},{7,5},{8,10},{9,11},{10,... | collective-permute-start | bytes 1769480 | tf_op jit(solution)/shard_map/ppermute | solution.py:515
  331.5 13.2 %collective-permute-start.38 = (bf16[384,768]{1,0:T(8,128)(2,1)S(1)}, bf16[384,768]{1,0:T(8,128)(2,1)S(1)}, u32[]{:S(2)}, u32[]{:S(2)}) collective-permute-start(bf16[384,768]{1,0:T(8,128)(2,1)S(1)} %add_convert_fusion.6), channel_id=1, source_target_pairs={{4,8},{8,4},{5,9},{9,5},{6,10},{10,6},{7,11},{11,7},{20,24},{24,20... | collective-permute-start | bytes 1769480 | tf_op jit(solution)/shard_map/ppermute | solution.py:580
  332.4 23.8 %collective-permute-start.46 = (bf16[384,768]{1,0:T(8,128)(2,1)S(1)}, bf16[384,768]{1,0:T(8,128)(2,1)S(1)}, u32[]{:S(2)}, u32[]{:S(2)}) collective-permute-start(bf16[384,768]{1,0:T(8,128)(2,1)S(1)} %add_convert_fusion.5), channel_id=1, source_target_pairs={{4,0},{8,12},{5,1},{9,13},{6,2},{10,14},{7,3},{11,15},{20,16},{24,... | collective-permute-start | bytes 1769480 | tf_op jit(solution)/shard_map/ppermute | solution.py:568
  343.9 13.9 %collective-permute-start.43 = (bf16[400,768]{1,0:T(8,128)(2,1)S(1)}, bf16[400,768]{1,0:T(8,128)(2,1)S(1)}, u32[]{:S(2)}, u32[]{:S(2)}) collective-permute-start(bf16[400,768]{1,0:T(8,128)(2,1)S(1)} %add_convert_fusion.1), channel_id=1, source_target_pairs={{4,8},{8,4},{5,9},{9,5},{6,10},{10,6},{7,11},{11,7},{20,24},{24,20... | collective-permute-start | bytes 1843208 | tf_op jit(solution)/shard_map/ppermute | solution.py:580
  344.9 24.0 %collective-permute-start.44 = (bf16[384,768]{1,0:T(8,128)(2,1)S(1)}, bf16[384,768]{1,0:T(8,128)(2,1)S(1)}, u32[]{:S(2)}, u32[]{:S(2)}) collective-permute-start(bf16[384,768]{1,0:T(8,128)(2,1)S(1)} %add_convert_fusion.4), channel_id=1, source_target_pairs={{4,0},{8,12},{5,1},{9,13},{6,2},{10,14},{7,3},{11,15},{20,16},{24,... | collective-permute-start | bytes 1769480 | tf_op jit(solution)/shard_map/ppermute | solution.py:568
  346.2 13.1 %collective-permute-start.41 = (bf16[3,1,128,768]{3,2,0,1:T(8,128)(2,1)S(1)}, bf16[3,1,128,768]{3,2,0,1:T(8,128)(2,1)S(1)}, u32[]{:S(2)}, u32[]{:S(2)}) collective-permute-start(bf16[3,1,128,768]{3,2,0,1:T(8,128)(2,1)S(1)} %bitcast.68), channel_id=1, source_target_pairs={{0,1},{1,0},{2,3},{3,2},{4,5},{5,4},{6,7},{7,6},{8,9},{9,8},{10,11... | collective-permute-start | bytes 1769480 | tf_op jit(solution)/shard_map/ppermute | solution.py:515
  346.3 13.1 %collective-permute-start.42 = (bf16[3,1,128,768]{3,2,0,1:T(8,128)(2,1)S(1)}, bf16[3,1,128,768]{3,2,0,1:T(8,128)(2,1)S(1)}, u32[]{:S(2)}, u32[]{:S(2)}) collective-permute-start(bf16[3,1,128,768]{3,2,0,1:T(8,128)(2,1)S(1)} %collective-permute-done.36), channel_id=1, source_target_pairs={{0,1},{1,0},{2,3},{3,2},{4,5},{5,4},{6,7},{7,6},{8,9},{9,8},{10,11... | collective-permute-start | bytes 1769480 | tf_op jit(solution)/shard_map/ppermute | solution.py:515
  358.0 23.1 %collective-permute-start.45 = (bf16[400,768]{1,0:T(8,128)(2,1)S(1)}, bf16[400,768]{1,0:T(8,128)(2,1)S(1)}, u32[]{:S(2)}, u32[]{:S(2)}) collective-permute-start(bf16[400,768]{1,0:T(8,128)(2,1)S(1)} %add_convert_fusion), channel_id=1, source_target_pairs={{4,0},{8,12},{5,1},{9,13},{6,2},{10,14},{7,3},{11,15},{20,16},{24,... | collective-permute-start | bytes 1843208 | tf_op jit(solution)/shard_map/ppermute | solution.py:568
  (30 other events, 169.6 us)
